TPU v7x, 256 devices: a whole 4x4x8 slice. The times are simulated.
256 devices in a mesh: box: 64 (over z, y, core), grp: 4 (over x).
Axes of the slice: x: 4, y: 4, z: 8, core: 2. Of those that a mesh axis runs over, the one named last changes fastest.
Arguments:
- exp_fine: bfloat16 [65536, 512], P('box'), may hold values from -6 to 6
- req_fine: int32 [4096, 128], P('box'), may hold values from -1 to 1023, as said below
- src_fine: int32 [2048, 1024], P(('box', 'grp')), may hold values from -1 to 9215, as said below
- exp_coarse: bfloat16 [8192, 512], P('box'), may hold values from -6 to 6
- req_coarse: int32 [4096, 32], P('box'), may hold values from -1 to 127, as said below
- src_coarse: int32 [2048, 128], P(('box', 'grp')), may hold values from -1 to 2175, as said below
- operators: bfloat16 [32, 512, 512], P('grp'), may hold values from -0.03125 to 0.03125
- l2l_ops: bfloat16 [8, 512, 512], replicated, may hold values from -0.25 to 0.25
- relay_src: int32 [65536], P('box'), may hold values from 0 to 65535, as said below
Outputs:
- local_field: bfloat16 [65536, 512], P('box')
Inputs may be any that keep to these rules, and one draw needn't show every extreme that they name: `req_fine`: -1 marks an empty slot. `req_coarse`: -1 marks an empty slot. `src_fine`: -1 marks a target box that the operator does not reach; in every block of 32 rows the first row has no -1. `src_coarse`: -1 marks a target box that the operator does not reach; in every block of 32 rows the first row has no -1. A permutation; relay_src[i] lies in the block of 1024 rows that holds i or within 32 rows of it in a neighbouring block.
All inputs are finite; a program needn't handle non-finite values.
Results may differ from a plain program's by a relative error of at most 0.0049.
Values may be sent and summed in bfloat16 or wider, within the bound.
No kernel may reach another device: no remote copies, remote signals or barrier semaphores. Data moves between devices by JAX's collectives and lax.ppermute only.
A program may use at most 128 MiB of HBM per device.

v0:
```python
import jax
import jax.numpy as jnp
from jax import lax
from jax.sharding import PartitionSpec as P

R = 32


coarse_factor = 0.5


def with_halo(cells, sides, width):
    for axis, dim in sides:
        count = lax.axis_size(axis)
        ends = count - 1
        head = lax.slice_in_dim(cells, 0, width, axis=dim)
        tail = lax.slice_in_dim(cells, cells.shape[dim] - width, cells.shape[dim], axis=dim)
        cells = jnp.concatenate(
            [
                lax.ppermute(tail, axis, [(i, (i + 1) % count) for i in range(ends)]),
                cells,
                lax.ppermute(head, axis, [((i + 1) % count, i) for i in range(ends)]),
            ],
            axis=dim,
        )
    return cells


def picked_rows(expansions, wanted):
    chosen = jnp.take(expansions, jnp.clip(wanted, 0, expansions.shape[0] - 1), axis=0)
    return jnp.where((wanted >= 0)[:, :, None], chosen, jnp.zeros((), expansions.dtype))


def fetched(expansions, requests):
    wanted = lax.all_to_all(requests, "box", split_axis=0, concat_axis=0, tiled=True)
    return lax.all_to_all(
        picked_rows(expansions, wanted), "box", split_axis=0, concat_axis=0, tiled=True
    )


def far_field(expansions, received, sources, operators, level_factor):
    coefficients = expansions.shape[1]
    zero_row = jnp.zeros((1, coefficients), expansions.dtype)
    source_table = jnp.concatenate([expansions, received.reshape(-1, coefficients), zero_row], 0)
    empty_index = source_table.shape[0] - 1
    picked = jnp.take(source_table, jnp.where(sources >= 0, sources, empty_index), axis=0)
    summed = jnp.einsum("okp,opq->kq", picked, operators, preferred_element_type=jnp.float32)
    return lax.psum(summed * level_factor, "grp").astype(jnp.bfloat16)


def per_device(
    exp_fine, req_fine, src_fine, exp_coarse, req_coarse, src_coarse, operators, l2l_ops, relay_src
):
    got_coarse = fetched(exp_coarse, req_coarse)
    got_fine = fetched(exp_fine, req_fine)
    parent_field = far_field(exp_coarse, got_coarse, src_coarse, operators, coarse_factor)
    fine_field = far_field(exp_fine, got_fine, src_fine, operators, 1.0)
    children = jnp.einsum(
        "cp,kpq->ckq", parent_field, l2l_ops, preferred_element_type=jnp.float32
    ).reshape(fine_field.shape)
    padded = with_halo(fine_field, (("box", 0),), R)
    offsets = relay_src - (lax.axis_index("box") * fine_field.shape[0] - R)
    relayed = jnp.take(padded, offsets, axis=0)
    return (children + relayed.astype(jnp.float32)).astype(jnp.bfloat16)


def solution(mesh):
    return jax.shard_map(
        per_device,
        mesh=mesh,
        in_specs=(
            P("box", None),
            P("box", None),
            P(("box", "grp"), None),
            P("box", None),
            P("box", None),
            P(("box", "grp"), None),
            P("grp", None, None),
            P(),
            P("box"),
        ),
        out_specs=P("box", None),
        check_vma=False,
    )
```

profile of v0, /device:TPU:1, one launch (start us, length us, event | category | flops | bytes accessed | tf_op | source)
XLA Modules:
  0.0 418.2 jit_solution(2584910817875831709)
XLA Ops:
  0.0 0.0 copy-start.1
  0.0 0.8 copy.18
  0.8 22.3 %all_to_all.28 = s32[64,1,32]{2,1,0:T(1,128)S(1)} all-to-all(s32[64,1,32]{2,1,0:T(1,128)S(1)} %bitcast.62), channel_id=1, replica_groups=mesh['box'=64,'grp'=4] {'box'}, dimensions={0} | all-to-all | bytes 16384 | tf_op jit(solution)/shard_map/all_to_all | solution.py:35
  23.2 4.7 %all-to-all-start.2 = ((s32[64,1,128]{2,1,0:T(1,128)}), s32[64,1,128]{2,1,0:T(1,128)S(1)}, u32[]{:S(2)}, u32[]{:S(2)}) async-start(s32[64,1,128]{2,1,0:T(1,128)} %bitcast.63), calls=%async_computation.2 | async-start | bytes 65536 | tf_op jit(solution)/shard_map/all_to_all | solution.py:35
  27.9 0.1 copy.19
  28.0 0.1 copy.23
  28.1 0.1 reshape.109
  28.2 0.1 copy.20
  28.3 0.1 copy.22
  28.4 0.0 copy-done.1
  28.4 7.5 %gather_fusion = bf16[2048,512]{1,0:T(8,128)(2,1)S(1)} fusion(bf16[128,512]{1,0:T(8,128)(2,1)S(1)} %copy-done.1, s32[2048]{0:T(1024)S(1)} %broadcast_clamp_fusion), kind=kCustom, calls=%fused_computation | custom fusion | bytes 4202496 | tf_op jit(solution)/shard_map/jit(_take)/gather | solution.py:30
  35.9 0.0 copy-start
  35.9 1.7 select_select_fusion.1
  37.6 0.0 all-to-all-done.2
  37.7 10.4 %all-to-all-start.1 = ((bf16[64,32,512]{2,1,0:T(8,128)(2,1)}), bf16[64,32,512]{2,1,0:T(8,128)(2,1)S(1)}, u32[]{:S(2)}, u32[]{:S(2)}) async-start(bf16[64,32,512]{2,1,0:T(8,128)(2,1)} %select_select_fusion.1), calls=%async_computation.1 | async-start | bytes 4194304 | tf_op jit(solution)/shard_map/all_to_all | solution.py:36
  48.1 0.0 copy-done
  48.1 33.8 %gather_fusion.2 = bf16[8192,512]{1,0:T(8,128)(2,1)} fusion(bf16[1024,512]{1,0:T(8,128)(2,1)S(1)} %copy-done, s32[8192]{0:T(1024)S(1)} %fusion.16), kind=kCustom, calls=%fused_computation.2 | custom fusion | bytes 16809984 | tf_op jit(solution)/shard_map/jit(_take)/gather | solution.py:30
  81.9 8.1 %select_select_fusion = bf16[64,128,512]{2,1,0:T(8,128)(2,1)} fusion(bf16[64,128,512]{2,1,0:T(8,128)(2,1)} %bitcast.54, pred[64,128]{1,0:T(8,128)(4,1)S(1)} %compare_and_fusion, pred[64,128]{1,0:T(8,128)(4,1)S(1)} %compare_bitcast_fusion), kind=kLoop, calls=%fused_computation.8 | loop fusion | flops 8388608 | bytes 16793600 | tf_op jit(solution)/shard_map/jit(_where)/select_n | solution.py:31
  90.0 0.0 copy-start.7
  90.0 0.0 copy-start.8
  90.0 0.0 copy-start.6
  90.0 7.8 %all-to-all-done.1 = bf16[64,32,512]{2,1,0:T(8,128)(2,1)S(1)} async-done(((bf16[64,32,512]{2,1,0:T(8,128)(2,1)}), bf16[64,32,512]{2,1,0:T(8,128)(2,1)S(1)}, u32[]{:S(2)}, u32[]{:S(2)}) %all-to-all-start.1) | async-done | bytes 2097184 | tf_op jit(solution)/shard_map/all_to_all | solution.py:36
  97.7 0.0 copy-start.2
  97.7 1.3 copy-done.2
  99.0 7.3 %all-to-all-start.3 = ((bf16[64,128,512]{2,1,0:T(8,128)(2,1)}), bf16[64,128,512]{2,1,0:T(8,128)(2,1)}, u32[]{:S(2)}, u32[]{:S(2)}) async-start(bf16[64,128,512]{2,1,0:T(8,128)(2,1)} %select_select_fusion), calls=%async_computation.3 | async-start | bytes 16777216 | tf_op jit(solution)/shard_map/all_to_all | solution.py:36
  106.3 0.0 copy-done.7
  106.3 0.5 compare_and_fusion.4
  106.9 0.0 copy-done.8
  106.9 0.6 compare_and_fusion.3
  107.5 0.0 copy-done.6
  107.5 0.6 bitcast_clamp_fusion
  108.1 1.7 pad_maximum_fusion.1
  109.9 0.0 copy-start.10
  109.9 5.1 %gather_fusion.1 = bf16[1024,512]{1,0:T(8,128)(2,1)} fusion(bf16[2177,512]{1,0:T(8,128)(2,1)S(1)} %pad_maximum_fusion.1, s32[1024]{0:T(1024)S(1)} %bitcast_clamp_fusion.1), kind=kCustom, calls=%fused_computation.1 | custom fusion | bytes 2101248 | tf_op jit(solution)/shard_map/jit(_take)/gather | solution.py:46
  115.0 0.0 copy-done.10
  115.0 3.3 fusion.8
  118.2 170.9 %all-to-all-done.3 = bf16[64,128,512]{2,1,0:T(8,128)(2,1)} async-done(((bf16[64,128,512]{2,1,0:T(8,128)(2,1)}), bf16[64,128,512]{2,1,0:T(8,128)(2,1)}, u32[]{:S(2)}, u32[]{:S(2)}) %all-to-all-start.3) | async-done | bytes 8388640 | tf_op jit(solution)/shard_map/all_to_all | solution.py:36
  289.2 0.0 copy-start.5
  289.2 14.8 %pad_maximum_fusion = bf16[9217,512]{1,0:T(8,128)(2,1)} fusion(bf16[1,512]{1,0:T(2,128)(2,1)S(1)} %broadcast.122, bf16[8192,512]{1,0:T(8,128)(2,1)} %bitcast.19, bf16[1024,512]{1,0:T(8,128)(2,1)S(1)} %copy-done), kind=kLoop, calls=%fused_computation.5 | loop fusion | flops 28314624 | bytes 18876416 | tf_op jit(solution)/shard_map/concatenate | solution.py:44
  303.9 0.0 copy-done.5
  303.9 38.7 %gather_fusion.3 = bf16[8192,512]{1,0:T(8,128)(2,1)} fusion(bf16[9217,512]{1,0:T(8,128)(2,1)} %pad_maximum_fusion, s32[8192]{0:T(1024)S(1)} %copy-done.5), kind=kCustom, calls=%fused_computation.3 | custom fusion | bytes 16809984 | tf_op jit(solution)/shard_map/jit(_take)/gather | solution.py:46
  342.6 8.3 %fusion.5 = f32[1024,512]{1,0:T(8,128)S(1)} fusion(bf16[8,512,512]{2,1,0:T(8,128)(2,1)} %param.15, bf16[8,1024,512]{2,1,0:T(8,128)(2,1)} %bitcast.55, pred[8,1024]{1,0:T(8,128)(4,1)S(1)} %compare_and_fusion.1), kind=kOutput, calls=%fused_computation.15 | convolution fusion | flops 4299161600 | bytes 14688256 | tf_op jit(solution)/shard_map/okp,opq->kq/dot_general | solution.py:47
  350.9 42.6 %all-reduce.2 = (bf16[128,512]{1,0:T(8,128)(2,1)S(1)}, bf16[1024,512]{1,0:T(8,128)(2,1)S(1)}) all-reduce(f32[128,512]{1,0:T(8,128)S(1)} %fusion.8, f32[1024,512]{1,0:T(8,128)S(1)} %fusion.5), channel_id=1, replica_groups=mesh['box'=64,'grp'=4] {'grp'}, use_global_device_ids=true, to_apply=%region_0.1 | all-reduce | flops 589824 | bytes 3538944 | tf_op jit(solution)/shard_map/psum | solution.py:48
  393.5 0.0 copy-start.3
  393.5 10.9 %collective-permute-start = (bf16[32,512]{1,0:T(8,128)(2,1)S(1)}, bf16[32,512]{1,0:T(8,128)(2,1)S(1)}, u32[]{:S(2)}, u32[]{:S(2)}) collective-permute-start(bf16[32,512]{1,0:T(8,128)(2,1)S(1)} %get-tuple-element.7), channel_id=1, source_target_pairs={{0,4},{4,8},{8,12},{12,16},{16,20},{20,24},{24,28},{28,32},{32,36}... | collective-permute-start | bytes 98312 | tf_op jit(solution)/shard_map/ppermute | solution.py:20
  404.4 1.9 collective-permute-start.1
  406.3 0.0 copy-done.3
  406.3 0.0 copy-start.4
  406.3 3.0 fusion.12
  409.3 0.0 collective-permute-done
  409.4 0.3 collective-permute-done.1
  409.6 0.0 copy-done.4
  409.6 0.1 pad_maximum_fusion.2
  409.7 0.0 copy-start.9
  409.7 5.1 %gather_fusion.4 = bf16[1024,512]{1,0:T(8,128)(2,1)} fusion(bf16[1088,512]{1,0:T(8,128)(2,1)S(1)} %pad_maximum_fusion.2, s32[1024]{0:T(1024)S(1)} %fusion.18), kind=kCustom, calls=%fused_computation.4 | custom fusion | bytes 2101248 | tf_op jit(solution)/shard_map/jit(_take)/gather | solution.py:63
  414.8 0.0 copy-done.9
  414.8 3.4 fusion.4
  (13 shorter events, 0.1 us)
Async XLA Ops:
  0.0 28.4 %copy-start.1 = (bf16[128,512]{1,0:T(8,128)(2,1)S(1)}, bf16[128,512]{1,0:T(8,128)(2,1)}, u32[]{:S(2)}) copy-start(bf16[128,512]{1,0:T(8,128)(2,1)} %param.12) | copy-start | bytes 393220
  23.2 14.5 %all-to-all-start.2 = ((s32[64,1,128]{2,1,0:T(1,128)}), s32[64,1,128]{2,1,0:T(1,128)S(1)}, u32[]{:S(2)}, u32[]{:S(2)}) async-start(s32[64,1,128]{2,1,0:T(1,128)} %bitcast.63), calls=%async_computation.2 | async-start | bytes 65536 | tf_op jit(solution)/shard_map/all_to_all | solution.py:35
  35.9 12.2 %copy-start = (bf16[1024,512]{1,0:T(8,128)(2,1)S(1)}, bf16[1024,512]{1,0:T(8,128)(2,1)}, u32[]{:S(2)}) copy-start(bf16[1024,512]{1,0:T(8,128)(2,1)} %param.9) | copy-start | bytes 3145732
  37.7 60.1 %all-to-all-start.1 = ((bf16[64,32,512]{2,1,0:T(8,128)(2,1)}), bf16[64,32,512]{2,1,0:T(8,128)(2,1)S(1)}, u32[]{:S(2)}, u32[]{:S(2)}) async-start(bf16[64,32,512]{2,1,0:T(8,128)(2,1)} %select_select_fusion.1), calls=%async_computation.1 | async-start | bytes 4194304 | tf_op jit(solution)/shard_map/all_to_all | solution.py:36
  90.0 16.3 %copy-start.7 = (s32[8,128]{1,0:T(8,128)S(1)}, s32[8,128]{1,0:T(8,128)}, u32[]{:S(2)}) copy-start(s32[8,128]{1,0:T(8,128)} %param.14) | copy-start | bytes 12292
  90.0 16.9 %copy-start.8 = (s32[1024]{0:T(1024)S(1)}, s32[1024]{0:T(1024)}, u32[]{:S(2)}) copy-start(s32[1024]{0:T(1024)} %param.17) | copy-start | bytes 12292
  90.0 17.5 %copy-start.6 = (s32[8,1024]{1,0:T(8,128)S(1)}, s32[8,1024]{1,0:T(8,128)}, u32[]{:S(2)}) copy-start(s32[8,1024]{1,0:T(8,128)} %param.11) | copy-start | bytes 98308
  97.7 1.3 copy-start.2
  99.0 190.1 %all-to-all-start.3 = ((bf16[64,128,512]{2,1,0:T(8,128)(2,1)}), bf16[64,128,512]{2,1,0:T(8,128)(2,1)}, u32[]{:S(2)}, u32[]{:S(2)}) async-start(bf16[64,128,512]{2,1,0:T(8,128)(2,1)} %select_select_fusion), calls=%async_computation.3 | async-start | bytes 16777216 | tf_op jit(solution)/shard_map/all_to_all | solution.py:36
  109.9 5.1 %copy-start.10 = (pred[8,128]{1,0:T(8,128)(4,1)S(1)}, pred[8,128]{1,0:T(8,128)(4,1)}, u32[]{:S(2)}) copy-start(pred[8,128]{1,0:T(8,128)(4,1)} %compare_and_fusion.4) | copy-start | bytes 3076
  289.2 14.8 %copy-start.5 = (s32[8192]{0:T(1024)S(1)}, s32[8192]{0:T(1024)}, u32[]{:S(2)}) copy-start(s32[8192]{0:T(1024)} %bitcast_clamp_fusion) | copy-start | bytes 98308
  393.5 12.9 %copy-start.3 = (bf16[1024,512]{1,0:T(8,128)(2,1)}, bf16[1024,512]{1,0:T(8,128)(2,1)S(1)}, u32[]{:S(2)}) copy-start(bf16[1024,512]{1,0:T(8,128)(2,1)S(1)} %get-tuple-element.6) | copy-start | bytes 3145732
  393.5 15.9 %collective-permute-start = (bf16[32,512]{1,0:T(8,128)(2,1)S(1)}, bf16[32,512]{1,0:T(8,128)(2,1)S(1)}, u32[]{:S(2)}, u32[]{:S(2)}) collective-permute-start(bf16[32,512]{1,0:T(8,128)(2,1)S(1)} %get-tuple-element.7), channel_id=1, source_target_pairs={{0,4},{4,8},{8,12},{12,16},{16,20},{20,24},{24,28},{28,32},{32,36}... | collective-permute-start | bytes 98312 | tf_op jit(solution)/shard_map/ppermute | solution.py:20
  404.4 5.2 %collective-permute-start.1 = (bf16[32,512]{1,0:T(8,128)(2,1)S(1)}, bf16[32,512]{1,0:T(8,128)(2,1)S(1)}, u32[]{:S(2)}, u32[]{:S(2)}) collective-permute-start(bf16[32,512]{1,0:T(8,128)(2,1)S(1)} %get-tuple-element.8), channel_id=1, source_target_pairs={{4,0},{8,4},{12,8},{16,12},{20,16},{24,20},{28,24},{32,28},{36,32}... | collective-permute-start | bytes 98312 | tf_op jit(solution)/shard_map/ppermute | solution.py:22
  406.3 3.3 copy-start.4
  409.7 5.1 %copy-start.9 = (pred[1024]{0:T(1024)(128)(4,1)S(1)}, pred[1024]{0:T(1024)(128)(4,1)}, u32[]{:S(2)}) copy-start(pred[1024]{0:T(1024)(128)(4,1)} %compare_and_fusion.3) | copy-start | bytes 3076
where the time goes:
time: 420 us; the launch traced here: 418 us
  waiting for transfers between devices  179 us (43%)
  local copies, waits for them, and re-layouts  92.7 us (22%)
  blocking collectives  64.9 us (15%)
  starting transfers between devices  35.2 us (8%)
  other arithmetic  31.6 us (8%)
  matrix products  14.5 us (3%)
    all_to_all x2, waiting for transfers between devices, fetched(): lax.all_to_all(picked_rows(expansions, wanted), 'box', split_axis=0, conc...  179 us
    gather x2, local copies, waits for them, and re-layouts, far_field(): jnp.take(source_table, jnp.where(sources >= 0, sources, empty_index), axi...  43.7 us
    psum x1, blocking collectives, far_field(): return lax.psum(summed * level_factor, 'grp').astype(jnp.bfloat16)  42.6 us
    gather x2, local copies, waits for them, and re-layouts, picked_rows(): jnp.take(expansions, jnp.clip(wanted, 0, expansions.shape[0] - 1), axis=0)  41.3 us
    all_to_all x1, blocking collectives, fetched(): lax.all_to_all(requests, 'box', split_axis=0, concat_axis=0, tiled=True)  22.3 us
    all_to_all x2, starting transfers between devices, fetched(): lax.all_to_all(picked_rows(expansions, wanted), 'box', split_axis=0, conc...  17.7 us
    concatenate x2, other arithmetic, far_field(): jnp.concatenate([expansions, received.reshape(-1, coefficients), zero_row...  16.5 us
    dot_general x2, matrix products, far_field(): jnp.einsum('okp,opq->kq', picked, operators, preferred_element_type=jnp.f...  11.5 us
  transfers between devices with their start and end apart: 5, of which 3 were waited for; matrix products, arithmetic and copies ran while one was open for 16% of the time, Pallas kernels for 0%

commit v1 on v0

v1 whole, which is shorter than its diff:
```python
import functools

import jax
import jax.numpy as jnp
from jax import lax
from jax.experimental import pallas as pl
from jax.experimental.pallas import tpu as pltpu
from jax.sharding import PartitionSpec as P

R = 32
LANES = 128
COARSE_FACTOR = 0.5
VMEM_LIMIT = 48 << 20


def gather_rows(idx_ref, base, table, out, rows, unroll):
    def step(i, carry):
        first = pl.multiple_of(i * unroll, unroll)
        start = base + first
        picked = [table[pl.ds(idx_ref[start + k], 1), :] for k in range(unroll)]
        for k in range(unroll):
            out[pl.ds(first + k, 1), :] = picked[k]
        return carry

    lax.fori_loop(0, rows // unroll, step, 0)


def widen(source, target, offset, block):
    def step(i, carry):
        first = pl.multiple_of(i * block, block)
        target[pl.ds(offset + first, block), :] = source[pl.ds(first, block), :].astype(jnp.float32)
        return carry

    lax.fori_loop(0, source.shape[0] // block, step, 0)


def pick_kernel(idx_ref, own_ref, out_ref, table, rows):
    step = pl.program_id(0)
    count = own_ref.shape[0]

    @pl.when(step == 0)
    def _():
        widen(own_ref, table, 0, 128)
        table[pl.ds(count, 8), :] = jnp.zeros((8, LANES), jnp.float32)

    block = out_ref.shape[0]
    gather_rows(idx_ref, step * block, table, rows, block, 64)
    out_ref[...] = rows[...].astype(out_ref.dtype)


def pick(own, wanted):
    total, block = wanted.shape[0], 1024
    return pl.pallas_call(
        pick_kernel,
        grid=(total // block,),
        out_shape=jax.ShapeDtypeStruct((total, LANES), own.dtype),
        in_specs=[
            pl.BlockSpec(memory_space=pltpu.SMEM),
            pl.BlockSpec(own.shape, lambda i: (0, 0)),
        ],
        out_specs=pl.BlockSpec((block, LANES), lambda i: (i, 0)),
        scratch_shapes=[
            pltpu.VMEM((own.shape[0] + 8, LANES), jnp.float32),
            pltpu.VMEM((block, LANES), jnp.float32),
        ],
        compiler_params=pltpu.CompilerParams(vmem_limit_bytes=VMEM_LIMIT),
        name="pick",
    )(wanted, own)


def translate_kernel(
    halo_rows, chunk_rows, chunks, ops, idx_ref, own_ref, got_ref, w0, w1, w2, w3, *refs
):
    outs = refs[: 2 if halo_rows else 1]
    table, rows, weights, sems = refs[len(outs) :]
    copies = [
        pltpu.make_async_copy(w, weights.at[g], sems.at[g]) for g, w in enumerate((w0, w1, w2, w3))
    ]
    for copy in copies:
        copy.start()
    own, got = own_ref.shape[0], got_ref.shape[0]
    widen(own_ref, table, 0, 128)
    widen(got_ref, table, own, 512)
    table[pl.ds(own + got, 8), :] = jnp.zeros((8, LANES), jnp.float32)
    for copy in copies:
        copy.wait()

    def summed(base, count, unroll):
        total = jnp.zeros((count, weights.shape[-1]), jnp.float32)
        for g in range(4):
            for o in range(ops):
                gather_rows(idx_ref, base + (g * ops + o) * count, table, rows.at[o], count, unroll)
            left = jnp.concatenate(
                [rows[o, pl.ds(0, count), :].astype(jnp.bfloat16) for o in range(ops)], axis=1
            )
            right = weights[g].reshape(ops * LANES, weights.shape[-1])
            total = total + jnp.dot(left, right, preferred_element_type=jnp.float32)
        return total

    base = 0
    if halo_rows:
        outs[1][...] = summed(0, halo_rows, 64).astype(outs[1].dtype)
        base = 4 * ops * halo_rows

    def chunk(c, carry):
        start = base + c * (4 * ops * chunk_rows)
        outs[0][c] = summed(start, chunk_rows, 96).astype(outs[0].dtype)
        return carry

    lax.fori_loop(0, chunks, chunk, 0)


def translate(idx, own, got, weights, halo_rows, chunk_rows, chunks, dtype):
    ops, _, columns = weights[0].shape
    out_shape = [jax.ShapeDtypeStruct((chunks, chunk_rows, columns), dtype)]
    if halo_rows:
        out_shape.append(jax.ShapeDtypeStruct((halo_rows, columns), dtype))
    vmem = pl.BlockSpec(memory_space=pltpu.VMEM)
    return pl.pallas_call(
        functools.partial(translate_kernel, halo_rows, chunk_rows, chunks, ops),
        out_shape=out_shape,
        in_specs=[pl.BlockSpec(memory_space=pltpu.SMEM), vmem, vmem]
        + [pl.BlockSpec(memory_space=pl.ANY)] * 4,
        out_specs=[vmem] * len(out_shape),
        scratch_shapes=[
            pltpu.VMEM((own.shape[0] + got.shape[0] + 8, LANES), jnp.float32),
            pltpu.VMEM((ops, chunk_rows, LANES), jnp.float32),
            pltpu.VMEM((4, ops, LANES, columns), weights[0].dtype),
            pltpu.SemaphoreType.DMA((4,)),
        ],
        compiler_params=pltpu.CompilerParams(vmem_limit_bytes=VMEM_LIMIT),
        name="translate",
    )(idx, own, got, *weights)


def finish_kernel(own_ref, a_ref, b_ref, c_ref, place_ref, halo_ref, l2l_ref, out_ref, acc):
    quarter = out_ref.shape[0]
    total = own_ref[...] + a_ref[...].astype(jnp.float32)
    total = total + b_ref[...].astype(jnp.float32) + c_ref[...].astype(jnp.float32)
    fine = total[:quarter].astype(jnp.bfloat16).astype(jnp.float32)
    parent = (total[quarter:] * COARSE_FACTOR).astype(jnp.bfloat16)
    acc[...] = jnp.zeros_like(acc)
    for k in range(8):
        child = jnp.dot(parent, l2l_ref[k], preferred_element_type=jnp.float32)
        for j in range(4):
            acc[j, pl.ds(k, parent.shape[0], stride=8), :] = child[:, j * LANES : (j + 1) * LANES]
    halo = halo_ref.shape[0]
    spread = (lax.broadcasted_iota(jnp.int32, (quarter, halo), 1) == place_ref[...]).astype(
        jnp.bfloat16
    )
    foreign = jnp.dot(spread, halo_ref[...], preferred_element_type=jnp.float32)
    children = jnp.concatenate([acc[j] for j in range(4)], axis=1)
    out_ref[...] = (children + (fine + foreign)).astype(out_ref.dtype)


def finish(own, parts, place, halo, l2l_ops, quarter):
    columns = own.shape[1]
    vmem = pl.BlockSpec(memory_space=pltpu.VMEM)
    return pl.pallas_call(
        finish_kernel,
        out_shape=jax.ShapeDtypeStruct((quarter, columns), jnp.bfloat16),
        in_specs=[vmem] * 7,
        out_specs=vmem,
        scratch_shapes=[pltpu.VMEM((columns // LANES, quarter, LANES), jnp.float32)],
        compiler_params=pltpu.CompilerParams(vmem_limit_bytes=VMEM_LIMIT),
        name="finish",
    )(own, *parts, place, halo, l2l_ops)


def per_device(
    exp_fine, req_fine, src_fine, exp_coarse, req_coarse, src_coarse, operators, l2l_ops, relay_src
):
    members = lax.axis_size("grp")
    me = lax.axis_index("grp")
    blocks = lax.axis_size("box")
    here = lax.axis_index("box")
    rows_f, rows_c = exp_fine.shape[0], exp_coarse.shape[0]
    slots_f, slots_c = req_fine.shape[1], req_coarse.shape[1]
    slots = slots_f + slots_c
    own_rows = rows_f + rows_c
    zero_row = own_rows + blocks * slots
    ops, coefficients, _ = operators.shape

    def shifted(value, by):
        return lax.ppermute(value, "grp", [(i, (i + by) % members) for i in range(members)])

    requests = jnp.concatenate(
        [
            jnp.where(req_fine >= 0, req_fine, own_rows),
            jnp.where(req_coarse >= 0, req_coarse + rows_f, own_rows),
        ],
        axis=1,
    )
    wanted = lax.all_to_all(requests[:, None, :], "box", split_axis=0, concat_axis=0, tiled=True)
    first = me * LANES
    own = jnp.concatenate(
        [
            lax.dynamic_slice_in_dim(exp_fine, first, LANES, 1),
            lax.dynamic_slice_in_dim(exp_coarse, first, LANES, 1),
        ],
        axis=0,
    )
    sent = pick(own, wanted.reshape(-1)).reshape(blocks, slots, LANES)
    got = lax.all_to_all(sent, "box", split_axis=0, concat_axis=0, tiled=True)
    got = got.reshape(blocks * slots, LANES)

    by_member = operators.reshape(ops, members, LANES, coefficients)

    def rows_for(member):
        return lax.dynamic_index_in_dim(by_member, member % members, 1, keepdims=False)

    weights = [rows_for(me)] + [shifted(rows_for(me + s), s) for s in range(1, members)]

    q = src_fine - rows_f
    table_f = jnp.where(
        src_fine < rows_f, src_fine, own_rows + (q // slots_f) * slots + q % slots_f
    )
    table_f = jnp.where(src_fine >= 0, table_f, zero_row)
    q = src_coarse - rows_c
    table_c = jnp.where(
        src_coarse < rows_c,
        src_coarse + rows_f,
        own_rows + (q // slots_c) * slots + slots_f + q % slots_c,
    )
    table_c = jnp.where(src_coarse >= 0, table_c, zero_row)
    local = relay_src - here * rows_f
    inside = (local >= 0) & (local < rows_f)
    relayed = jnp.take(table_f.T, jnp.clip(local, 0, rows_f - 1), axis=0).T
    relayed = jnp.where(inside[None, :], relayed, zero_row)
    quarter = rows_f // members
    chunked = jnp.concatenate(
        [relayed.reshape(ops, members, quarter), table_c.reshape(ops, members, rows_c // members)],
        axis=2,
    )
    chunk_rows = chunked.shape[2]
    halo_idx = jnp.concatenate([table_f[:, :R], table_f[:, rows_f - R :]], axis=1)
    packed = jnp.concatenate([chunked.reshape(ops, -1), halo_idx], axis=1)
    every = jnp.stack([packed] + [shifted(packed, s) for s in range(1, members)])
    every_chunk = every[:, :, : members * chunk_rows].reshape(members * ops, members, chunk_rows)

    def chunk_of(member):
        return lax.dynamic_index_in_dim(every_chunk, member % members, 1, keepdims=False).reshape(-1)

    idx_away = jnp.concatenate(
        [every[:, :, members * chunk_rows :].reshape(-1)] + [chunk_of(me + s) for s in range(1, members)]
    )
    idx_here = chunk_of(me)

    away, halo = translate(
        idx_away, own, got, weights, 2 * R, chunk_rows, members - 1, jnp.bfloat16
    )
    parts = [shifted(away[s - 1], s) for s in range(1, members)]
    halo_sum = halo.astype(jnp.float32)
    for s in range(1, members):
        halo_sum = halo_sum + shifted(halo, s).astype(jnp.float32)
    edge = halo_sum.astype(jnp.bfloat16)
    from_left = lax.ppermute(edge[R:], "box", [(i, i + 1) for i in range(blocks - 1)])
    from_right = lax.ppermute(edge[:R], "box", [(i + 1, i) for i in range(blocks - 1)])
    (mine,) = translate(idx_here, own, got, weights, 0, chunk_rows, 1, jnp.float32)

    place = jnp.where(local < 0, local + R, jnp.where(local >= rows_f, local - rows_f + R, -1))
    place = lax.dynamic_slice_in_dim(place, me * quarter, quarter, 0)[:, None]
    done = finish(
        mine[0], parts, place, jnp.concatenate([from_left, from_right], axis=0), l2l_ops, quarter
    )
    out = jnp.zeros((rows_f, coefficients), jnp.bfloat16)
    for s in range(members):
        piece = done if s == 0 else shifted(done, s)
        out = lax.dynamic_update_slice_in_dim(out, piece, ((me - s) % members) * quarter, 0)
    return out


def solution(mesh):
    return jax.shard_map(
        per_device,
        mesh=mesh,
        in_specs=(
            P("box", None),
            P("box", None),
            P(("box", "grp"), None),
            P("box", None),
            P("box", None),
            P(("box", "grp"), None),
            P("grp", None, None),
            P(),
            P("box"),
        ),
        out_specs=P("box", None),
        check_vma=False,
    )
```

time: 420 us -> 201 us (0.48)
  waiting for transfers between devices: 179 us -> 57.8 us
  blocking collectives: 64.9 us -> 0 us
  local copies, waits for them, and re-layouts: 92.7 us -> 30.7 us
  Pallas kernels: 0 us -> 59.1 us
  other arithmetic: 31.6 us -> 7.06 us
  matrix products: 14.5 us -> 0 us
  starting transfers between devices: 35.2 us -> 45.3 us
    all_to_all x3 -> x2, waiting for transfers between devices: 179 us -> 9.25 us  [the longest x1 9.25 us: per_device(): lax.all_to_all(requests[:, None, :], 'box', split_axis=0, concat_axis=0,...]
    gather x5 -> x1, local copies, waits for them, and re-layouts: 90.1 us -> 5.07 us  [per_device(): relayed = jnp.take(table_f.T, jnp.clip(local, 0, rows_f - 1), axis=0).T]
    pallas_call x0 -> x4, Pallas kernels: none -> 59.1 us  [the longest x2 46.4 us: translate(): pl.pallas_call(functools.partial(translate_kernel, halo_rows, chunk_rows,...]
    ppermute x2 -> x17, waiting for transfers between devices: 0.27 us -> 48.5 us  [the longest x15 48.5 us: shifted(): lax.ppermute(value, 'grp', [(i, (i + by) % members) for i in range(member...]
    psum x1 -> x0, blocking collectives: 42.6 us -> none  [far_field(): return lax.psum(summed * level_factor, 'grp').astype(jnp.bfloat16)]
    all_to_all x1 -> x0, blocking collectives: 22.3 us -> none  [fetched(): lax.all_to_all(requests, 'box', split_axis=0, concat_axis=0, tiled=True)]
    dot_general x3 -> x0, matrix products: 14.5 us -> none  [the longest x2 11.5 us: far_field(): jnp.einsum('okp,opq->kq', picked, operators, preferred_element_type=jnp.f...]
    concatenate x3 -> x5, other arithmetic: 16.6 us -> 2.28 us  [the longest x1 1.45 us: per_device(): jnp.concatenate([every[:, :, members * chunk_rows:].reshape(-1)] + [chunk...]
  transfers between devices with their start and end apart: 5 -> 19, of which waited for: 3 -> 5; matrix products, arithmetic and copies ran while one was open for 16% -> 15% of each run, Pallas kernels for 0% -> 6%
where the time goes in v1:
time: 201 us; the launch traced here: 200 us
  Pallas kernels  59.1 us (29%)
  waiting for transfers between devices  57.8 us (29%)
  starting transfers between devices  45.3 us (23%)
  local copies, waits for them, and re-layouts  30.7 us (15%)
  other arithmetic  7.06 us (4%)
    ppermute x15, waiting for transfers between devices, shifted(): lax.ppermute(value, 'grp', [(i, (i + by) % members) for i in range(member...  48.5 us
    pallas_call x2, Pallas kernels, translate(): pl.pallas_call(functools.partial(translate_kernel, halo_rows, chunk_rows,...  46.4 us
    ppermute x15, starting transfers between devices, shifted(): lax.ppermute(value, 'grp', [(i, (i + by) % members) for i in range(member...  18.4 us
    all_to_all x1, starting transfers between devices, per_device(): lax.all_to_all(requests[:, None, :], 'box', split_axis=0, concat_axis=0,...  13.2 us
    pallas_call x1, Pallas kernels, pick(): pl.pallas_call(pick_kernel, grid=(total // block,), out_shape=jax.ShapeDt...  10.6 us
    all_to_all x1, waiting for transfers between devices, per_device(): lax.all_to_all(requests[:, None, :], 'box', split_axis=0, concat_axis=0,...  9.25 us
    all_to_all x1, starting transfers between devices, per_device(): got = lax.all_to_all(sent, 'box', split_axis=0, concat_axis=0, tiled=True)  5.32 us
    gather x1, local copies, waits for them, and re-layouts, per_device(): relayed = jnp.take(table_f.T, jnp.clip(local, 0, rows_f - 1), axis=0).T  5.07 us
  transfers between devices with their start and end apart: 19, of which 5 were waited for; matrix products, arithmetic and copies ran while one was open for 15% of the time, Pallas kernels for 6%

profile of v1, /device:TPU:1, one launch (start us, length us, event | category | flops | bytes accessed | tf_op | source)
XLA Modules:
  0.0 200.3 jit_solution(1573167345425635943)
XLA Ops:
  0.0 0.9 copy.90
  0.9 0.8 compare_select_fusion
  1.7 0.7 broadcast_in_dim.64
  2.4 13.2 %all-to-all-start = ((s32[64,1,160]{2,1,0:T(1,128)}), s32[64,1,160]{2,1,0:T(1,128)S(1)}, u32[]{:S(2)}, u32[]{:S(2)}) async-start(s32[64,1,160]{2,1,0:T(1,128)} %broadcast_in_dim.64), calls=%async_computation | async-start | bytes 131072 | tf_op jit(solution)/shard_map/all_to_all | solution.py:194
  15.5 0.8 constant_dynamic-slice_fusion
  16.4 9.2 %all-to-all-done = s32[64,1,160]{2,1,0:T(1,128)S(1)} async-done(((s32[64,1,160]{2,1,0:T(1,128)}), s32[64,1,160]{2,1,0:T(1,128)S(1)}, u32[]{:S(2)}, u32[]{:S(2)}) %all-to-all-start) | async-done | bytes 40992 | tf_op jit(solution)/shard_map/all_to_all | solution.py:194
  25.6 0.2 reduce.1
  25.8 0.1 reshape.54.idx_ref
  25.9 10.6 %pick.1 = bf16[10240,128]{1,0:T(8,128)(2,1)S(1)} custom-call(s32[10240]{0:T(1024)S(1)} %reshape.54.idx_ref, bf16[1152,128]{1,0:T(8,128)(2,1)S(1)} %pad_maximum_fusion.own_ref), custom_call_target="tpu_custom_call" | custom-call | tf_op jit(solution)/shard_map/pick/pallas_call | solution.py:53
  36.4 1.6 copy-done.1
  38.0 5.3 %all-to-all-start.1 = ((bf16[64,160,128]{2,1,0:T(8,128)(2,1)}), bf16[64,160,128]{2,1,0:T(8,128)(2,1)}, u32[]{:S(2)}, u32[]{:S(2)}) async-start(bf16[64,160,128]{2,1,0:T(8,128)(2,1)} %bitcast.36), calls=%async_computation.1 | async-start | bytes 5242880 | tf_op jit(solution)/shard_map/all_to_all | solution.py:204
  43.4 0.0 copy-start.9
  43.4 4.0 %dynamic-slice_bitcast_fusion = (bf16[8,128,512]{2,1,0:T(8,128)(2,1)}, bf16[8,128,512]{2,1,0:T(8,128)(2,1)}, bf16[8,128,512]{2,1,0:T(8,128)(2,1)}, bf16[8,128,512]{2,1,0:T(8,128)(2,1)S(1)}) fusion(bf16[8,4,128,512]{3,2,1,0:T(8,128)(2,1)} %bitcast.38, s32[]{:T(128)S(6)} %select_n.169, s32[]{:T(128)S(6)} %select_n.167, s32[]{:T(128)S(6)} %select_n.165, ...), kind=kLoop, calls=%fused_computation.1 | loop fusion | bytes 8388624 | tf_op jit(solution)/shard_map/jit(dynamic_index_in_dim)/squeeze | solution.py:210
  47.4 1.2 collective-permute-start.3
  48.6 2.5 %collective-permute-start.4 = (bf16[8,128,512]{2,1,0:T(8,128)(2,1)}, bf16[8,128,512]{2,1,0:T(8,128)(2,1)}, u32[]{:S(2)}, u32[]{:S(2)}) collective-permute-start(bf16[8,128,512]{2,1,0:T(8,128)(2,1)} %get-tuple-element.14), channel_id=1, source_target_pairs={{0,2},{1,3},{2,0},{3,1},{4,6},{5,7},{6,4},{7,5},{8,10},{9,11},{10,... | collective-permute-start | bytes 3145736 | tf_op jit(solution)/shard_map/ppermute | solution.py:185
  51.1 1.2 collective-permute-start.5
  52.3 0.1 reshape.50
  52.4 1.0 copy.88
  53.4 5.1 %gather_fusion = s32[1024,8]{1,0:T(8,128)} fusion(s32[1024,8]{1,0:T(8,128)} %copy.88, s32[1024]{0:T(1024)S(1)} %get-tuple-element.25), kind=kCustom, calls=%fused_computation | custom fusion | bytes 69632 | tf_op jit(solution)/shard_map/jit(_take)/gather | solution.py:228
  58.5 2.2 %select_select_fusion = s32[1024,8]{1,0:T(8,128)} fusion(s32[1024,8]{1,0:T(8,128)} %gather_fusion, pred[1024]{0:T(1024)(128)(4,1)S(1)} %get-tuple-element.27, pred[1024]{0:T(1024)(128)(4,1)S(1)} %get-tuple-element.26), kind=kLoop, calls=%fused_computation.5 | loop fusion | flops 16384 | bytes 67584 | tf_op jit(solution)/shard_map/jit(_where)/select_n | solution.py:229
  60.7 1.2 copy.89
  61.9 0.1 reshape.51
  62.0 0.8 fusion.3
  62.8 0.1 fusion.19
  62.9 0.1 concatenate.19
  63.0 2.1 %collective-permute-start.1 = (s32[8,1216]{1,0:T(8,128)S(1)}, s32[8,1216]{1,0:T(8,128)S(1)}, u32[]{:S(2)}, u32[]{:S(2)}) collective-permute-start(s32[8,1216]{1,0:T(8,128)S(1)} %concatenate.19), channel_id=1, source_target_pairs={{0,2},{1,3},{2,0},{3,1},{4,6},{5,7},{6,4},{7,5},{8,10},{9,11},{10,... | collective-permute-start | bytes 116744 | tf_op jit(solution)/shard_map/ppermute | solution.py:185
  65.1 32.0 %collective-permute-done.2 = s32[8,1216]{1,0:T(8,128)S(1)} collective-permute-done((s32[8,1216]{1,0:T(8,128)S(1)}, s32[8,1216]{1,0:T(8,128)S(1)}, u32[]{:S(2)}, u32[]{:S(2)}) %collective-permute-start.2) | collective-permute-done | bytes 38944 | tf_op jit(solution)/shard_map/ppermute | solution.py:185
  97.1 1.6 collective-permute-start
  98.7 3.9 %collective-permute-done = s32[8,1216]{1,0:T(8,128)S(1)} collective-permute-done((s32[8,1216]{1,0:T(8,128)S(1)}, s32[8,1216]{1,0:T(8,128)S(1)}, u32[]{:S(2)}, u32[]{:S(2)}) %collective-permute-start) | collective-permute-done | bytes 38944 | tf_op jit(solution)/shard_map/ppermute | solution.py:185
  102.6 0.6 copy-done.8
  103.2 0.7 slice.40
  103.9 1.8 reshape.52
  105.6 2.4 %dynamic-slice_reduce_fusion.2 = (s32[32,288]{1,0:T(8,128)}, s32[32,288]{1,0:T(8,128)}, s32[32,288]{1,0:T(8,128)}, s32[32,288]{1,0:T(8,128)S(1)}) fusion(s32[32,4,288]{2,1,0:T(4,128)} %reshape.52, s32[]{:T(128)S(6)} %select_n.165, s32[]{:T(128)S(6)} %select_n.169, s32[]{:T(128)S(6)} %select_n.167, s32[]{:T(128)S(6)} %select_n.160), kind=kLoop, calls=%fused_computation.20 | loop fusion | bytes 294928 | tf_op jit(solution)/shard_map/jit(dynamic_index_in_dim)/dynamic_slice | solution.py:242
  108.1 1.5 reshape.61
  109.6 1.5 reshape.60
  111.1 1.5 reshape.59
  112.6 0.7 pad_add_fusion.4
  113.3 0.1 reshape.58
  113.4 1.5 pad_add_fusion.1.idx_ref
  114.8 0.9 copy-done.4
  115.7 33.6 %translate.3 = (bf16[3,288,512]{2,1,0:T(8,128)(2,1)S(1)}, bf16[64,512]{1,0:T(8,128)(2,1)S(1)}) custom-call(s32[29696]{0:T(1024)S(1)} %copy-done.4, bf16[1152,128]{1,0:T(8,128)(2,1)S(1)} %pad_maximum_fusion.own_ref, bf16[10240,128]{1,0:T(8,128)(2,1)} %bitcast.8.got_ref, bf16[8,128,512]{2,1,0:T(8,128)(2,1)S(1)} %get-tuple-element.16.w0, ...), custom_call_target="tpu_custom_call" | custom-call | tf_op jit(solution)/shard_map/translate/pallas_call | solution.py:119
  149.3 1.5 collective-permute-start.11
  150.9 0.7 collective-permute-start.9
  151.6 0.9 slice_bitcast_fusion
  152.5 2.0 collective-permute-start.6
  154.5 1.2 collective-permute-start.7
  155.7 1.8 collective-permute-start.8
  157.5 0.6 fusion.18
  158.2 5.0 %collective-permute-start.13 = (bf16[32,512]{1,0:T(8,128)(2,1)}, bf16[32,512]{1,0:T(8,128)(2,1)}, u32[]{:S(2)}, u32[]{:S(2)}) collective-permute-start(bf16[32,512]{1,0:T(8,128)(2,1)} %get-tuple-element.21), channel_id=1, source_target_pairs={{4,0},{8,4},{12,8},{16,12},{20,16},{24,20},{28,24},{32,28},{36,32}... | collective-permute-start | bytes 98312 | tf_op jit(solution)/shard_map/ppermute | solution.py:258
  163.2 3.4 %collective-permute-start.12 = (bf16[32,512]{1,0:T(8,128)(2,1)}, bf16[32,512]{1,0:T(8,128)(2,1)}, u32[]{:S(2)}, u32[]{:S(2)}) collective-permute-start(bf16[32,512]{1,0:T(8,128)(2,1)} %get-tuple-element.20), channel_id=1, source_target_pairs={{0,4},{4,8},{8,12},{12,16},{16,20},{20,24},{24,28},{28,32},{32,36}... | collective-permute-start | bytes 98312 | tf_op jit(solution)/shard_map/ppermute | solution.py:257
  166.6 0.1 dynamic_slice.45
  166.7 0.8 copy.96.place_ref
  167.5 0.1 reshape.53.idx_ref
  167.6 12.8 %translate.2 = f32[1,288,512]{2,1,0:T(8,128)S(1)} custom-call(s32[9216]{0:T(1024)S(1)} %reshape.53.idx_ref, bf16[1152,128]{1,0:T(8,128)(2,1)S(1)} %pad_maximum_fusion.own_ref, bf16[10240,128]{1,0:T(8,128)(2,1)} %bitcast.8.got_ref, bf16[8,128,512]{2,1,0:T(8,128)(2,1)S(1)} %get-tuple-element.16.w0, bf16[8,128,512]{2,1,0:T(8,128)(2,1)S(1)} %collective-permute-done.3.w1, ...), custom_call_target="tpu_custom_call" | custom-call | tf_op jit(solution)/shard_map/translate/pallas_call | solution.py:119
  180.5 0.8 pad_maximum_fusion.1.halo_ref
  181.3 2.1 %finish.1 = bf16[256,512]{1,0:T(8,128)(2,1)S(1)} custom-call(f32[288,512]{1,0:T(8,128)S(1)} %bitcast.37, bf16[288,512]{1,0:T(8,128)(2,1)} %collective-permute-done.6.a_ref, bf16[288,512]{1,0:T(8,128)(2,1)} %collective-permute-done.7.b_ref, bf16[288,512]{1,0:T(8,128)(2,1)} %collective-permute-done.8.c_ref, s32[256,1]{1,0:T(8,128)S(1)} %copy-done.3, ...), custom_call_target="tpu_custom_call" | custom-call | tf_op jit(solution)/shard_map/finish/pallas_call | solution.py:159
  183.4 0.2 collective-permute-start.14
  183.6 1.0 collective-permute-start.15
  184.6 1.6 collective-permute-start.16
  186.2 0.1 broadcast_in_dim.54
  186.3 12.3 %collective-permute-done.14 = bf16[256,512]{1,0:T(8,128)(2,1)S(1)} collective-permute-done((bf16[256,512]{1,0:T(8,128)(2,1)S(1)}, bf16[256,512]{1,0:T(8,128)(2,1)S(1)}, u32[]{:S(2)}, u32[]{:S(2)}) %collective-permute-start.14) | collective-permute-done | bytes 262176 | tf_op jit(solution)/shard_map/ppermute | solution.py:185
  198.7 0.3 collective-permute-done.16
  198.9 0.7 copy-done.5
  199.6 0.7 constant_dynamic-update-slice_fusion
  (49 shorter events, 0.4 us)
Async XLA Ops:
  0.0 16.3 %copy-start = (bf16[1024,512]{1,0:T(8,128)(2,1)S(1)}, bf16[1024,512]{1,0:T(8,128)(2,1)}, u32[]{:S(2)}) copy-start(bf16[1024,512]{1,0:T(8,128)(2,1)} %param.9) | copy-start | bytes 3145732
  2.4 23.3 %all-to-all-start = ((s32[64,1,160]{2,1,0:T(1,128)}), s32[64,1,160]{2,1,0:T(1,128)S(1)}, u32[]{:S(2)}, u32[]{:S(2)}) async-start(s32[64,1,160]{2,1,0:T(1,128)} %broadcast_in_dim.64), calls=%async_computation | async-start | bytes 131072 | tf_op jit(solution)/shard_map/all_to_all | solution.py:194
  36.4 1.6 copy-start.1
  38.0 76.8 %all-to-all-start.1 = ((bf16[64,160,128]{2,1,0:T(8,128)(2,1)}), bf16[64,160,128]{2,1,0:T(8,128)(2,1)}, u32[]{:S(2)}, u32[]{:S(2)}) async-start(bf16[64,160,128]{2,1,0:T(8,128)(2,1)} %bitcast.36), calls=%async_computation.1 | async-start | bytes 5242880 | tf_op jit(solution)/shard_map/all_to_all | solution.py:204
  43.4 8.9 %copy-start.11 = (s32[8,128]{1,0:T(8,128)S(1)}, s32[8,128]{1,0:T(8,128)}, u32[]{:S(2)}) copy-start(s32[8,128]{1,0:T(8,128)} %param.14) | copy-start | bytes 12292
  43.4 9.0 %copy-start.9 = (s32[8,1024]{1,0:T(8,128)S(1)}, s32[8,1024]{1,0:T(8,128)}, u32[]{:S(2)}) copy-start(s32[8,1024]{1,0:T(8,128)} %param.11) | copy-start | bytes 98308
  43.4 10.0 %copy-start.10 = (s32[1024]{0:T(1024)S(1)}, s32[1024]{0:T(1024)}, u32[]{:S(2)}) copy-start(s32[1024]{0:T(1024)} %param.17) | copy-start | bytes 12292
  47.4 67.4 %collective-permute-start.3 = (bf16[8,128,512]{2,1,0:T(8,128)(2,1)}, bf16[8,128,512]{2,1,0:T(8,128)(2,1)S(1)}, u32[]{:S(2)}, u32[]{:S(2)}) collective-permute-start(bf16[8,128,512]{2,1,0:T(8,128)(2,1)} %get-tuple-element.15), channel_id=1, source_target_pairs={{0,1},{1,2},{2,3},{3,0},{4,5},{5,6},{6,7},{7,4},{8,9},{9,10},{10,1... | collective-permute-start | bytes 3145736 | tf_op jit(solution)/shard_map/ppermute | solution.py:185
  48.6 66.2 %collective-permute-start.4 = (bf16[8,128,512]{2,1,0:T(8,128)(2,1)}, bf16[8,128,512]{2,1,0:T(8,128)(2,1)}, u32[]{:S(2)}, u32[]{:S(2)}) collective-permute-start(bf16[8,128,512]{2,1,0:T(8,128)(2,1)} %get-tuple-element.14), channel_id=1, source_target_pairs={{0,2},{1,3},{2,0},{3,1},{4,6},{5,7},{6,4},{7,5},{8,10},{9,11},{10,... | collective-permute-start | bytes 3145736 | tf_op jit(solution)/shard_map/ppermute | solution.py:185
  51.1 63.7 %collective-permute-start.5 = (bf16[8,128,512]{2,1,0:T(8,128)(2,1)}, bf16[8,128,512]{2,1,0:T(8,128)(2,1)}, u32[]{:S(2)}, u32[]{:S(2)}) collective-permute-start(bf16[8,128,512]{2,1,0:T(8,128)(2,1)} %get-tuple-element.13), channel_id=1, source_target_pairs={{0,3},{1,0},{2,1},{3,2},{4,7},{5,4},{6,5},{7,6},{8,11},{9,8},{10,9... | collective-permute-start | bytes 3145736 | tf_op jit(solution)/shard_map/ppermute | solution.py:185
  63.0 34.1 %collective-permute-start.2 = (s32[8,1216]{1,0:T(8,128)S(1)}, s32[8,1216]{1,0:T(8,128)S(1)}, u32[]{:S(2)}, u32[]{:S(2)}) collective-permute-start(s32[8,1216]{1,0:T(8,128)S(1)} %concatenate.19), channel_id=1, source_target_pairs={{0,3},{1,0},{2,1},{3,2},{4,7},{5,4},{6,5},{7,6},{8,11},{9,8},{10,9... | collective-permute-start | bytes 116744 | tf_op jit(solution)/shard_map/ppermute | solution.py:185
  63.0 35.7 %collective-permute-start.1 = (s32[8,1216]{1,0:T(8,128)S(1)}, s32[8,1216]{1,0:T(8,128)S(1)}, u32[]{:S(2)}, u32[]{:S(2)}) collective-permute-start(s32[8,1216]{1,0:T(8,128)S(1)} %concatenate.19), channel_id=1, source_target_pairs={{0,2},{1,3},{2,0},{3,1},{4,6},{5,7},{6,4},{7,5},{8,10},{9,11},{10,... | collective-permute-start | bytes 116744 | tf_op jit(solution)/shard_map/ppermute | solution.py:185
  97.1 5.5 %copy-start.6 = (s32[8,1216]{1,0:T(8,128)}, s32[8,1216]{1,0:T(8,128)S(1)}, u32[]{:S(2)}) copy-start(s32[8,1216]{1,0:T(8,128)S(1)} %collective-permute-done.2) | copy-start | bytes 116740
  97.1 5.4 %collective-permute-start = (s32[8,1216]{1,0:T(8,128)S(1)}, s32[8,1216]{1,0:T(8,128)S(1)}, u32[]{:S(2)}, u32[]{:S(2)}) collective-permute-start(s32[8,1216]{1,0:T(8,128)S(1)} %concatenate.19), channel_id=1, source_target_pairs={{0,1},{1,2},{2,3},{3,0},{4,5},{5,6},{6,7},{7,4},{8,9},{9,10},{10,1... | collective-permute-start | bytes 116744 | tf_op jit(solution)/shard_map/ppermute | solution.py:185
  98.7 3.9 %copy-start.7 = (s32[8,1216]{1,0:T(8,128)}, s32[8,1216]{1,0:T(8,128)S(1)}, u32[]{:S(2)}) copy-start(s32[8,1216]{1,0:T(8,128)S(1)} %collective-permute-done.1) | copy-start | bytes 116740
  102.6 0.6 copy-start.8
  114.8 0.9 copy-start.4
  149.3 6.3 %collective-permute-start.11 = (bf16[64,512]{1,0:T(8,128)(2,1)S(1)}, bf16[64,512]{1,0:T(8,128)(2,1)S(1)}, u32[]{:S(2)}, u32[]{:S(2)}) collective-permute-start(bf16[64,512]{1,0:T(8,128)(2,1)S(1)} %get-tuple-element.8), channel_id=1, source_target_pairs={{0,3},{1,0},{2,1},{3,2},{4,7},{5,4},{6,5},{7,6},{8,11},{9,8},{10,9... | collective-permute-start | bytes 196616 | tf_op jit(solution)/shard_map/ppermute | solution.py:185
  150.9 6.6 %collective-permute-start.10 = (bf16[64,512]{1,0:T(8,128)(2,1)S(1)}, bf16[64,512]{1,0:T(8,128)(2,1)S(1)}, u32[]{:S(2)}, u32[]{:S(2)}) collective-permute-start(bf16[64,512]{1,0:T(8,128)(2,1)S(1)} %get-tuple-element.8), channel_id=1, source_target_pairs={{0,2},{1,3},{2,0},{3,1},{4,6},{5,7},{6,4},{7,5},{8,10},{9,11},{10,... | collective-permute-start | bytes 196616 | tf_op jit(solution)/shard_map/ppermute | solution.py:185
  150.9 6.6 %collective-permute-start.9 = (bf16[64,512]{1,0:T(8,128)(2,1)S(1)}, bf16[64,512]{1,0:T(8,128)(2,1)S(1)}, u32[]{:S(2)}, u32[]{:S(2)}) collective-permute-start(bf16[64,512]{1,0:T(8,128)(2,1)S(1)} %get-tuple-element.8), channel_id=1, source_target_pairs={{0,1},{1,2},{2,3},{3,0},{4,5},{5,6},{6,7},{7,4},{8,9},{9,10},{10,1... | collective-permute-start | bytes 196616 | tf_op jit(solution)/shard_map/ppermute | solution.py:185
  152.5 28.8 %collective-permute-start.6 = (bf16[288,512]{1,0:T(8,128)(2,1)}, bf16[288,512]{1,0:T(8,128)(2,1)}, u32[]{:S(2)}, u32[]{:S(2)}) collective-permute-start(bf16[288,512]{1,0:T(8,128)(2,1)} %get-tuple-element.19), channel_id=1, source_target_pairs={{0,1},{1,2},{2,3},{3,0},{4,5},{5,6},{6,7},{7,4},{8,9},{9,10},{10,1... | collective-permute-start | bytes 884744 | tf_op jit(solution)/shard_map/ppermute | solution.py:185
  154.5 26.8 %collective-permute-start.7 = (bf16[288,512]{1,0:T(8,128)(2,1)}, bf16[288,512]{1,0:T(8,128)(2,1)}, u32[]{:S(2)}, u32[]{:S(2)}) collective-permute-start(bf16[288,512]{1,0:T(8,128)(2,1)} %get-tuple-element.18), channel_id=1, source_target_pairs={{0,2},{1,3},{2,0},{3,1},{4,6},{5,7},{6,4},{7,5},{8,10},{9,11},{10,... | collective-permute-start | bytes 884744 | tf_op jit(solution)/shard_map/ppermute | solution.py:185
  155.7 25.6 %collective-permute-start.8 = (bf16[288,512]{1,0:T(8,128)(2,1)}, bf16[288,512]{1,0:T(8,128)(2,1)}, u32[]{:S(2)}, u32[]{:S(2)}) collective-permute-start(bf16[288,512]{1,0:T(8,128)(2,1)} %get-tuple-element.17), channel_id=1, source_target_pairs={{0,3},{1,0},{2,1},{3,2},{4,7},{5,4},{6,5},{7,6},{8,11},{9,8},{10,9... | collective-permute-start | bytes 884744 | tf_op jit(solution)/shard_map/ppermute | solution.py:185
  158.2 22.3 %collective-permute-start.13 = (bf16[32,512]{1,0:T(8,128)(2,1)}, bf16[32,512]{1,0:T(8,128)(2,1)}, u32[]{:S(2)}, u32[]{:S(2)}) collective-permute-start(bf16[32,512]{1,0:T(8,128)(2,1)} %get-tuple-element.21), channel_id=1, source_target_pairs={{4,0},{8,4},{12,8},{16,12},{20,16},{24,20},{28,24},{32,28},{36,32}... | collective-permute-start | bytes 98312 | tf_op jit(solution)/shard_map/ppermute | solution.py:258
  163.2 17.3 %collective-permute-start.12 = (bf16[32,512]{1,0:T(8,128)(2,1)}, bf16[32,512]{1,0:T(8,128)(2,1)}, u32[]{:S(2)}, u32[]{:S(2)}) collective-permute-start(bf16[32,512]{1,0:T(8,128)(2,1)} %get-tuple-element.20), channel_id=1, source_target_pairs={{0,4},{4,8},{8,12},{12,16},{16,20},{20,24},{24,28},{28,32},{32,36}... | collective-permute-start | bytes 98312 | tf_op jit(solution)/shard_map/ppermute | solution.py:257
  167.6 13.7 %copy-start.2 = (bf16[8,512,512]{2,1,0:T(8,128)(2,1)S(1)}, bf16[8,512,512]{2,1,0:T(8,128)(2,1)}, u32[]{:S(2)}) copy-start(bf16[8,512,512]{2,1,0:T(8,128)(2,1)} %l2l_ref.1) | copy-start | bytes 12582916
  167.6 13.7 %copy-start.3 = (s32[256,1]{1,0:T(8,128)S(1)}, s32[256,1]{1,0:T(8,128)}, u32[]{:S(2)}) copy-start(s32[256,1]{1,0:T(8,128)} %copy.96.place_ref) | copy-start | bytes 3076
  183.4 15.2 %collective-permute-start.14 = (bf16[256,512]{1,0:T(8,128)(2,1)S(1)}, bf16[256,512]{1,0:T(8,128)(2,1)S(1)}, u32[]{:S(2)}, u32[]{:S(2)}) collective-permute-start(bf16[256,512]{1,0:T(8,128)(2,1)S(1)} %finish.1), channel_id=1, source_target_pairs={{0,1},{1,2},{2,3},{3,0},{4,5},{5,6},{6,7},{7,4},{8,9},{9,10},{10,1... | collective-permute-start | bytes 786440 | tf_op jit(solution)/shard_map/ppermute | solution.py:185
  183.6 15.0 %collective-permute-start.15 = (bf16[256,512]{1,0:T(8,128)(2,1)S(1)}, bf16[256,512]{1,0:T(8,128)(2,1)S(1)}, u32[]{:S(2)}, u32[]{:S(2)}) collective-permute-start(bf16[256,512]{1,0:T(8,128)(2,1)S(1)} %finish.1), channel_id=1, source_target_pairs={{0,2},{1,3},{2,0},{3,1},{4,6},{5,7},{6,4},{7,5},{8,10},{9,11},{10,... | collective-permute-start | bytes 786440 | tf_op jit(solution)/shard_map/ppermute | solution.py:185
  184.6 14.3 %collective-permute-start.16 = (bf16[256,512]{1,0:T(8,128)(2,1)S(1)}, bf16[256,512]{1,0:T(8,128)(2,1)S(1)}, u32[]{:S(2)}, u32[]{:S(2)}) collective-permute-start(bf16[256,512]{1,0:T(8,128)(2,1)S(1)} %finish.1), channel_id=1, source_target_pairs={{0,3},{1,0},{2,1},{3,2},{4,7},{5,4},{6,5},{7,6},{8,11},{9,8},{10,9... | collective-permute-start | bytes 786440 | tf_op jit(solution)/shard_map/ppermute | solution.py:185
  198.6 1.0 copy-start.5

commit v2 on v0

v2 whole, which is shorter than its diff:
```python
import functools

import jax
import jax.numpy as jnp
from jax import lax
from jax.experimental import pallas as pl
from jax.experimental.pallas import tpu as pltpu
from jax.sharding import PartitionSpec as P

R = 32
LANES = 128
COARSE_FACTOR = 0.5
VMEM_LIMIT = 48 << 20


def widen(source, target, block):
    def step(i, carry):
        first = pl.multiple_of(i * block, block)
        target[pl.ds(first, block), :] = source[pl.ds(first, block), :].astype(jnp.float32)
        return carry

    lax.fori_loop(0, source.shape[0] // block, step, 0)


def gather_rows(lists, table, out, count, unroll):
    def step(i, carry):
        for k in range(unroll):
            r = i * unroll + k
            picked = [table[pl.ds(entries[0, r], 1), :] for entries in lists]
            for s, row in enumerate(picked):
                out[s, pl.ds(r, 1), :] = row
        return carry

    lax.fori_loop(0, count // unroll, step, 0)


def pick_kernel(wanted_ref, own_ref, out_ref, table, rows, sem, *lists):
    copies = [pltpu.make_async_copy(wanted_ref.at[s], entries, sem) for s, entries in enumerate(lists)]
    for copy in copies:
        copy.start()
    count = own_ref.shape[0]
    widen(own_ref, table, 128)
    table[pl.ds(count, 8), :] = jnp.zeros((8, LANES), jnp.float32)
    for copy in copies:
        copy.wait()
    gather_rows(lists, table, rows, rows.shape[1], 2)

    def narrow(s, carry):
        out_ref[s] = rows[s].astype(out_ref.dtype)
        return carry

    lax.fori_loop(0, len(lists), narrow, 0)


def pick(own, wanted):
    parts, _, length = wanted.shape
    vmem = pl.BlockSpec(memory_space=pltpu.VMEM)
    return pl.pallas_call(
        pick_kernel,
        out_shape=jax.ShapeDtypeStruct((parts, length, LANES), own.dtype),
        in_specs=[pl.BlockSpec(memory_space=pl.ANY), vmem],
        out_specs=vmem,
        scratch_shapes=[
            pltpu.VMEM((own.shape[0] + 8, LANES), jnp.float32),
            pltpu.VMEM((parts, length, LANES), jnp.float32),
            pltpu.SemaphoreType.DMA,
        ]
        + [pltpu.SMEM((1, length), jnp.int32)] * parts,
        compiler_params=pltpu.CompilerParams(vmem_limit_bytes=VMEM_LIMIT),
        cost_estimate=pl.CostEstimate(
            flops=0, bytes_accessed=2 * parts * length * LANES * 8, transcendentals=0
        ),
        name="pick",
    )(wanted, own)


def operator_sum(rows, weights, count):
    operators, _, columns = weights.shape
    total = jnp.zeros((count, columns), jnp.float32)
    together = 8
    for first in range(0, operators, together):
        left = jnp.concatenate(
            [rows[first + o, pl.ds(0, count), :].astype(jnp.bfloat16) for o in range(together)],
            axis=1,
        )
        right = weights[pl.ds(first, together)].reshape(together * LANES, columns)
        total = total + jnp.dot(left, right, preferred_element_type=jnp.float32)
    return total


def translate_kernel(shifts, halo, pieces, idx_ref, me_ref, own_ref, got_ref, w0, w1, w2, w3, *refs):
    out_ref, table, landed, rows, weights, got_sem, list_sem, weight_sem = refs[:8]
    lists = refs[8:]
    operators, chunk = rows.shape[:2]
    members = 4
    ops = operators // members
    own, got = own_ref.shape[0], got_ref.shape[0]
    piece = got // pieces
    me = me_ref[0]
    arrivals = [
        pltpu.make_async_copy(
            got_ref.at[pl.ds(n * piece, piece), :], landed.at[pl.ds(n * piece, piece), :], got_sem.at[n]
        )
        for n in range(pieces)
    ]
    stride = (idx_ref.shape[2] - LANES) // members
    sets = [(pl.multiple_of(lax.rem(me + s, members) * stride, LANES), chunk) for s in shifts]
    if halo:
        sets = [(members * stride, halo)] + sets
    copies = []
    for n, (first, _) in enumerate(sets):
        batch = []
        for o in range(operators):
            entries = lists[n * operators + o]
            source = idx_ref.at[o, :, pl.ds(first, entries.shape[1])]
            batch.append(pltpu.make_async_copy(source, entries, list_sem.at[n]))
        copies.append(batch)
    heavy = []
    for s, ref in enumerate((w0, w1, w2, w3)):
        heavy.append(pltpu.make_async_copy(ref, weights.at[pl.ds(s * ops, ops)], weight_sem))
    for copy in arrivals + copies[0] + heavy:
        copy.start()
    for batch in copies[1:]:
        for copy in batch:
            copy.start()
    widen(own_ref, table, 128)
    table[pl.ds(own + got, 8), :] = jnp.zeros((8, LANES), jnp.float32)
    for n, copy in enumerate(arrivals):
        copy.wait()
        widen(
            landed.at[pl.ds(n * piece, piece), :], table.at[pl.ds(own + n * piece, piece), :], 512
        )
    for n, (_, count) in enumerate(sets):
        for copy in copies[n]:
            copy.wait()
        gather_rows(lists[n * operators : (n + 1) * operators], table, rows, count, 4)
        if n == 0:
            for copy in heavy:
                copy.wait()
        total = operator_sum(rows, weights, count).astype(out_ref.dtype)
        if halo and n == 0:
            for m in range(len(shifts)):
                out_ref[m, pl.ds(chunk, halo), :] = total
        else:
            out_ref[n - (1 if halo else 0), pl.ds(0, chunk), :] = total


def translate(idx, me, own, got, weights, chunk, shifts, halo, dtype):
    operators, columns = idx.shape[0], weights[0].shape[2]
    vmem = pl.BlockSpec(memory_space=pltpu.VMEM)
    hbm = pl.BlockSpec(memory_space=pltpu.HBM)
    pieces = 4
    stride = (idx.shape[2] - LANES) // 4
    lengths = ([LANES] if halo else []) + [stride] * len(shifts)
    return pl.pallas_call(
        functools.partial(translate_kernel, shifts, halo, pieces),
        out_shape=jax.ShapeDtypeStruct((len(shifts), chunk + halo, columns), dtype),
        in_specs=[hbm, pl.BlockSpec(memory_space=pltpu.SMEM), vmem, hbm] + [hbm] * 4,
        out_specs=vmem,
        scratch_shapes=[
            pltpu.VMEM((own.shape[0] + got.shape[0] + 8, LANES), jnp.float32),
            pltpu.VMEM(got.shape, got.dtype),
            pltpu.VMEM((operators, chunk, LANES), jnp.float32),
            pltpu.VMEM((operators, LANES, columns), weights[0].dtype),
            pltpu.SemaphoreType.DMA((pieces,)),
            pltpu.SemaphoreType.DMA((len(lengths),)),
            pltpu.SemaphoreType.DMA,
        ]
        + [pltpu.SMEM((1, length), jnp.int32) for length in lengths for _ in range(operators)],
        compiler_params=pltpu.CompilerParams(vmem_limit_bytes=VMEM_LIMIT),
        cost_estimate=pl.CostEstimate(
            flops=2 * operators * LANES * columns * chunk * len(shifts),
            bytes_accessed=2 * operators * (chunk * len(shifts) + halo) * LANES * 8,
            transcendentals=0,
        ),
        name="translate",
    )(idx, me, own, got, *weights)


def children_kernel(own_ref, a_ref, b_ref, c_ref, l2l_ref, out_ref, acc):
    count = out_ref.shape[0] // l2l_ref.shape[0]
    first = own_ref.shape[1] - count
    total = own_ref[0, pl.ds(first, count), :]
    for ref in (a_ref, b_ref, c_ref):
        total = total + ref[pl.ds(first, count), :].astype(jnp.float32)
    parent = (total * COARSE_FACTOR).astype(jnp.bfloat16)
    slabs = acc.shape[0]
    for k in range(l2l_ref.shape[0]):
        child = jnp.dot(parent, l2l_ref[k], preferred_element_type=jnp.float32)
        for j in range(slabs):
            acc[j, pl.ds(k, parent.shape[0], stride=l2l_ref.shape[0]), :] = child[
                :, j * LANES : (j + 1) * LANES
            ]
    for j in range(slabs):
        out_ref[:, j * LANES : (j + 1) * LANES] = acc[j]


def children_of(own, parts, l2l_ops, rows):
    columns = l2l_ops.shape[1]
    vmem = pl.BlockSpec(memory_space=pltpu.VMEM)
    return pl.pallas_call(
        children_kernel,
        out_shape=jax.ShapeDtypeStruct((rows, columns), jnp.float32),
        in_specs=[vmem] * 5,
        out_specs=vmem,
        scratch_shapes=[pltpu.VMEM((columns // LANES, rows, LANES), jnp.float32)],
        compiler_params=pltpu.CompilerParams(vmem_limit_bytes=VMEM_LIMIT),
        name="children",
    )(own, *parts, l2l_ops)


def finish_kernel(own_ref, a_ref, b_ref, c_ref, place_ref, left_ref, right_ref, child_ref, out_ref):
    rows = out_ref.shape[0]
    total = own_ref[0, pl.ds(0, rows), :]
    for ref in (a_ref, b_ref, c_ref):
        total = total + ref[pl.ds(0, rows), :].astype(jnp.float32)
    fine = total.astype(jnp.bfloat16).astype(jnp.float32)
    halo = jnp.concatenate([left_ref[...], right_ref[...]], axis=0)
    spread = (
        lax.broadcasted_iota(jnp.int32, (rows, halo.shape[0]), 1) == place_ref[...]
    ).astype(jnp.bfloat16)
    foreign = jnp.dot(spread, halo, preferred_element_type=jnp.float32)
    out_ref[...] = (child_ref[...] + (fine + foreign)).astype(out_ref.dtype)


def finish(own, parts, place, left, right, children):
    vmem = pl.BlockSpec(memory_space=pltpu.VMEM)
    return pl.pallas_call(
        finish_kernel,
        out_shape=jax.ShapeDtypeStruct(children.shape, jnp.bfloat16),
        in_specs=[vmem] * 8,
        out_specs=vmem,
        compiler_params=pltpu.CompilerParams(vmem_limit_bytes=VMEM_LIMIT),
        name="finish",
    )(own, *parts, place, left, right, children)


def per_device(
    exp_fine, req_fine, src_fine, exp_coarse, req_coarse, src_coarse, operators, l2l_ops, relay_src
):
    members = lax.axis_size("grp")
    me = lax.axis_index("grp")
    blocks = lax.axis_size("box")
    here = lax.axis_index("box")
    rows_f, rows_c = exp_fine.shape[0], exp_coarse.shape[0]
    slots_f, slots_c = req_fine.shape[1], req_coarse.shape[1]
    own_rows, slots = rows_f + rows_c, slots_f + slots_c
    zero_row = own_rows + blocks * slots
    ops, coefficients, _ = operators.shape
    quarter_f, quarter_c = rows_f // members, rows_c // members
    chunk = quarter_f + quarter_c
    me_arg = me[None].astype(jnp.int32)

    def shifted(value, by):
        return lax.ppermute(value, "grp", [(i, (i + by) % members) for i in range(members)])

    requests = jnp.concatenate(
        [
            jnp.where(req_fine >= 0, req_fine, own_rows),
            jnp.where(req_coarse >= 0, req_coarse + rows_f, own_rows),
        ],
        axis=1,
    )[:, None, :]
    wanted = lax.all_to_all(requests, "box", split_axis=0, concat_axis=0, tiled=True)
    own = jnp.concatenate(
        [
            lax.dynamic_slice_in_dim(exp_fine, me * LANES, LANES, 1),
            lax.dynamic_slice_in_dim(exp_coarse, me * LANES, LANES, 1),
        ],
        axis=0,
    )
    raw = jnp.concatenate([src_fine, src_coarse], axis=1)
    own, raw = lax.optimization_barrier((own, raw))
    raws = [raw] + [shifted(raw, s) for s in range(1, members)]
    sent = pick(own, wanted)
    sent, raws = lax.optimization_barrier((sent, raws))
    got = lax.all_to_all(sent, "box", split_axis=0, concat_axis=0, tiled=True)
    got = got.reshape(blocks * slots, LANES)

    by_member = operators.reshape(ops, members, LANES, coefficients)

    def rows_for(member):
        return lax.dynamic_index_in_dim(by_member, member % members, 1, keepdims=False)

    weights = [rows_for(me)] + [shifted(rows_for(me + s), s) for s in range(1, members)]

    raw = jnp.concatenate(raws, axis=0)
    src_f, src_c = raw[:, :rows_f], raw[:, rows_f:]
    q = src_f - rows_f
    table_f = jnp.where(src_f < rows_f, src_f, own_rows + (q // slots_f) * slots + q % slots_f)
    table_f = jnp.where(src_f >= 0, table_f, zero_row)
    q = src_c - rows_c
    table_c = own_rows + (q // slots_c) * slots + slots_f + q % slots_c
    table_c = jnp.where(src_c < rows_c, src_c + rows_f, table_c)
    table_c = jnp.where(src_c >= 0, table_c, zero_row)
    local = relay_src - here * rows_f
    inside = (local >= 0) & (local < rows_f)
    relayed = jnp.take(table_f.T, jnp.clip(local, 0, rows_f - 1), axis=0).T
    relayed = jnp.where(inside[None, :], relayed, zero_row)
    every = members * ops
    gap = -chunk % LANES
    chunks = jnp.concatenate(
        [
            relayed.reshape(every, members, quarter_f),
            table_c.reshape(every, members, quarter_c),
            jnp.full((every, members, gap), zero_row, jnp.int32),
        ],
        axis=2,
    )
    idx = jnp.concatenate(
        [
            chunks.reshape(every, -1),
            table_f[:, :R],
            table_f[:, rows_f - R :],
            jnp.full((every, LANES - 2 * R), zero_row, jnp.int32),
        ],
        axis=1,
    )[:, None, :]
    place = jnp.where(local < 0, local + R, jnp.where(local >= rows_f, local - rows_f + R, -1))
    place = lax.dynamic_slice_in_dim(place, me * quarter_f, quarter_f, 0)[:, None]
    got, place, idx = lax.optimization_barrier((got, place, idx))

    def sums(shifts, halo, dtype):
        return translate(idx, me_arg, own, got, weights, chunk, shifts, halo, dtype)

    away = sums((2, 1, 3), 2 * R, jnp.bfloat16)
    others = [shifted(away[n], s) for n, s in enumerate((2, 1, 3))]
    mine = sums((0,), 0, jnp.float32)
    others, mine = lax.optimization_barrier((others, mine))
    edge = away[0, chunk:].astype(jnp.float32)
    for other in others:
        edge = edge + other[chunk:].astype(jnp.float32)
    edge = edge.astype(jnp.bfloat16)
    from_left = lax.ppermute(edge[R:], "box", [(i, i + 1) for i in range(blocks - 1)])
    from_right = lax.ppermute(edge[:R], "box", [(i + 1, i) for i in range(blocks - 1)])
    children = children_of(mine, others, l2l_ops, quarter_f)
    done = finish(mine, others, place, from_left, from_right, children)
    out = jnp.zeros((rows_f, coefficients), jnp.bfloat16)
    for s in range(members):
        piece = done if s == 0 else shifted(done, s)
        out = lax.dynamic_update_slice_in_dim(out, piece, ((me - s) % members) * quarter_f, 0)
    return out


def solution(mesh):
    return jax.shard_map(
        per_device,
        mesh=mesh,
        in_specs=(
            P("box", None),
            P("box", None),
            P(("box", "grp"), None),
            P("box", None),
            P("box", None),
            P(("box", "grp"), None),
            P("grp", None, None),
            P(),
            P("box"),
        ),
        out_specs=P("box", None),
        check_vma=False,
    )
```

time: 420 us -> 179 us (0.43)
  waiting for transfers between devices: 179 us -> 70.3 us
  local copies, waits for them, and re-layouts: 92.7 us -> 18 us
  blocking collectives: 64.9 us -> 0 us
  Pallas kernels: 0 us -> 45.2 us
  other arithmetic: 31.6 us -> 3.96 us
  matrix products: 14.5 us -> 0 us
  starting transfers between devices: 35.2 us -> 40.5 us
    all_to_all x3 -> x2, waiting for transfers between devices: 179 us -> 50.5 us  [the longest x1 46.8 us: per_device(): got = lax.all_to_all(sent, 'box', split_axis=0, concat_axis=0, tiled=True)]
    gather x5 -> x1, local copies, waits for them, and re-layouts: 90.1 us -> 2.81 us  [per_device(): relayed = jnp.take(table_f.T, jnp.clip(local, 0, rows_f - 1), axis=0).T]
    pallas_call x0 -> x5, Pallas kernels: none -> 45.2 us  [the longest x2 33.9 us: translate(): pl.pallas_call(functools.partial(translate_kernel, shifts, halo, pieces),...]
    psum x1 -> x0, blocking collectives: 42.6 us -> none  [far_field(): return lax.psum(summed * level_factor, 'grp').astype(jnp.bfloat16)]
    all_to_all x1 -> x0, blocking collectives: 22.3 us -> none  [fetched(): lax.all_to_all(requests, 'box', split_axis=0, concat_axis=0, tiled=True)]
    ppermute x2 -> x14, waiting for transfers between devices: 0.27 us -> 19.9 us  [the longest x12 19.9 us: shifted(): lax.ppermute(value, 'grp', [(i, (i + by) % members) for i in range(member...]
    concatenate x3 -> x4, other arithmetic: 16.6 us -> 0.85 us  [the longest x1 0.78 us: per_device(): raw = jnp.concatenate([src_fine, src_coarse], axis=1)]
    dot_general x3 -> x0, matrix products: 14.5 us -> none  [the longest x2 11.5 us: far_field(): jnp.einsum('okp,opq->kq', picked, operators, preferred_element_type=jnp.f...]
  transfers between devices with their start and end apart: 5 -> 16, of which waited for: 3 -> 5; matrix products, arithmetic and copies ran while one was open for 16% -> 7% of each run, Pallas kernels for 0% -> 11%
where the time goes in v2:
time: 179 us; the launch traced here: 178 us
  waiting for transfers between devices  70.3 us (39%)
  Pallas kernels  45.2 us (25%)
  starting transfers between devices  40.5 us (23%)
  local copies, waits for them, and re-layouts  18 us (10%)
  other arithmetic  3.96 us (2%)
    all_to_all x1, waiting for transfers between devices, per_device(): got = lax.all_to_all(sent, 'box', split_axis=0, concat_axis=0, tiled=True)  46.8 us
    pallas_call x2, Pallas kernels, translate(): pl.pallas_call(functools.partial(translate_kernel, shifts, halo, pieces),...  33.9 us
    ppermute x12, waiting for transfers between devices, shifted(): lax.ppermute(value, 'grp', [(i, (i + by) % members) for i in range(member...  19.9 us
    ppermute x12, starting transfers between devices, shifted(): lax.ppermute(value, 'grp', [(i, (i + by) % members) for i in range(member...  14.1 us
    all_to_all x1, starting transfers between devices, per_device(): lax.all_to_all(requests, 'box', split_axis=0, concat_axis=0, tiled=True)  13.2 us
    pallas_call x1, Pallas kernels, pick(): pl.pallas_call(pick_kernel, out_shape=jax.ShapeDtypeStruct((parts, length...  7.93 us
    all_to_all x1, starting transfers between devices, per_device(): got = lax.all_to_all(sent, 'box', split_axis=0, concat_axis=0, tiled=True)  7.68 us
    unnamed x23, local copies, waits for them, and re-layouts  6.57 us
  transfers between devices with their start and end apart: 16, of which 5 were waited for; matrix products, arithmetic and copies ran while one was open for 7% of the time, Pallas kernels for 11%

profile of v2, /device:TPU:1, one launch (start us, length us, event | category | flops | bytes accessed | tf_op | source)
XLA Modules:
  0.0 178.4 jit_solution(4686155036778334273)
XLA Ops:
  0.0 0.9 copy.18
  0.9 0.8 compare_select_fusion.1
  1.7 0.7 broadcast_in_dim.69
  2.4 13.2 %all-to-all-start = ((s32[64,1,160]{2,1,0:T(1,128)}), s32[64,1,160]{2,1,0:T(1,128)S(1)}, u32[]{:S(2)}, u32[]{:S(2)}) async-start(s32[64,1,160]{2,1,0:T(1,128)} %broadcast_in_dim.69), calls=%async_computation | async-start | bytes 131072 | tf_op jit(solution)/shard_map/all_to_all | solution.py:264
  15.6 0.8 constant_dynamic-slice_fusion
  16.4 0.8 pad_add_fusion.1
  17.2 1.2 collective-permute-start
  18.4 2.5 %collective-permute-start.1 = (s32[8,1152]{1,0:T(8,128)S(1)}, s32[8,1152]{1,0:T(8,128)S(1)}, u32[]{:S(2)}, u32[]{:S(2)}) collective-permute-start(s32[8,1152]{1,0:T(8,128)S(1)} %pad_add_fusion.1), channel_id=1, source_target_pairs={{0,2},{1,3},{2,0},{3,1},{4,6},{5,7},{6,4},{7,5},{8,10},{9,11},{10,... | collective-permute-start | bytes 110600 | tf_op jit(solution)/shard_map/ppermute | solution.py:255
  20.8 1.2 collective-permute-start.2
  22.0 3.6 %all-to-all-done.wanted_ref = s32[64,1,160]{2,1,0:T(1,128)S(1)} async-done(((s32[64,1,160]{2,1,0:T(1,128)}), s32[64,1,160]{2,1,0:T(1,128)S(1)}, u32[]{:S(2)}, u32[]{:S(2)}) %all-to-all-start) | async-done | bytes 40992 | tf_op jit(solution)/shard_map/all_to_all | solution.py:264
  25.6 7.9 %pick.1 = bf16[64,160,128]{2,1,0:T(8,128)(2,1)S(1)} custom-call(s32[64,1,160]{2,1,0:T(1,128)S(1)} %all-to-all-done.wanted_ref, bf16[1152,128]{1,0:T(8,128)(2,1)S(1)} %pad_maximum_fusion.own_ref), custom_call_target="tpu_custom_call" | custom-call | bytes 20971520 | tf_op jit(solution)/shard_map/pick/pallas_call | solution.py:58
  33.6 1.5 copy-done.1
  35.1 0.0 collective-permute-done
  35.1 7.7 %all-to-all-start.1 = ((bf16[64,160,128]{2,1,0:T(8,128)(2,1)}), bf16[64,160,128]{2,1,0:T(8,128)(2,1)}, u32[]{:S(2)}, u32[]{:S(2)}) async-start(bf16[64,160,128]{2,1,0:T(8,128)(2,1)} %copy-done.1), calls=%async_computation.1 | async-start | bytes 5242880 | tf_op jit(solution)/shard_map/all_to_all | solution.py:277
  42.8 0.0 copy-start.8
  42.9 3.9 %dynamic-slice_bitcast_fusion = (bf16[8,128,512]{2,1,0:T(8,128)(2,1)}, bf16[8,128,512]{2,1,0:T(8,128)(2,1)}, bf16[8,128,512]{2,1,0:T(8,128)(2,1)}, bf16[8,128,512]{2,1,0:T(8,128)(2,1)S(1)}) fusion(bf16[8,4,128,512]{3,2,1,0:T(8,128)(2,1)} %bitcast.38, s32[]{:T(128)S(6)} %select_n.159, s32[]{:T(128)S(6)} %select_n.157, s32[]{:T(128)S(6)} %select_n.155, ...), kind=kLoop, calls=%fused_computation.1 | loop fusion | bytes 8388624 | tf_op jit(solution)/shard_map/jit(dynamic_index_in_dim)/squeeze | solution.py:283
  46.8 0.3 collective-permute-start.3
  47.1 1.0 collective-permute-start.4
  48.1 1.4 collective-permute-start.5
  49.5 0.1 pad.2.clone
  49.6 0.6 dynamic_slice.24
  50.3 0.7 copy-done.7
  51.0 0.1 fusion.23
  51.1 0.2 copy.20
  51.3 2.8 %gather_fusion = s32[1024,32]{1,0:T(8,128)S(1)} fusion(s32[1024,32]{1,0:T(8,128)S(1)} %copy.20, s32[1024]{0:T(1024)S(1)} %get-tuple-element.46), kind=kCustom, calls=%fused_computation | custom fusion | bytes 266240 | tf_op jit(solution)/shard_map/jit(_take)/gather | solution.py:298
  54.1 0.3 select_select_fusion
  54.5 0.2 copy.21
  54.7 0.7 fusion.15
  55.4 0.1 reshape.25
  55.6 1.1 fusion.3
  56.6 0.1 fusion.21
  56.7 0.1 concatenate.23
  56.8 0.1 broadcast_in_dim.81.idx_ref
  56.9 46.8 %all-to-all-done.1 = bf16[64,160,128]{2,1,0:T(8,128)(2,1)} async-done(((bf16[64,160,128]{2,1,0:T(8,128)(2,1)}), bf16[64,160,128]{2,1,0:T(8,128)(2,1)}, u32[]{:S(2)}, u32[]{:S(2)}) %all-to-all-start.1) | async-done | bytes 2621472 | tf_op jit(solution)/shard_map/all_to_all | solution.py:277
  103.8 0.0 collective-permute-done.5.w3
  103.8 25.1 %translate.2 = bf16[3,352,512]{2,1,0:T(8,128)(2,1)S(1)} custom-call(s32[32,1,1664]{2,1,0:T(1,128)S(1)} %broadcast_in_dim.81.idx_ref, s32[1]{0:T(128)} %bitcast.5.me_ref, bf16[1152,128]{1,0:T(8,128)(2,1)S(1)} %pad_maximum_fusion.own_ref, bf16[10240,128]{1,0:T(8,128)(2,1)} %bitcast.got_ref, bf16[8,128,512]{2,1,0:T(8,128)(2,1)S(1)} %get-tuple-element.36.w0, ...), custom_call_target="tpu_custom_call" | custom-call | flops 3623878656 | bytes 60817408 | tf_op jit(solution)/shard_map/translate/pallas_call | solution.py:155
  128.8 0.1 slice_bitcast_fusion
  128.9 0.9 collective-permute-start.6
  129.9 0.3 collective-permute-start.7
  130.2 2.4 %collective-permute-start.8 = (bf16[352,512]{1,0:T(8,128)(2,1)S(1)}, bf16[352,512]{1,0:T(8,128)(2,1)S(1)}, u32[]{:S(2)}, u32[]{:S(2)}) collective-permute-start(bf16[352,512]{1,0:T(8,128)(2,1)S(1)} %get-tuple-element.37), channel_id=1, source_target_pairs={{0,3},{1,0},{2,1},{3,2},{4,7},{5,4},{6,5},{7,6},{8,11},{9,8},{10,9... | collective-permute-start | bytes 1081352 | tf_op jit(solution)/shard_map/ppermute | solution.py:255
  132.5 8.8 %translate.3.own_ref = f32[1,288,512]{2,1,0:T(8,128)S(1)} custom-call(s32[32,1,1664]{2,1,0:T(1,128)S(1)} %broadcast_in_dim.81.idx_ref, s32[1]{0:T(128)} %bitcast.5.me_ref, bf16[1152,128]{1,0:T(8,128)(2,1)S(1)} %pad_maximum_fusion.own_ref, bf16[10240,128]{1,0:T(8,128)(2,1)} %bitcast.got_ref, bf16[8,128,512]{2,1,0:T(8,128)(2,1)S(1)} %get-tuple-element.36.w0, ...), custom_call_target="tpu_custom_call" | custom-call | flops 1207959552 | bytes 18874368 | tf_op jit(solution)/shard_map/translate/pallas_call | solution.py:155
  141.4 0.0 collective-permute-done.6.a_ref
  141.4 7.2 %collective-permute-done.7.b_ref = bf16[352,512]{1,0:T(8,128)(2,1)S(1)} collective-permute-done((bf16[352,512]{1,0:T(8,128)(2,1)S(1)}, bf16[352,512]{1,0:T(8,128)(2,1)S(1)}, u32[]{:S(2)}, u32[]{:S(2)}) %collective-permute-start.7) | collective-permute-done | bytes 360480 | tf_op jit(solution)/shard_map/ppermute | solution.py:255
  148.6 0.0 collective-permute-done.8.c_ref
  148.6 0.0 copy-start.2
  148.6 0.7 copy-done.2
  149.4 0.7 copy-done.4
  150.1 2.4 %collective-permute-start.10 = (bf16[32,512]{1,0:T(8,128)(2,1)S(1)}, bf16[32,512]{1,0:T(8,128)(2,1)S(1)}, u32[]{:S(2)}, u32[]{:S(2)}) collective-permute-start(bf16[32,512]{1,0:T(8,128)(2,1)S(1)} %get-tuple-element.42), channel_id=1, source_target_pairs={{4,0},{8,4},{12,8},{16,12},{20,16},{24,20},{28,24},{32,28},{36,32}... | collective-permute-start | bytes 98312 | tf_op jit(solution)/shard_map/ppermute | solution.py:335
  152.5 3.2 %collective-permute-start.9 = (bf16[32,512]{1,0:T(8,128)(2,1)S(1)}, bf16[32,512]{1,0:T(8,128)(2,1)S(1)}, u32[]{:S(2)}, u32[]{:S(2)}) collective-permute-start(bf16[32,512]{1,0:T(8,128)(2,1)S(1)} %get-tuple-element.43), channel_id=1, source_target_pairs={{0,4},{4,8},{8,12},{12,16},{16,20},{20,24},{24,28},{28,32},{32,36}... | collective-permute-start | bytes 98312 | tf_op jit(solution)/shard_map/ppermute | solution.py:334
  155.7 0.7 copy.26.place_ref
  156.4 0.0 copy-start.3
  156.4 1.0 copy-done.3
  157.4 1.0 copy-done.5
  158.4 3.1 %children.1.child_ref = f32[256,512]{1,0:T(8,128)S(1)} custom-call(f32[1,288,512]{2,1,0:T(8,128)S(1)} %translate.3.own_ref, bf16[352,512]{1,0:T(8,128)(2,1)S(1)} %collective-permute-done.6.a_ref, bf16[352,512]{1,0:T(8,128)(2,1)S(1)} %copy-done.3, bf16[352,512]{1,0:T(8,128)(2,1)S(1)} %copy-done.5, bf16[8,512,512]{2,1,0:T(8,128)(2,1)} %l2l_ref.1), custom_call_target="tpu_custom_call" | custom-call | tf_op jit(solution)/shard_map/children/pallas_call | solution.py:201
  161.5 0.0 collective-permute-done.9.left_ref
  161.5 0.3 finish.1
  161.8 0.4 collective-permute-start.11
  162.2 1.4 collective-permute-start.12
  163.6 1.2 collective-permute-start.13
  164.8 0.1 broadcast_in_dim.66
  164.9 11.6 %collective-permute-done.11 = bf16[256,512]{1,0:T(8,128)(2,1)S(1)} collective-permute-done((bf16[256,512]{1,0:T(8,128)(2,1)S(1)}, bf16[256,512]{1,0:T(8,128)(2,1)S(1)}, u32[]{:S(2)}, u32[]{:S(2)}) %collective-permute-start.11) | collective-permute-done | bytes 262176 | tf_op jit(solution)/shard_map/ppermute | solution.py:255
  176.5 0.0 copy-start.6
  176.5 1.1 collective-permute-done.13
  177.7 0.7 constant_dynamic-update-slice_fusion.4
  (33 shorter events, 0.3 us)
Async XLA Ops:
  0.0 15.5 %copy-start = (bf16[1024,512]{1,0:T(8,128)(2,1)S(1)}, bf16[1024,512]{1,0:T(8,128)(2,1)}, u32[]{:S(2)}) copy-start(bf16[1024,512]{1,0:T(8,128)(2,1)} %param.9) | copy-start | bytes 3145732
  2.4 23.3 %all-to-all-start = ((s32[64,1,160]{2,1,0:T(1,128)}), s32[64,1,160]{2,1,0:T(1,128)S(1)}, u32[]{:S(2)}, u32[]{:S(2)}) async-start(s32[64,1,160]{2,1,0:T(1,128)} %broadcast_in_dim.69), calls=%async_computation | async-start | bytes 131072 | tf_op jit(solution)/shard_map/all_to_all | solution.py:264
  17.2 17.9 %collective-permute-start = (s32[8,1152]{1,0:T(8,128)S(1)}, s32[8,1152]{1,0:T(8,128)S(1)}, u32[]{:S(2)}, u32[]{:S(2)}) collective-permute-start(s32[8,1152]{1,0:T(8,128)S(1)} %pad_add_fusion.1), channel_id=1, source_target_pairs={{0,1},{1,2},{2,3},{3,0},{4,5},{5,6},{6,7},{7,4},{8,9},{9,10},{10,1... | collective-permute-start | bytes 110600 | tf_op jit(solution)/shard_map/ppermute | solution.py:255
  18.4 16.7 %collective-permute-start.1 = (s32[8,1152]{1,0:T(8,128)S(1)}, s32[8,1152]{1,0:T(8,128)S(1)}, u32[]{:S(2)}, u32[]{:S(2)}) collective-permute-start(s32[8,1152]{1,0:T(8,128)S(1)} %pad_add_fusion.1), channel_id=1, source_target_pairs={{0,2},{1,3},{2,0},{3,1},{4,6},{5,7},{6,4},{7,5},{8,10},{9,11},{10,... | collective-permute-start | bytes 110600 | tf_op jit(solution)/shard_map/ppermute | solution.py:255
  20.8 14.3 %collective-permute-start.2 = (s32[8,1152]{1,0:T(8,128)S(1)}, s32[8,1152]{1,0:T(8,128)S(1)}, u32[]{:S(2)}, u32[]{:S(2)}) collective-permute-start(s32[8,1152]{1,0:T(8,128)S(1)} %pad_add_fusion.1), channel_id=1, source_target_pairs={{0,3},{1,0},{2,1},{3,2},{4,7},{5,4},{6,5},{7,6},{8,11},{9,8},{10,9... | collective-permute-start | bytes 110600 | tf_op jit(solution)/shard_map/ppermute | solution.py:255
  33.5 1.5 copy-start.1
  35.1 68.7 %all-to-all-start.1 = ((bf16[64,160,128]{2,1,0:T(8,128)(2,1)}), bf16[64,160,128]{2,1,0:T(8,128)(2,1)}, u32[]{:S(2)}, u32[]{:S(2)}) async-start(bf16[64,160,128]{2,1,0:T(8,128)(2,1)} %copy-done.1), calls=%async_computation.1 | async-start | bytes 5242880 | tf_op jit(solution)/shard_map/all_to_all | solution.py:277
  42.8 6.8 %copy-start.8 = (s32[1024]{0:T(1024)S(1)}, s32[1024]{0:T(1024)}, u32[]{:S(2)}) copy-start(s32[1024]{0:T(1024)} %param.17) | copy-start | bytes 12292
  46.8 57.0 %collective-permute-start.3 = (bf16[8,128,512]{2,1,0:T(8,128)(2,1)}, bf16[8,128,512]{2,1,0:T(8,128)(2,1)}, u32[]{:S(2)}, u32[]{:S(2)}) collective-permute-start(bf16[8,128,512]{2,1,0:T(8,128)(2,1)} %get-tuple-element.35), channel_id=1, source_target_pairs={{0,1},{1,2},{2,3},{3,0},{4,5},{5,6},{6,7},{7,4},{8,9},{9,10},{10,1... | collective-permute-start | bytes 3145736 | tf_op jit(solution)/shard_map/ppermute | solution.py:255
  47.1 56.7 %collective-permute-start.4 = (bf16[8,128,512]{2,1,0:T(8,128)(2,1)}, bf16[8,128,512]{2,1,0:T(8,128)(2,1)}, u32[]{:S(2)}, u32[]{:S(2)}) collective-permute-start(bf16[8,128,512]{2,1,0:T(8,128)(2,1)} %get-tuple-element.34), channel_id=1, source_target_pairs={{0,2},{1,3},{2,0},{3,1},{4,6},{5,7},{6,4},{7,5},{8,10},{9,11},{10,... | collective-permute-start | bytes 3145736 | tf_op jit(solution)/shard_map/ppermute | solution.py:255
  48.1 55.7 %collective-permute-start.5 = (bf16[8,128,512]{2,1,0:T(8,128)(2,1)}, bf16[8,128,512]{2,1,0:T(8,128)(2,1)}, u32[]{:S(2)}, u32[]{:S(2)}) collective-permute-start(bf16[8,128,512]{2,1,0:T(8,128)(2,1)} %get-tuple-element.33), channel_id=1, source_target_pairs={{0,3},{1,0},{2,1},{3,2},{4,7},{5,4},{6,5},{7,6},{8,11},{9,8},{10,9... | collective-permute-start | bytes 3145736 | tf_op jit(solution)/shard_map/ppermute | solution.py:255
  50.3 0.7 copy-start.7
  128.9 12.4 %collective-permute-start.6 = (bf16[352,512]{1,0:T(8,128)(2,1)S(1)}, bf16[352,512]{1,0:T(8,128)(2,1)S(1)}, u32[]{:S(2)}, u32[]{:S(2)}) collective-permute-start(bf16[352,512]{1,0:T(8,128)(2,1)S(1)} %get-tuple-element.39), channel_id=1, source_target_pairs={{0,2},{1,3},{2,0},{3,1},{4,6},{5,7},{6,4},{7,5},{8,10},{9,11},{10,... | collective-permute-start | bytes 1081352 | tf_op jit(solution)/shard_map/ppermute | solution.py:255
  129.9 18.7 %collective-permute-start.7 = (bf16[352,512]{1,0:T(8,128)(2,1)S(1)}, bf16[352,512]{1,0:T(8,128)(2,1)S(1)}, u32[]{:S(2)}, u32[]{:S(2)}) collective-permute-start(bf16[352,512]{1,0:T(8,128)(2,1)S(1)} %get-tuple-element.38), channel_id=1, source_target_pairs={{0,1},{1,2},{2,3},{3,0},{4,5},{5,6},{6,7},{7,4},{8,9},{9,10},{10,1... | collective-permute-start | bytes 1081352 | tf_op jit(solution)/shard_map/ppermute | solution.py:255
  130.2 18.4 %collective-permute-start.8 = (bf16[352,512]{1,0:T(8,128)(2,1)S(1)}, bf16[352,512]{1,0:T(8,128)(2,1)S(1)}, u32[]{:S(2)}, u32[]{:S(2)}) collective-permute-start(bf16[352,512]{1,0:T(8,128)(2,1)S(1)} %get-tuple-element.37), channel_id=1, source_target_pairs={{0,3},{1,0},{2,1},{3,2},{4,7},{5,4},{6,5},{7,6},{8,11},{9,8},{10,9... | collective-permute-start | bytes 1081352 | tf_op jit(solution)/shard_map/ppermute | solution.py:255
  148.6 0.7 copy-start.2
  149.4 0.7 copy-start.4
  150.1 11.4 %collective-permute-start.10 = (bf16[32,512]{1,0:T(8,128)(2,1)S(1)}, bf16[32,512]{1,0:T(8,128)(2,1)S(1)}, u32[]{:S(2)}, u32[]{:S(2)}) collective-permute-start(bf16[32,512]{1,0:T(8,128)(2,1)S(1)} %get-tuple-element.42), channel_id=1, source_target_pairs={{4,0},{8,4},{12,8},{16,12},{20,16},{24,20},{28,24},{32,28},{36,32}... | collective-permute-start | bytes 98312 | tf_op jit(solution)/shard_map/ppermute | solution.py:335
  152.5 9.0 %collective-permute-start.9 = (bf16[32,512]{1,0:T(8,128)(2,1)S(1)}, bf16[32,512]{1,0:T(8,128)(2,1)S(1)}, u32[]{:S(2)}, u32[]{:S(2)}) collective-permute-start(bf16[32,512]{1,0:T(8,128)(2,1)S(1)} %get-tuple-element.43), channel_id=1, source_target_pairs={{0,4},{4,8},{8,12},{12,16},{16,20},{20,24},{24,28},{28,32},{32,36}... | collective-permute-start | bytes 98312 | tf_op jit(solution)/shard_map/ppermute | solution.py:334
  156.4 1.0 copy-start.3
  157.4 1.0 copy-start.5
  161.8 14.7 %collective-permute-start.11 = (bf16[256,512]{1,0:T(8,128)(2,1)S(1)}, bf16[256,512]{1,0:T(8,128)(2,1)S(1)}, u32[]{:S(2)}, u32[]{:S(2)}) collective-permute-start(bf16[256,512]{1,0:T(8,128)(2,1)S(1)} %finish.1), channel_id=1, source_target_pairs={{0,1},{1,2},{2,3},{3,0},{4,5},{5,6},{6,7},{7,4},{8,9},{9,10},{10,1... | collective-permute-start | bytes 786440 | tf_op jit(solution)/shard_map/ppermute | solution.py:255
  162.2 14.3 %collective-permute-start.12 = (bf16[256,512]{1,0:T(8,128)(2,1)S(1)}, bf16[256,512]{1,0:T(8,128)(2,1)S(1)}, u32[]{:S(2)}, u32[]{:S(2)}) collective-permute-start(bf16[256,512]{1,0:T(8,128)(2,1)S(1)} %finish.1), channel_id=1, source_target_pairs={{0,2},{1,3},{2,0},{3,1},{4,6},{5,7},{6,4},{7,5},{8,10},{9,11},{10,... | collective-permute-start | bytes 786440 | tf_op jit(solution)/shard_map/ppermute | solution.py:255
  163.6 14.0 %collective-permute-start.13 = (bf16[256,512]{1,0:T(8,128)(2,1)S(1)}, bf16[256,512]{1,0:T(8,128)(2,1)S(1)}, u32[]{:S(2)}, u32[]{:S(2)}) collective-permute-start(bf16[256,512]{1,0:T(8,128)(2,1)S(1)} %finish.1), channel_id=1, source_target_pairs={{0,3},{1,0},{2,1},{3,2},{4,7},{5,4},{6,5},{7,6},{8,11},{9,8},{10,9... | collective-permute-start | bytes 786440 | tf_op jit(solution)/shard_map/ppermute | solution.py:255
  176.5 1.1 copy-start.6

commit v3 on v2

v3 whole, which is shorter than its diff:
```python
import functools

import jax
import jax.numpy as jnp
from jax import lax
from jax.experimental import pallas as pl
from jax.experimental.pallas import tpu as pltpu
from jax.sharding import PartitionSpec as P

R = 32
LANES = 128
CORES = 2
COARSE_FACTOR = 0.5
VMEM_LIMIT = 48 << 20


def widen(source, target, block):
    def step(i, carry):
        first = pl.multiple_of(i * block, block)
        target[pl.ds(first, block), :] = source[pl.ds(first, block), :].astype(jnp.float32)
        return carry

    lax.fori_loop(0, source.shape[0] // block, step, 0)


def gather_rows(lists, table, out, count, unroll):
    def step(i, carry):
        for k in range(unroll):
            r = i * unroll + k
            picked = [table[pl.ds(entries[0, r], 1), :] for entries in lists]
            for s, row in enumerate(picked):
                out[s, pl.ds(r, 1), :] = row
        return carry

    lax.fori_loop(0, count // unroll, step, 0)


def pick_kernel(wanted_ref, own_ref, out_ref, table, rows, sem, *lists):
    copies = [pltpu.make_async_copy(wanted_ref.at[s], entries, sem) for s, entries in enumerate(lists)]
    for copy in copies:
        copy.start()
    count = own_ref.shape[0]
    widen(own_ref, table, 128)
    table[pl.ds(count, 8), :] = jnp.zeros((8, LANES), jnp.float32)
    for copy in copies:
        copy.wait()
    gather_rows(lists, table, rows, rows.shape[1], 2)

    def narrow(s, carry):
        out_ref[s] = rows[s].astype(out_ref.dtype)
        return carry

    lax.fori_loop(0, len(lists), narrow, 0)


def pick(own, wanted):
    parts, _, length = wanted.shape
    vmem = pl.BlockSpec(memory_space=pltpu.VMEM)
    return pl.pallas_call(
        pick_kernel,
        out_shape=jax.ShapeDtypeStruct((parts, length, LANES), own.dtype),
        in_specs=[pl.BlockSpec(memory_space=pl.ANY), vmem],
        out_specs=vmem,
        scratch_shapes=[
            pltpu.VMEM((own.shape[0] + 8, LANES), jnp.float32),
            pltpu.VMEM((parts, length, LANES), jnp.float32),
            pltpu.SemaphoreType.DMA,
        ]
        + [pltpu.SMEM((1, length), jnp.int32)] * parts,
        compiler_params=pltpu.CompilerParams(vmem_limit_bytes=VMEM_LIMIT),
        cost_estimate=pl.CostEstimate(
            flops=0, bytes_accessed=2 * parts * length * LANES * 8, transcendentals=0
        ),
        name="pick",
    )(wanted, own)


def operator_sum(rows, weights, count):
    operators, _, columns = weights.shape
    total = jnp.zeros((count, columns), jnp.float32)
    together = 8
    for first in range(0, operators, together):
        left = jnp.concatenate(
            [rows[first + o, pl.ds(0, count), :].astype(jnp.bfloat16) for o in range(together)],
            axis=1,
        )
        right = weights[pl.ds(first, together)].reshape(together * LANES, columns)
        total = total + jnp.dot(left, right, preferred_element_type=jnp.float32)
    return total


def translate_kernel(shifts, halo, idx_ref, at_ref, own_ref, got_ref, ops_ref, *refs):
    weight_refs, refs = refs[:6], refs[6:]
    outs, refs = refs[: len(shifts)], refs[len(shifts) :]
    table, landed, rows, weights, got_sem, list_sem, weight_sem = refs[:7]
    lists = refs[7:]
    operators, chunk = rows.shape[:2]
    members, ops = 4, ops_ref.shape[0]
    me, core = at_ref[0], at_ref[1]
    own, got = own_ref.shape[0], landed.shape[0]
    piece = got // got_sem.shape[0]
    arrivals = []
    for n in range(got // piece):
        part = pl.ds(n * piece, piece)
        arrivals.append(
            pltpu.make_async_copy(got_ref.at[part, :], landed.at[part, :], got_sem.at[n])
        )
    stride = (idx_ref.shape[2] - LANES) // members
    sets = [(pl.multiple_of(lax.rem(me + s, members) * stride, LANES), chunk) for s in shifts]
    if halo:
        sets = [(members * stride, halo)] + sets
    copies = []
    for n, (start, _) in enumerate(sets):
        batch = []
        for o in range(operators):
            entries = lists[n * operators + o]
            source = idx_ref.at[o, :, pl.ds(start, entries.shape[1])]
            batch.append(pltpu.make_async_copy(source, entries, list_sem.at[n]))
        copies.append(batch)
    columns = pl.ds(pl.multiple_of(me * LANES, LANES), LANES)
    heavy = [
        pltpu.make_async_copy(ops_ref.at[:, columns, :], weights.at[pl.ds(0, ops)], weight_sem)
    ]
    half = ops // 2
    for n, ref in enumerate(weight_refs):
        side = core if n % 2 == 0 else 1 - core
        place = weights.at[pl.ds((n // 2 + 1) * ops + side * half, half)]
        heavy.append(pltpu.make_async_copy(ref, place, weight_sem))
    for copy in arrivals + copies[0] + heavy:
        copy.start()
    for batch in copies[1:]:
        for copy in batch:
            copy.start()
    widen(own_ref, table, 128)
    table[pl.ds(own + got, 8), :] = jnp.zeros((8, LANES), jnp.float32)
    for n, copy in enumerate(arrivals):
        copy.wait()
        widen(
            landed.at[pl.ds(n * piece, piece), :], table.at[pl.ds(own + n * piece, piece), :], 512
        )
    for n, (_, count) in enumerate(sets):
        for copy in copies[n]:
            copy.wait()
        chosen = lists[n * operators : (n + 1) * operators]
        edge_rows = halo and n == 0
        gather_rows(chosen, table, rows, count, 4)
        if n == 0:
            for copy in heavy:
                copy.wait()
        total = operator_sum(rows, weights, count).astype(outs[0].dtype)
        if edge_rows:
            for out in outs:
                out[pl.ds(chunk, halo), :] = total
        else:
            outs[n - (1 if halo else 0)][pl.ds(0, chunk), :] = total


def translate(idx, at, own, got, operators, weights, chunk, shifts, halo, dtype):
    every, columns = idx.shape[0], operators.shape[2]
    vmem = pl.BlockSpec(memory_space=pltpu.VMEM)
    hbm = pl.BlockSpec(memory_space=pltpu.HBM)
    stride = (idx.shape[2] - LANES) // 4
    lengths = ([LANES] if halo else []) + [stride] * len(shifts)
    return pl.pallas_call(
        functools.partial(translate_kernel, shifts, halo),
        out_shape=[jax.ShapeDtypeStruct((chunk + halo, columns), dtype)] * len(shifts),
        in_specs=[hbm, pl.BlockSpec(memory_space=pltpu.SMEM), vmem] + [hbm] * (2 + len(weights)),
        out_specs=[vmem] * len(shifts),
        scratch_shapes=[
            pltpu.VMEM((own.shape[0] + got.shape[0] + 8, LANES), jnp.float32),
            pltpu.VMEM(got.shape, own.dtype),
            pltpu.VMEM((every, chunk, LANES), jnp.float32),
            pltpu.VMEM((every, LANES, columns), operators.dtype),
            pltpu.SemaphoreType.DMA((4,)),
            pltpu.SemaphoreType.DMA((len(lengths),)),
            pltpu.SemaphoreType.DMA,
        ]
        + [pltpu.SMEM((1, length), jnp.int32) for length in lengths for _ in range(every)],
        compiler_params=pltpu.CompilerParams(vmem_limit_bytes=VMEM_LIMIT),
        cost_estimate=pl.CostEstimate(
            flops=2 * every * LANES * columns * chunk * len(shifts),
            bytes_accessed=2 * every * (chunk * len(shifts) + halo) * LANES * 8,
            transcendentals=0,
        ),
        name="translate",
    )(idx, at, own, got, operators, *weights)


def edge_kernel(own_ref, a_ref, b_ref, c_ref, head_ref, tail_ref):
    half = head_ref.shape[0]
    for out, last in ((head_ref, 2 * half), (tail_ref, half)):
        total = jnp.zeros(out.shape, jnp.float32)
        for ref in (own_ref, a_ref, b_ref, c_ref):
            total = total + ref[pl.ds(ref.shape[0] - last, half), :].astype(jnp.float32)
        out[...] = total.astype(out.dtype)


def edges(parts, halo):
    half = jax.ShapeDtypeStruct((halo // 2, parts[0].shape[1]), parts[0].dtype)
    vmem = pl.BlockSpec(memory_space=pltpu.VMEM)
    return pl.pallas_call(
        edge_kernel,
        out_shape=[half, half],
        in_specs=[vmem] * 4,
        out_specs=[vmem] * 2,
        compiler_params=pltpu.CompilerParams(vmem_limit_bytes=VMEM_LIMIT),
        name="edges",
    )(*parts)


def finish_kernel(
    own_ref, a_ref, b_ref, c_ref, place_ref, left_ref, right_ref, l2l_ref, out_ref, acc
):
    rows, columns = out_ref.shape
    octants = l2l_ref.shape[0]
    count = rows // octants

    def total(first, size):
        part = own_ref[pl.ds(first, size), :]
        for ref in (a_ref, b_ref, c_ref):
            part = part + ref[pl.ds(first, size), :].astype(jnp.float32)
        return part

    parent = (total(rows, count) * COARSE_FACTOR).astype(jnp.bfloat16)
    slabs = columns // LANES
    for k in range(octants):
        child = jnp.dot(parent, l2l_ref[k], preferred_element_type=jnp.float32)
        for j in range(slabs):
            acc[j, pl.ds(k, count, stride=octants), :] = child[:, j * LANES : (j + 1) * LANES]
    fine = total(0, rows).astype(jnp.bfloat16).astype(jnp.float32)
    halo = jnp.concatenate([left_ref[...], right_ref[...]], axis=0)
    spread = (
        lax.broadcasted_iota(jnp.int32, (halo.shape[0], rows), 0) == place_ref[...]
    ).astype(jnp.bfloat16)
    foreign = lax.dot_general(
        spread, halo, (((0,), (0,)), ((), ())), preferred_element_type=jnp.float32
    )
    far = fine + foreign
    for j in range(slabs):
        lanes = slice(j * LANES, (j + 1) * LANES)
        out_ref[:, lanes] = (acc[j] + far[:, lanes]).astype(out_ref.dtype)


def finish(own, parts, place, left, right, l2l_ops):
    rows, columns = place.shape[1], own.shape[1]
    vmem = pl.BlockSpec(memory_space=pltpu.VMEM)
    return pl.pallas_call(
        finish_kernel,
        out_shape=jax.ShapeDtypeStruct((rows, columns), jnp.bfloat16),
        in_specs=[vmem] * 8,
        out_specs=vmem,
        scratch_shapes=[pltpu.VMEM((columns // LANES, rows, LANES), jnp.float32)],
        compiler_params=pltpu.CompilerParams(vmem_limit_bytes=VMEM_LIMIT),
        name="finish",
    )(own, *parts, place, left, right, l2l_ops)


def per_device(
    exp_fine, req_fine, src_fine, exp_coarse, req_coarse, src_coarse, operators, l2l_ops, relay_src
):
    members = lax.axis_size("grp")
    me = lax.axis_index("grp")
    blocks = lax.axis_size("box")
    here = lax.axis_index("box")
    rows_f, rows_c = exp_fine.shape[0], exp_coarse.shape[0]
    slots_f, slots_c = req_fine.shape[1], req_coarse.shape[1]
    own_rows, slots = rows_f + rows_c, slots_f + slots_c
    zero_row = own_rows + blocks * slots
    ops, coefficients, _ = operators.shape
    quarter_f, quarter_c = rows_f // members, rows_c // members
    chunk = quarter_f + quarter_c
    at = jnp.stack([me, here % CORES]).astype(jnp.int32)

    def shifted(value, by):
        return lax.ppermute(value, "grp", [(i, (i + by) % members) for i in range(members)])

    def swapped(value):
        return lax.ppermute(value, "box", [(i, i ^ 1) for i in range(blocks)])

    requests = jnp.concatenate(
        [
            jnp.where(req_fine >= 0, req_fine, own_rows),
            jnp.where(req_coarse >= 0, req_coarse + rows_f, own_rows),
        ],
        axis=1,
    )[:, None, :]
    wanted = lax.all_to_all(requests, "box", split_axis=0, concat_axis=0, tiled=True)
    own = jnp.concatenate(
        [
            lax.dynamic_slice_in_dim(exp_fine, me * LANES, LANES, 1),
            lax.dynamic_slice_in_dim(exp_coarse, me * LANES, LANES, 1),
        ],
        axis=0,
    )
    sent = pick(own, wanted)
    got = lax.all_to_all(sent, "box", split_axis=0, concat_axis=0, tiled=True)
    got = got.reshape(blocks * slots, LANES)

    raw = jnp.concatenate([src_fine, src_coarse], axis=1)
    raws = [raw] + [shifted(raw, s) for s in range(1, members)]
    raws, held = lax.optimization_barrier((raws, operators))
    raw = jnp.concatenate(raws, axis=0)

    half = ops // CORES
    weights = []
    for s in range(1, members):
        start = ((here % CORES) * half, ((me + s) % members) * LANES, 0)
        fetched = shifted(lax.dynamic_slice(held, start, (half, LANES, coefficients)), s)
        weights += [fetched, swapped(fetched)]

    src_f, src_c = raw[:, :rows_f], raw[:, rows_f:]
    q = src_f - rows_f
    table_f = jnp.where(src_f < rows_f, src_f, own_rows + (q // slots_f) * slots + q % slots_f)
    table_f = jnp.where(src_f >= 0, table_f, zero_row)
    q = src_c - rows_c
    table_c = own_rows + (q // slots_c) * slots + slots_f + q % slots_c
    table_c = jnp.where(src_c < rows_c, src_c + rows_f, table_c)
    table_c = jnp.where(src_c >= 0, table_c, zero_row)
    local = relay_src - here * rows_f
    inside = (local >= 0) & (local < rows_f)
    relayed = jnp.take(table_f.T, jnp.clip(local, 0, rows_f - 1), axis=0).T
    relayed = jnp.where(inside[None, :], relayed, zero_row)
    every = members * ops
    gap = -chunk % LANES
    chunks = jnp.concatenate(
        [
            relayed.reshape(every, members, quarter_f),
            table_c.reshape(every, members, quarter_c),
            jnp.full((every, members, gap), zero_row, jnp.int32),
        ],
        axis=2,
    )
    idx = jnp.concatenate(
        [
            chunks.reshape(every, -1),
            table_f[:, :R],
            table_f[:, rows_f - R :],
            jnp.full((every, LANES - 2 * R), zero_row, jnp.int32),
        ],
        axis=1,
    )[:, None, :]
    place = jnp.where(local < 0, local + R, jnp.where(local >= rows_f, local - rows_f + R, -1))
    place = lax.dynamic_slice_in_dim(place, me * quarter_f, quarter_f, 0)[None, :]
    got, place, idx = lax.optimization_barrier((got, place, idx))

    def sums(shifts, halo, dtype):
        return translate(idx, at, own, got, operators, weights, chunk, shifts, halo, dtype)

    away = sums((2, 1, 3), 2 * R, jnp.bfloat16)
    others = [shifted(part, s) for part, s in zip(away, (2, 1, 3))]
    (mine,) = sums((0,), 0, jnp.float32)
    others, mine = lax.optimization_barrier((others, mine))
    head, tail = edges([away[0]] + others, 2 * R)
    from_left = lax.ppermute(tail, "box", [(i, i + 1) for i in range(blocks - 1)])
    from_right = lax.ppermute(head, "box", [(i + 1, i) for i in range(blocks - 1)])
    done = finish(mine, others, place, from_left, from_right, l2l_ops)
    out = jnp.zeros((rows_f, coefficients), jnp.bfloat16)
    for s in range(members):
        piece = done if s == 0 else shifted(done, s)
        out = lax.dynamic_update_slice_in_dim(out, piece, ((me - s) % members) * quarter_f, 0)
    return out


def solution(mesh):
    return jax.shard_map(
        per_device,
        mesh=mesh,
        in_specs=(
            P("box", None),
            P("box", None),
            P(("box", "grp"), None),
            P("box", None),
            P("box", None),
            P(("box", "grp"), None),
            P("grp", None, None),
            P(),
            P("box"),
        ),
        out_specs=P("box", None),
        check_vma=False,
    )
```

time: 179 us -> 174 us (0.972)
  waiting for transfers between devices: 70.3 us -> 58.7 us
  starting transfers between devices: 40.5 us -> 48.7 us
  local copies, waits for them, and re-layouts: 18 us -> 14.9 us
  other arithmetic: 3.96 us -> 5.82 us
    all_to_all x1, waiting for transfers between devices: 46.8 us -> 21.7 us  [per_device(): got = lax.all_to_all(sent, 'box', split_axis=0, concat_axis=0, tiled=True)]
    ppermute x2 -> x5, starting transfers between devices: 5.55 us -> 14 us  [the longest x3 6.92 us: swapped(): return lax.ppermute(value, 'box', [(i, i ^ 1) for i in range(blocks)])]
    all_to_all x1, waiting for transfers between devices: 3.63 us -> 9.19 us  [per_device(): lax.all_to_all(requests, 'box', split_axis=0, concat_axis=0, tiled=True)]
    ppermute x12, waiting for transfers between devices: 19.9 us -> 24.5 us  [shifted(): lax.ppermute(value, 'grp', [(i, (i + by) % members) for i in range(member...]
    squeeze x2 -> x0, local copies, waits for them, and re-layouts: 4.02 us -> none  [the longest x1 3.95 us: rows_for(): lax.dynamic_index_in_dim(by_member, member % members, 1, keepdims=False)]
    ppermute x2 -> x5, waiting for transfers between devices: 0.01 us -> 3.31 us  [the longest x1 3.29 us: per_device(): lax.ppermute(head, 'box', [(i + 1, i) for i in range(blocks - 1)])]
    unnamed x23 -> x22, local copies, waits for them, and re-layouts: 6.57 us -> 3.45 us
    all_to_all x1, starting transfers between devices: 7.68 us -> 5.33 us  [per_device(): got = lax.all_to_all(sent, 'box', split_axis=0, concat_axis=0, tiled=True)]
  transfers between devices with their start and end apart: 16 -> 19, of which waited for: 5 -> 10; matrix products, arithmetic and copies ran while one was open for 7% -> 9% of each run, Pallas kernels for 11% -> 5%
where the time goes in v3:
time: 174 us; the launch traced here: 172 us
  waiting for transfers between devices  58.7 us (34%)
  starting transfers between devices  48.7 us (28%)
  Pallas kernels  43.9 us (25%)
  local copies, waits for them, and re-layouts  14.9 us (9%)
  other arithmetic  5.82 us (3%)
    pallas_call x2, Pallas kernels, translate(): pl.pallas_call(functools.partial(translate_kernel, shifts, halo), out_sha...  35 us
    ppermute x12, waiting for transfers between devices, shifted(): lax.ppermute(value, 'grp', [(i, (i + by) % members) for i in range(member...  24.5 us
    all_to_all x1, waiting for transfers between devices, per_device(): got = lax.all_to_all(sent, 'box', split_axis=0, concat_axis=0, tiled=True)  21.7 us
    ppermute x12, starting transfers between devices, shifted(): lax.ppermute(value, 'grp', [(i, (i + by) % members) for i in range(member...  16.2 us
    all_to_all x1, starting transfers between devices, per_device(): lax.all_to_all(requests, 'box', split_axis=0, concat_axis=0, tiled=True)  13.2 us
    all_to_all x1, waiting for transfers between devices, per_device(): lax.all_to_all(requests, 'box', split_axis=0, concat_axis=0, tiled=True)  9.19 us
    pallas_call x1, Pallas kernels, pick(): pl.pallas_call(pick_kernel, out_shape=jax.ShapeDtypeStruct((parts, length...  7.93 us
    ppermute x3, starting transfers between devices, swapped(): return lax.ppermute(value, 'box', [(i, i ^ 1) for i in range(blocks)])  6.92 us
  transfers between devices with their start and end apart: 19, of which 10 were waited for; matrix products, arithmetic and copies ran while one was open for 9% of the time, Pallas kernels for 5%

profile of v3, /device:TPU:1, one launch (start us, length us, event | category | flops | bytes accessed | tf_op | source)
XLA Modules:
  0.0 172.3 jit_solution(15424994718864784094)
XLA Ops:
  0.0 0.9 copy.10
  0.9 0.8 compare_select_fusion.1
  1.7 0.7 broadcast_in_dim.66
  2.4 13.2 %all-to-all-start = ((s32[64,1,160]{2,1,0:T(1,128)}), s32[64,1,160]{2,1,0:T(1,128)S(1)}, u32[]{:S(2)}, u32[]{:S(2)}) async-start(s32[64,1,160]{2,1,0:T(1,128)} %broadcast_in_dim.66), calls=%async_computation | async-start | bytes 131072 | tf_op jit(solution)/shard_map/all_to_all | solution.py:287
  15.6 0.8 constant_dynamic-slice_fusion.3
  16.4 0.0 copy-start.5
  16.4 0.0 copy-start.7
  16.4 0.0 copy-start.6
  16.4 9.2 %all-to-all-done.wanted_ref = s32[64,1,160]{2,1,0:T(1,128)S(1)} async-done(((s32[64,1,160]{2,1,0:T(1,128)}), s32[64,1,160]{2,1,0:T(1,128)S(1)}, u32[]{:S(2)}, u32[]{:S(2)}) %all-to-all-start) | async-done | bytes 40992 | tf_op jit(solution)/shard_map/all_to_all | solution.py:287
  25.6 7.9 %pick.1 = bf16[64,160,128]{2,1,0:T(8,128)(2,1)S(1)} custom-call(s32[64,1,160]{2,1,0:T(1,128)S(1)} %all-to-all-done.wanted_ref, bf16[1152,128]{1,0:T(8,128)(2,1)S(1)} %pad_maximum_fusion.own_ref), custom_call_target="tpu_custom_call" | custom-call | bytes 20971520 | tf_op jit(solution)/shard_map/pick/pallas_call | solution.py:59
  33.5 1.5 copy-done.1
  35.1 5.3 %all-to-all-start.1 = ((bf16[64,160,128]{2,1,0:T(8,128)(2,1)}), bf16[64,160,128]{2,1,0:T(8,128)(2,1)}, u32[]{:S(2)}, u32[]{:S(2)}) async-start(bf16[64,160,128]{2,1,0:T(8,128)(2,1)} %copy-done.1), calls=%async_computation.1 | async-start | bytes 5242880 | tf_op jit(solution)/shard_map/all_to_all | solution.py:296
  40.5 1.3 collective-permute-start
  41.7 2.5 %collective-permute-start.1 = (s32[8,1152]{1,0:T(8,128)S(1)}, s32[8,1152]{1,0:T(8,128)S(1)}, u32[]{:S(2)}, u32[]{:S(2)}) collective-permute-start(s32[8,1152]{1,0:T(8,128)S(1)} %constant_dynamic-update-slice_fusion), channel_id=1, source_target_pairs={{0,2},{1,3},{2,0},{3,1},{4,6},{5,7},{6,4},{7,5},{8,10},{9,11},{10,... | collective-permute-start | bytes 110600 | tf_op jit(solution)/shard_map/ppermute | solution.py:275
  44.2 1.2 collective-permute-start.2
  45.4 0.1 pad_add_fusion.1.at_ref
  45.5 0.1 pad.4.clone
  45.5 0.1 dynamic_slice.20
  45.6 0.4 collective-permute-done.1
  46.1 1.3 collective-permute-done.2
  47.4 2.6 %constant_dynamic-slice_fusion = (bf16[4,128,512]{2,1,0:T(8,128)(2,1)}, bf16[4,128,512]{2,1,0:T(8,128)(2,1)}, bf16[4,128,512]{2,1,0:T(8,128)(2,1)}) fusion(bf16[8,512,512]{2,1,0:T(8,128)(2,1)} %ops_ref.3, s32[]{:T(128)S(6)} %select_n.162, s32[]{:T(128)S(6)} %select_n.168, s32[]{:T(128)S(6)} %select_n.166, s32[]{:T(128)S(6)} %select_n.164), kind=kLoop, calls=%fused_computation.52 | loop fusion | bytes 3145744 | tf_op jit(solution)/shard_map/dynamic_slice | solution.py:308
  50.0 0.3 collective-permute-start.3
  50.2 3.3 %collective-permute-start.5 = (bf16[4,128,512]{2,1,0:T(8,128)(2,1)}, bf16[4,128,512]{2,1,0:T(8,128)(2,1)S(1)}, u32[]{:S(2)}, u32[]{:S(2)}) collective-permute-start(bf16[4,128,512]{2,1,0:T(8,128)(2,1)} %get-tuple-element.40), channel_id=1, source_target_pairs={{0,2},{1,3},{2,0},{3,1},{4,6},{5,7},{6,4},{7,5},{8,10},{9,11},{10,... | collective-permute-start | bytes 1572872 | tf_op jit(solution)/shard_map/ppermute | solution.py:275
  53.5 0.0 collective-permute-start.7
  53.6 0.7 copy-done.4
  54.3 0.8 fusion.19
  55.1 1.1 copy.12
  56.2 4.0 %gather_fusion = s32[1024,32]{1,0:T(8,128)} fusion(s32[1024,32]{1,0:T(8,128)S(1)} %copy.12, s32[1024]{0:T(1024)S(1)} %get-tuple-element.46), kind=kCustom, calls=%fused_computation | custom fusion | bytes 266240 | tf_op jit(solution)/shard_map/jit(_take)/gather | solution.py:321
  60.2 1.4 select_select_fusion
  61.6 0.8 copy.13
  62.4 0.7 fusion.12
  63.2 0.1 reshape.20
  63.3 0.0 collective-permute-done.3.refs_0_
  63.3 4.0 %collective-permute-start.4 = (bf16[4,128,512]{2,1,0:T(8,128)(2,1)S(1)}, bf16[4,128,512]{2,1,0:T(8,128)(2,1)}, u32[]{:S(2)}, u32[]{:S(2)}) collective-permute-start(bf16[4,128,512]{2,1,0:T(8,128)(2,1)S(1)} %collective-permute-done.3.refs_0_), channel_id=1, source_target_pairs={{0,4},{4,0},{8,12},{12,8},{16,20},{20,16},{24,28},{28,24},{32,36},... | collective-permute-start | bytes 1572872 | tf_op jit(solution)/shard_map/ppermute | solution.py:278
  67.3 7.7 %collective-permute-done.5.refs_2_ = bf16[4,128,512]{2,1,0:T(8,128)(2,1)S(1)} collective-permute-done((bf16[4,128,512]{2,1,0:T(8,128)(2,1)}, bf16[4,128,512]{2,1,0:T(8,128)(2,1)S(1)}, u32[]{:S(2)}, u32[]{:S(2)}) %collective-permute-start.5) | collective-permute-done | bytes 524320 | tf_op jit(solution)/shard_map/ppermute | solution.py:275
  75.0 2.9 %collective-permute-start.6 = (bf16[4,128,512]{2,1,0:T(8,128)(2,1)S(1)}, bf16[4,128,512]{2,1,0:T(8,128)(2,1)}, u32[]{:S(2)}, u32[]{:S(2)}) collective-permute-start(bf16[4,128,512]{2,1,0:T(8,128)(2,1)S(1)} %collective-permute-done.5.refs_2_), channel_id=1, source_target_pairs={{0,4},{4,0},{8,12},{12,8},{16,20},{20,16},{24,28},{28,24},{32,36},... | collective-permute-start | bytes 1572872 | tf_op jit(solution)/shard_map/ppermute | solution.py:278
  77.8 0.0 collective-permute-done.7.refs_4_
  77.8 0.0 collective-permute-start.8
  77.8 0.9 add_add_fusion
  78.8 1.1 fusion.3
  79.9 0.1 fusion.18
  79.9 0.1 concatenate.23
  80.0 0.1 broadcast_in_dim.78.idx_ref
  80.2 21.7 %all-to-all-done.1 = bf16[64,160,128]{2,1,0:T(8,128)(2,1)} async-done(((bf16[64,160,128]{2,1,0:T(8,128)(2,1)}), bf16[64,160,128]{2,1,0:T(8,128)(2,1)}, u32[]{:S(2)}, u32[]{:S(2)}) %all-to-all-start.1) | async-done | bytes 2621472 | tf_op jit(solution)/shard_map/all_to_all | solution.py:296
  101.9 25.6 %translate.2 = (bf16[352,512]{1,0:T(8,128)(2,1)S(1)}, bf16[352,512]{1,0:T(8,128)(2,1)S(1)}, bf16[352,512]{1,0:T(8,128)(2,1)S(1)}) custom-call(s32[32,1,1664]{2,1,0:T(1,128)S(1)} %broadcast_in_dim.78.idx_ref, s32[2]{0:T(128)S(1)} %pad_add_fusion.1.at_ref, bf16[1152,128]{1,0:T(8,128)(2,1)S(1)} %pad_maximum_fusion.own_ref, bf16[10240,128]{1,0:T(8,128)(2,1)} %bitcast.got_ref, ...), custom_call_target="tpu_custom_call" | custom-call | flops 3623878656 | bytes 60817408 | tf_op jit(solution)/shard_map/translate/pallas_call | solution.py:164
  127.5 1.3 collective-permute-start.10
  128.8 1.5 collective-permute-start.11
  130.2 1.5 collective-permute-start.9
  131.8 9.4 %translate.3.own_ref = f32[288,512]{1,0:T(8,128)S(1)} custom-call(s32[32,1,1664]{2,1,0:T(1,128)S(1)} %broadcast_in_dim.78.idx_ref, s32[2]{0:T(128)S(1)} %pad_add_fusion.1.at_ref, bf16[1152,128]{1,0:T(8,128)(2,1)S(1)} %pad_maximum_fusion.own_ref, bf16[10240,128]{1,0:T(8,128)(2,1)} %bitcast.got_ref, bf16[8,512,512]{2,1,0:T(8,128)(2,1)} %ops_ref.3, ...), custom_call_target="tpu_custom_call" | custom-call | flops 1207959552 | bytes 18874368 | tf_op jit(solution)/shard_map/translate/pallas_call | solution.py:164
  141.2 4.5 %collective-permute-done.9.a_ref = bf16[352,512]{1,0:T(8,128)(2,1)S(1)} collective-permute-done((bf16[352,512]{1,0:T(8,128)(2,1)S(1)}, bf16[352,512]{1,0:T(8,128)(2,1)S(1)}, u32[]{:S(2)}, u32[]{:S(2)}) %collective-permute-start.9) | collective-permute-done | bytes 360480 | tf_op jit(solution)/shard_map/ppermute | solution.py:275
  145.7 5.2 %collective-permute-start.12 = (bf16[32,512]{1,0:T(8,128)(2,1)S(1)}, bf16[32,512]{1,0:T(8,128)(2,1)S(1)}, u32[]{:S(2)}, u32[]{:S(2)}) collective-permute-start(bf16[32,512]{1,0:T(8,128)(2,1)S(1)} %get-tuple-element.37), channel_id=1, source_target_pairs={{0,4},{4,8},{8,12},{12,16},{16,20},{20,24},{24,28},{28,32},{32,36}... | collective-permute-start | bytes 98312 | tf_op jit(solution)/shard_map/ppermute | solution.py:354
  150.9 1.9 %collective-permute-start.13 = (bf16[32,512]{1,0:T(8,128)(2,1)S(1)}, bf16[32,512]{1,0:T(8,128)(2,1)S(1)}, u32[]{:S(2)}, u32[]{:S(2)}) collective-permute-start(bf16[32,512]{1,0:T(8,128)(2,1)S(1)} %get-tuple-element.38), channel_id=1, source_target_pairs={{4,0},{8,4},{12,8},{16,12},{20,16},{24,20},{28,24},{32,28},{36,32}... | collective-permute-start | bytes 98312 | tf_op jit(solution)/shard_map/ppermute | solution.py:355
  152.8 3.3 %collective-permute-done.13.right_ref = bf16[32,512]{1,0:T(8,128)(2,1)S(1)} collective-permute-done((bf16[32,512]{1,0:T(8,128)(2,1)S(1)}, bf16[32,512]{1,0:T(8,128)(2,1)S(1)}, u32[]{:S(2)}, u32[]{:S(2)}) %collective-permute-start.13) | collective-permute-done | bytes 32800 | tf_op jit(solution)/shard_map/ppermute | solution.py:355
  156.1 1.0 finish.1
  157.1 0.9 collective-permute-start.14
  158.0 2.0 %collective-permute-start.15 = (bf16[256,512]{1,0:T(8,128)(2,1)S(1)}, bf16[256,512]{1,0:T(8,128)(2,1)S(1)}, u32[]{:S(2)}, u32[]{:S(2)}) collective-permute-start(bf16[256,512]{1,0:T(8,128)(2,1)S(1)} %finish.1), channel_id=1, source_target_pairs={{0,2},{1,3},{2,0},{3,1},{4,6},{5,7},{6,4},{7,5},{8,10},{9,11},{10,... | collective-permute-start | bytes 786440 | tf_op jit(solution)/shard_map/ppermute | solution.py:275
  160.1 0.5 collective-permute-start.16
  160.5 0.1 broadcast_in_dim.63
  160.6 5.9 %collective-permute-done.14 = bf16[256,512]{1,0:T(8,128)(2,1)S(1)} collective-permute-done((bf16[256,512]{1,0:T(8,128)(2,1)S(1)}, bf16[256,512]{1,0:T(8,128)(2,1)S(1)}, u32[]{:S(2)}, u32[]{:S(2)}) %collective-permute-start.14) | collective-permute-done | bytes 262176 | tf_op jit(solution)/shard_map/ppermute | solution.py:275
  166.6 4.0 %collective-permute-done.15 = bf16[256,512]{1,0:T(8,128)(2,1)S(1)} collective-permute-done((bf16[256,512]{1,0:T(8,128)(2,1)S(1)}, bf16[256,512]{1,0:T(8,128)(2,1)S(1)}, u32[]{:S(2)}, u32[]{:S(2)}) %collective-permute-start.15) | collective-permute-done | bytes 262176 | tf_op jit(solution)/shard_map/ppermute | solution.py:275
  170.6 0.0 copy-start.3
  170.6 0.6 collective-permute-done.16
  171.3 0.3 copy-done.3
  171.6 0.7 constant_dynamic-update-slice_fusion.6
  (35 shorter events, 0.3 us)
Async XLA Ops:
  0.0 15.5 %copy-start = (bf16[1024,512]{1,0:T(8,128)(2,1)S(1)}, bf16[1024,512]{1,0:T(8,128)(2,1)}, u32[]{:S(2)}) copy-start(bf16[1024,512]{1,0:T(8,128)(2,1)} %param.9) | copy-start | bytes 3145732
  2.4 23.3 %all-to-all-start = ((s32[64,1,160]{2,1,0:T(1,128)}), s32[64,1,160]{2,1,0:T(1,128)S(1)}, u32[]{:S(2)}, u32[]{:S(2)}) async-start(s32[64,1,160]{2,1,0:T(1,128)} %broadcast_in_dim.66), calls=%async_computation | async-start | bytes 131072 | tf_op jit(solution)/shard_map/all_to_all | solution.py:287
  16.4 24.0 %copy-start.5 = (s32[8,1024]{1,0:T(8,128)S(1)}, s32[8,1024]{1,0:T(8,128)}, u32[]{:S(2)}) copy-start(s32[8,1024]{1,0:T(8,128)} %param.11) | copy-start | bytes 98308
  16.4 24.1 %copy-start.7 = (s32[8,128]{1,0:T(8,128)S(1)}, s32[8,128]{1,0:T(8,128)}, u32[]{:S(2)}) copy-start(s32[8,128]{1,0:T(8,128)} %param.14) | copy-start | bytes 12292
  16.4 29.0 %copy-start.6 = (s32[1024]{0:T(1024)S(1)}, s32[1024]{0:T(1024)}, u32[]{:S(2)}) copy-start(s32[1024]{0:T(1024)} %param.17) | copy-start | bytes 12292
  33.5 1.5 copy-start.1
  35.1 66.8 %all-to-all-start.1 = ((bf16[64,160,128]{2,1,0:T(8,128)(2,1)}), bf16[64,160,128]{2,1,0:T(8,128)(2,1)}, u32[]{:S(2)}, u32[]{:S(2)}) async-start(bf16[64,160,128]{2,1,0:T(8,128)(2,1)} %copy-done.1), calls=%async_computation.1 | async-start | bytes 5242880 | tf_op jit(solution)/shard_map/all_to_all | solution.py:296
  40.5 5.2 %collective-permute-start = (s32[8,1152]{1,0:T(8,128)S(1)}, s32[8,1152]{1,0:T(8,128)S(1)}, u32[]{:S(2)}, u32[]{:S(2)}) collective-permute-start(s32[8,1152]{1,0:T(8,128)S(1)} %constant_dynamic-update-slice_fusion), channel_id=1, source_target_pairs={{0,1},{1,2},{2,3},{3,0},{4,5},{5,6},{6,7},{7,4},{8,9},{9,10},{10,1... | collective-permute-start | bytes 110600 | tf_op jit(solution)/shard_map/ppermute | solution.py:275
  41.7 4.3 %collective-permute-start.1 = (s32[8,1152]{1,0:T(8,128)S(1)}, s32[8,1152]{1,0:T(8,128)S(1)}, u32[]{:S(2)}, u32[]{:S(2)}) collective-permute-start(s32[8,1152]{1,0:T(8,128)S(1)} %constant_dynamic-update-slice_fusion), channel_id=1, source_target_pairs={{0,2},{1,3},{2,0},{3,1},{4,6},{5,7},{6,4},{7,5},{8,10},{9,11},{10,... | collective-permute-start | bytes 110600 | tf_op jit(solution)/shard_map/ppermute | solution.py:275
  44.2 3.2 %collective-permute-start.2 = (s32[8,1152]{1,0:T(8,128)S(1)}, s32[8,1152]{1,0:T(8,128)S(1)}, u32[]{:S(2)}, u32[]{:S(2)}) collective-permute-start(s32[8,1152]{1,0:T(8,128)S(1)} %constant_dynamic-update-slice_fusion), channel_id=1, source_target_pairs={{0,3},{1,0},{2,1},{3,2},{4,7},{5,4},{6,5},{7,6},{8,11},{9,8},{10,9... | collective-permute-start | bytes 110600 | tf_op jit(solution)/shard_map/ppermute | solution.py:275
  50.0 13.3 %collective-permute-start.3 = (bf16[4,128,512]{2,1,0:T(8,128)(2,1)}, bf16[4,128,512]{2,1,0:T(8,128)(2,1)S(1)}, u32[]{:S(2)}, u32[]{:S(2)}) collective-permute-start(bf16[4,128,512]{2,1,0:T(8,128)(2,1)} %get-tuple-element.41), channel_id=1, source_target_pairs={{0,1},{1,2},{2,3},{3,0},{4,5},{5,6},{6,7},{7,4},{8,9},{9,10},{10,1... | collective-permute-start | bytes 1572872 | tf_op jit(solution)/shard_map/ppermute | solution.py:275
  50.2 24.7 %collective-permute-start.5 = (bf16[4,128,512]{2,1,0:T(8,128)(2,1)}, bf16[4,128,512]{2,1,0:T(8,128)(2,1)S(1)}, u32[]{:S(2)}, u32[]{:S(2)}) collective-permute-start(bf16[4,128,512]{2,1,0:T(8,128)(2,1)} %get-tuple-element.40), channel_id=1, source_target_pairs={{0,2},{1,3},{2,0},{3,1},{4,6},{5,7},{6,4},{7,5},{8,10},{9,11},{10,... | collective-permute-start | bytes 1572872 | tf_op jit(solution)/shard_map/ppermute | solution.py:275
  53.5 24.3 %collective-permute-start.7 = (bf16[4,128,512]{2,1,0:T(8,128)(2,1)}, bf16[4,128,512]{2,1,0:T(8,128)(2,1)S(1)}, u32[]{:S(2)}, u32[]{:S(2)}) collective-permute-start(bf16[4,128,512]{2,1,0:T(8,128)(2,1)} %get-tuple-element.39), channel_id=1, source_target_pairs={{0,3},{1,0},{2,1},{3,2},{4,7},{5,4},{6,5},{7,6},{8,11},{9,8},{10,9... | collective-permute-start | bytes 1572872 | tf_op jit(solution)/shard_map/ppermute | solution.py:275
  53.6 0.7 copy-start.4
  63.3 38.6 %collective-permute-start.4 = (bf16[4,128,512]{2,1,0:T(8,128)(2,1)S(1)}, bf16[4,128,512]{2,1,0:T(8,128)(2,1)}, u32[]{:S(2)}, u32[]{:S(2)}) collective-permute-start(bf16[4,128,512]{2,1,0:T(8,128)(2,1)S(1)} %collective-permute-done.3.refs_0_), channel_id=1, source_target_pairs={{0,4},{4,0},{8,12},{12,8},{16,20},{20,16},{24,28},{28,24},{32,36},... | collective-permute-start | bytes 1572872 | tf_op jit(solution)/shard_map/ppermute | solution.py:278
  75.0 26.9 %collective-permute-start.6 = (bf16[4,128,512]{2,1,0:T(8,128)(2,1)S(1)}, bf16[4,128,512]{2,1,0:T(8,128)(2,1)}, u32[]{:S(2)}, u32[]{:S(2)}) collective-permute-start(bf16[4,128,512]{2,1,0:T(8,128)(2,1)S(1)} %collective-permute-done.5.refs_2_), channel_id=1, source_target_pairs={{0,4},{4,0},{8,12},{12,8},{16,20},{20,16},{24,28},{28,24},{32,36},... | collective-permute-start | bytes 1572872 | tf_op jit(solution)/shard_map/ppermute | solution.py:278
  77.8 24.0 %collective-permute-start.8 = (bf16[4,128,512]{2,1,0:T(8,128)(2,1)S(1)}, bf16[4,128,512]{2,1,0:T(8,128)(2,1)}, u32[]{:S(2)}, u32[]{:S(2)}) collective-permute-start(bf16[4,128,512]{2,1,0:T(8,128)(2,1)S(1)} %collective-permute-done.7.refs_4_), channel_id=1, source_target_pairs={{0,4},{4,0},{8,12},{12,8},{16,20},{20,16},{24,28},{28,24},{32,36},... | collective-permute-start | bytes 1572872 | tf_op jit(solution)/shard_map/ppermute | solution.py:278
  127.5 13.7 %collective-permute-start.10 = (bf16[352,512]{1,0:T(8,128)(2,1)S(1)}, bf16[352,512]{1,0:T(8,128)(2,1)S(1)}, u32[]{:S(2)}, u32[]{:S(2)}) collective-permute-start(bf16[352,512]{1,0:T(8,128)(2,1)S(1)} %get-tuple-element.30), channel_id=1, source_target_pairs={{0,1},{1,2},{2,3},{3,0},{4,5},{5,6},{6,7},{7,4},{8,9},{9,10},{10,1... | collective-permute-start | bytes 1081352 | tf_op jit(solution)/shard_map/ppermute | solution.py:275
  128.8 12.4 %collective-permute-start.11 = (bf16[352,512]{1,0:T(8,128)(2,1)S(1)}, bf16[352,512]{1,0:T(8,128)(2,1)S(1)}, u32[]{:S(2)}, u32[]{:S(2)}) collective-permute-start(bf16[352,512]{1,0:T(8,128)(2,1)S(1)} %get-tuple-element.31), channel_id=1, source_target_pairs={{0,3},{1,0},{2,1},{3,2},{4,7},{5,4},{6,5},{7,6},{8,11},{9,8},{10,9... | collective-permute-start | bytes 1081352 | tf_op jit(solution)/shard_map/ppermute | solution.py:275
  130.2 25.9 %copy-start.2 = (bf16[8,512,512]{2,1,0:T(8,128)(2,1)S(1)}, bf16[8,512,512]{2,1,0:T(8,128)(2,1)}, u32[]{:S(2)}) copy-start(bf16[8,512,512]{2,1,0:T(8,128)(2,1)} %l2l_ref.1) | copy-start | bytes 12582916
  130.2 15.5 %collective-permute-start.9 = (bf16[352,512]{1,0:T(8,128)(2,1)S(1)}, bf16[352,512]{1,0:T(8,128)(2,1)S(1)}, u32[]{:S(2)}, u32[]{:S(2)}) collective-permute-start(bf16[352,512]{1,0:T(8,128)(2,1)S(1)} %get-tuple-element.29.own_ref), channel_id=1, source_target_pairs={{0,2},{1,3},{2,0},{3,1},{4,6},{5,7},{6,4},{7,5},{8,10},{9,11},{10,... | collective-permute-start | bytes 1081352 | tf_op jit(solution)/shard_map/ppermute | solution.py:275
  145.7 7.1 %collective-permute-start.12 = (bf16[32,512]{1,0:T(8,128)(2,1)S(1)}, bf16[32,512]{1,0:T(8,128)(2,1)S(1)}, u32[]{:S(2)}, u32[]{:S(2)}) collective-permute-start(bf16[32,512]{1,0:T(8,128)(2,1)S(1)} %get-tuple-element.37), channel_id=1, source_target_pairs={{0,4},{4,8},{8,12},{12,16},{16,20},{20,24},{24,28},{28,32},{32,36}... | collective-permute-start | bytes 98312 | tf_op jit(solution)/shard_map/ppermute | solution.py:354
  150.9 5.2 %collective-permute-start.13 = (bf16[32,512]{1,0:T(8,128)(2,1)S(1)}, bf16[32,512]{1,0:T(8,128)(2,1)S(1)}, u32[]{:S(2)}, u32[]{:S(2)}) collective-permute-start(bf16[32,512]{1,0:T(8,128)(2,1)S(1)} %get-tuple-element.38), channel_id=1, source_target_pairs={{4,0},{8,4},{12,8},{16,12},{20,16},{24,20},{28,24},{32,28},{36,32}... | collective-permute-start | bytes 98312 | tf_op jit(solution)/shard_map/ppermute | solution.py:355
  157.1 9.4 %collective-permute-start.14 = (bf16[256,512]{1,0:T(8,128)(2,1)S(1)}, bf16[256,512]{1,0:T(8,128)(2,1)S(1)}, u32[]{:S(2)}, u32[]{:S(2)}) collective-permute-start(bf16[256,512]{1,0:T(8,128)(2,1)S(1)} %finish.1), channel_id=1, source_target_pairs={{0,1},{1,2},{2,3},{3,0},{4,5},{5,6},{6,7},{7,4},{8,9},{9,10},{10,1... | collective-permute-start | bytes 786440 | tf_op jit(solution)/shard_map/ppermute | solution.py:275
  158.0 12.5 %collective-permute-start.15 = (bf16[256,512]{1,0:T(8,128)(2,1)S(1)}, bf16[256,512]{1,0:T(8,128)(2,1)S(1)}, u32[]{:S(2)}, u32[]{:S(2)}) collective-permute-start(bf16[256,512]{1,0:T(8,128)(2,1)S(1)} %finish.1), channel_id=1, source_target_pairs={{0,2},{1,3},{2,0},{3,1},{4,6},{5,7},{6,4},{7,5},{8,10},{9,11},{10,... | collective-permute-start | bytes 786440 | tf_op jit(solution)/shard_map/ppermute | solution.py:275
  160.1 11.2 %collective-permute-start.16 = (bf16[256,512]{1,0:T(8,128)(2,1)S(1)}, bf16[256,512]{1,0:T(8,128)(2,1)S(1)}, u32[]{:S(2)}, u32[]{:S(2)}) collective-permute-start(bf16[256,512]{1,0:T(8,128)(2,1)S(1)} %finish.1), channel_id=1, source_target_pairs={{0,3},{1,0},{2,1},{3,2},{4,7},{5,4},{6,5},{7,6},{8,11},{9,8},{10,9... | collective-permute-start | bytes 786440 | tf_op jit(solution)/shard_map/ppermute | solution.py:275
  170.6 1.0 copy-start.3

commit v4 on v3

--- a/solution.py
+++ b/solution.py
@@ -143,19 +143,20 @@
             copy.wait()
         chosen = lists[n * operators : (n + 1) * operators]
         edge_rows = halo and n == 0
-        gather_rows(chosen, table, rows, count, 4)
+        gather_rows(chosen, table, rows, count, 8)
         if n == 0:
             for copy in heavy:
                 copy.wait()
-        total = operator_sum(rows, weights, count).astype(outs[0].dtype)
+        total = operator_sum(rows, weights, count)
         if edge_rows:
             for out in outs:
-                out[pl.ds(chunk, halo), :] = total
+                out[pl.ds(chunk, halo), :] = total.astype(out.dtype)
         else:
-            outs[n - (1 if halo else 0)][pl.ds(0, chunk), :] = total
-
-
-def translate(idx, at, own, got, operators, weights, chunk, shifts, halo, dtype):
+            out = outs[n - (1 if halo else 0)]
+            out[pl.ds(0, chunk), :] = total.astype(out.dtype)
+
+
+def translate(idx, at, own, got, operators, weights, chunk, shifts, halo, dtypes):
     every, columns = idx.shape[0], operators.shape[2]
     vmem = pl.BlockSpec(memory_space=pltpu.VMEM)
     hbm = pl.BlockSpec(memory_space=pltpu.HBM)
@@ -163,7 +164,7 @@
     lengths = ([LANES] if halo else []) + [stride] * len(shifts)
     return pl.pallas_call(
         functools.partial(translate_kernel, shifts, halo),
-        out_shape=[jax.ShapeDtypeStruct((chunk + halo, columns), dtype)] * len(shifts),
+        out_shape=[jax.ShapeDtypeStruct((chunk + halo, columns), dtype) for dtype in dtypes],
         in_specs=[hbm, pl.BlockSpec(memory_space=pltpu.SMEM), vmem] + [hbm] * (2 + len(weights)),
         out_specs=[vmem] * len(shifts),
         scratch_shapes=[
@@ -277,13 +278,9 @@
     def swapped(value):
         return lax.ppermute(value, "box", [(i, i ^ 1) for i in range(blocks)])
 
-    requests = jnp.concatenate(
-        [
-            jnp.where(req_fine >= 0, req_fine, own_rows),
-            jnp.where(req_coarse >= 0, req_coarse + rows_f, own_rows),
-        ],
-        axis=1,
-    )[:, None, :]
+    asked = jnp.concatenate([req_fine, req_coarse], axis=1)[:, None, :]
+    starts = jnp.where(jnp.arange(slots) < slots_f, 0, rows_f)
+    requests = jnp.where(asked >= 0, asked + starts, own_rows)
     wanted = lax.all_to_all(requests, "box", split_axis=0, concat_axis=0, tiled=True)
     own = jnp.concatenate(
         [
@@ -343,19 +340,21 @@
     place = lax.dynamic_slice_in_dim(place, me * quarter_f, quarter_f, 0)[None, :]
     got, place, idx = lax.optimization_barrier((got, place, idx))
 
-    def sums(shifts, halo, dtype):
-        return translate(idx, at, own, got, operators, weights, chunk, shifts, halo, dtype)
-
-    away = sums((2, 1, 3), 2 * R, jnp.bfloat16)
-    others = [shifted(part, s) for part, s in zip(away, (2, 1, 3))]
-    (mine,) = sums((0,), 0, jnp.float32)
-    others, mine = lax.optimization_barrier((others, mine))
-    head, tail = edges([away[0]] + others, 2 * R)
+    def sums(shifts, halo, dtypes):
+        return translate(idx, at, own, got, operators, weights, chunk, shifts, halo, dtypes)
+
+    away = sums((2, 1), 2 * R, (jnp.bfloat16, jnp.bfloat16))
+    halo_3 = shifted(away[0][chunk:], 3)
+    others = [shifted(part, s) for part, s in zip(away, (2, 1))]
+    last, mine = sums((3, 0), 0, (jnp.bfloat16, jnp.float32))
+    others, halo_3, last, mine = lax.optimization_barrier((others, halo_3, last, mine))
+    head, tail = edges([away[0]] + others + [halo_3], 2 * R)
     from_left = lax.ppermute(tail, "box", [(i, i + 1) for i in range(blocks - 1)])
     from_right = lax.ppermute(head, "box", [(i + 1, i) for i in range(blocks - 1)])
+    others = others + [shifted(last, 3)]
     done = finish(mine, others, place, from_left, from_right, l2l_ops)
     out = jnp.zeros((rows_f, coefficients), jnp.bfloat16)
-    for s in range(members):
+    for s in (0, 2, 1, 3):
         piece = done if s == 0 else shifted(done, s)
         out = lax.dynamic_update_slice_in_dim(out, piece, ((me - s) % members) * quarter_f, 0)
     return out

time: 174 us -> 171 us (0.983)
  waiting for transfers between devices: 58.7 us -> 49 us
  local copies, waits for them, and re-layouts: 14.9 us -> 19.7 us
  starting transfers between devices: 48.7 us -> 51.5 us
    ppermute x12 -> x13, waiting for transfers between devices: 24.5 us -> 18.7 us  [shifted(): lax.ppermute(value, 'grp', [(i, (i + by) % members) for i in range(member...]
    all_to_all x1, waiting for transfers between devices: 21.7 us -> 17.8 us  [per_device(): got = lax.all_to_all(sent, 'box', split_axis=0, concat_axis=0, tiled=True)]
    ppermute x12 -> x13, starting transfers between devices: 16.2 us -> 18.7 us  [shifted(): lax.ppermute(value, 'grp', [(i, (i + by) % members) for i in range(member...]
    unnamed x22 -> x26, local copies, waits for them, and re-layouts: 3.45 us -> 5.67 us
  transfers between devices with their start and end apart: 19 -> 20, of which waited for: 10 -> 8; matrix products, arithmetic and copies ran while one was open for 9% -> 11% of each run, Pallas kernels for 5% -> 9%
where the time goes in v4:
time: 171 us; the launch traced here: 170 us
  starting transfers between devices  51.5 us (30%)
  waiting for transfers between devices  49 us (29%)
  Pallas kernels  43.3 us (25%)
  local copies, waits for them, and re-layouts  19.7 us (12%)
  other arithmetic  6.5 us (4%)
    pallas_call x2, Pallas kernels, translate(): pl.pallas_call(functools.partial(translate_kernel, shifts, halo), out_sha...  34.3 us
    ppermute x13, waiting for transfers between devices, shifted(): lax.ppermute(value, 'grp', [(i, (i + by) % members) for i in range(member...  18.7 us
    ppermute x13, starting transfers between devices, shifted(): lax.ppermute(value, 'grp', [(i, (i + by) % members) for i in range(member...  18.7 us
    all_to_all x1, waiting for transfers between devices, per_device(): got = lax.all_to_all(sent, 'box', split_axis=0, concat_axis=0, tiled=True)  17.8 us
    all_to_all x1, starting transfers between devices, per_device(): lax.all_to_all(requests, 'box', split_axis=0, concat_axis=0, tiled=True)  13.2 us
    all_to_all x1, waiting for transfers between devices, per_device(): lax.all_to_all(requests, 'box', split_axis=0, concat_axis=0, tiled=True)  9.19 us
    pallas_call x1, Pallas kernels, pick(): pl.pallas_call(pick_kernel, out_shape=jax.ShapeDtypeStruct((parts, length...  7.93 us
    ppermute x3, starting transfers between devices, swapped(): return lax.ppermute(value, 'box', [(i, i ^ 1) for i in range(blocks)])  6.94 us
  transfers between devices with their start and end apart: 20, of which 8 were waited for; matrix products, arithmetic and copies ran while one was open for 11% of the time, Pallas kernels for 9%

profile of v4, /device:TPU:1, one launch (start us, length us, event | category | flops | bytes accessed | tf_op | source)
XLA Modules:
  0.0 170.3 jit_solution(1855075241056403862)
XLA Ops:
  0.0 0.9 copy.10
  0.9 1.5 compare_select_fusion.1
  2.4 13.2 %all-to-all-start = ((s32[64,1,160]{2,1,0:T(1,128)}), s32[64,1,160]{2,1,0:T(1,128)S(1)}, u32[]{:S(2)}, u32[]{:S(2)}) async-start(s32[64,1,160]{2,1,0:T(1,128)} %compare_select_fusion.1), calls=%async_computation | async-start | bytes 131072 | tf_op jit(solution)/shard_map/all_to_all | solution.py:284
  15.6 0.8 constant_dynamic-slice_fusion.3
  16.4 0.0 copy-start.7
  16.4 0.0 copy-start.9
  16.4 0.0 copy-start.8
  16.4 9.2 %all-to-all-done.wanted_ref = s32[64,1,160]{2,1,0:T(1,128)S(1)} async-done(((s32[64,1,160]{2,1,0:T(1,128)}), s32[64,1,160]{2,1,0:T(1,128)S(1)}, u32[]{:S(2)}, u32[]{:S(2)}) %all-to-all-start) | async-done | bytes 40992 | tf_op jit(solution)/shard_map/all_to_all | solution.py:284
  25.6 7.9 %pick.1 = bf16[64,160,128]{2,1,0:T(8,128)(2,1)S(1)} custom-call(s32[64,1,160]{2,1,0:T(1,128)S(1)} %all-to-all-done.wanted_ref, bf16[1152,128]{1,0:T(8,128)(2,1)S(1)} %pad_maximum_fusion.own_ref), custom_call_target="tpu_custom_call" | custom-call | bytes 20971520 | tf_op jit(solution)/shard_map/pick/pallas_call | solution.py:59
  33.6 1.5 copy-done.1
  35.1 5.3 %all-to-all-start.1 = ((bf16[64,160,128]{2,1,0:T(8,128)(2,1)}), bf16[64,160,128]{2,1,0:T(8,128)(2,1)}, u32[]{:S(2)}, u32[]{:S(2)}) async-start(bf16[64,160,128]{2,1,0:T(8,128)(2,1)} %copy-done.1), calls=%async_computation.1 | async-start | bytes 5242880 | tf_op jit(solution)/shard_map/all_to_all | solution.py:293
  40.5 1.3 collective-permute-start
  41.8 2.5 %collective-permute-start.1 = (s32[8,1152]{1,0:T(8,128)S(1)}, s32[8,1152]{1,0:T(8,128)S(1)}, u32[]{:S(2)}, u32[]{:S(2)}) collective-permute-start(s32[8,1152]{1,0:T(8,128)S(1)} %constant_dynamic-update-slice_fusion), channel_id=1, source_target_pairs={{0,2},{1,3},{2,0},{3,1},{4,6},{5,7},{6,4},{7,5},{8,10},{9,11},{10,... | collective-permute-start | bytes 110600 | tf_op jit(solution)/shard_map/ppermute | solution.py:276
  44.2 1.2 collective-permute-start.2
  45.4 0.1 pad_add_fusion.1.at_ref
  45.5 0.1 pad.4.clone
  45.6 0.1 dynamic_slice.20
  45.6 0.4 collective-permute-done.1
  46.1 1.3 collective-permute-done.2
  47.4 2.6 %constant_dynamic-slice_fusion = (bf16[4,128,512]{2,1,0:T(8,128)(2,1)}, bf16[4,128,512]{2,1,0:T(8,128)(2,1)}, bf16[4,128,512]{2,1,0:T(8,128)(2,1)}) fusion(bf16[8,512,512]{2,1,0:T(8,128)(2,1)} %ops_ref.3, s32[]{:T(128)S(6)} %select_n.174, s32[]{:T(128)S(6)} %select_n.180, s32[]{:T(128)S(6)} %select_n.178, s32[]{:T(128)S(6)} %select_n.176), kind=kLoop, calls=%fused_computation.51 | loop fusion | bytes 3145744 | tf_op jit(solution)/shard_map/dynamic_slice | solution.py:305
  50.0 0.3 collective-permute-start.3
  50.3 3.3 %collective-permute-start.5 = (bf16[4,128,512]{2,1,0:T(8,128)(2,1)}, bf16[4,128,512]{2,1,0:T(8,128)(2,1)S(1)}, u32[]{:S(2)}, u32[]{:S(2)}) collective-permute-start(bf16[4,128,512]{2,1,0:T(8,128)(2,1)} %get-tuple-element.44), channel_id=1, source_target_pairs={{0,2},{1,3},{2,0},{3,1},{4,6},{5,7},{6,4},{7,5},{8,10},{9,11},{10,... | collective-permute-start | bytes 1572872 | tf_op jit(solution)/shard_map/ppermute | solution.py:276
  53.5 0.0 collective-permute-start.7
  53.6 0.6 copy-done.6
  54.3 0.8 fusion.19
  55.1 1.1 copy.11
  56.2 4.0 %gather_fusion = s32[1024,32]{1,0:T(8,128)} fusion(s32[1024,32]{1,0:T(8,128)S(1)} %copy.11, s32[1024]{0:T(1024)S(1)} %get-tuple-element.50), kind=kCustom, calls=%fused_computation | custom fusion | bytes 266240 | tf_op jit(solution)/shard_map/jit(_take)/gather | solution.py:318
  60.2 1.4 select_select_fusion
  61.6 0.8 copy.12
  62.4 0.7 fusion.12
  63.2 0.1 reshape.108
  63.3 0.0 collective-permute-done.3.refs_0_
  63.3 4.1 %collective-permute-start.4 = (bf16[4,128,512]{2,1,0:T(8,128)(2,1)S(1)}, bf16[4,128,512]{2,1,0:T(8,128)(2,1)S(1)}, u32[]{:S(2)}, u32[]{:S(2)}) collective-permute-start(bf16[4,128,512]{2,1,0:T(8,128)(2,1)S(1)} %collective-permute-done.3.refs_0_), channel_id=1, source_target_pairs={{0,4},{4,0},{8,12},{12,8},{16,20},{20,16},{24,28},{28,24},{32,36},... | collective-permute-start | bytes 1572872 | tf_op jit(solution)/shard_map/ppermute | solution.py:279
  67.3 7.7 %collective-permute-done.5.refs_2_ = bf16[4,128,512]{2,1,0:T(8,128)(2,1)S(1)} collective-permute-done((bf16[4,128,512]{2,1,0:T(8,128)(2,1)}, bf16[4,128,512]{2,1,0:T(8,128)(2,1)S(1)}, u32[]{:S(2)}, u32[]{:S(2)}) %collective-permute-start.5) | collective-permute-done | bytes 524320 | tf_op jit(solution)/shard_map/ppermute | solution.py:276
  75.0 2.9 %collective-permute-start.6 = (bf16[4,128,512]{2,1,0:T(8,128)(2,1)S(1)}, bf16[4,128,512]{2,1,0:T(8,128)(2,1)}, u32[]{:S(2)}, u32[]{:S(2)}) collective-permute-start(bf16[4,128,512]{2,1,0:T(8,128)(2,1)S(1)} %collective-permute-done.5.refs_2_), channel_id=1, source_target_pairs={{0,4},{4,0},{8,12},{12,8},{16,20},{20,16},{24,28},{28,24},{32,36},... | collective-permute-start | bytes 1572872 | tf_op jit(solution)/shard_map/ppermute | solution.py:279
  77.9 0.0 collective-permute-done.7.refs_4_
  77.9 0.0 collective-permute-start.8
  77.9 0.9 add_add_fusion
  78.8 0.7 copy.13
  79.5 1.1 fusion.3
  80.5 0.1 fusion.18
  80.6 1.7 concatenate.42
  82.3 1.8 %broadcast_in_dim.81.idx_ref = s32[32,1,1664]{2,1,0:T(1,128)} reshape(s32[32,1664]{1,0:T(8,128)} %concatenate.42) | data formatting | bytes 425984 | tf_op jit(solution)/shard_map/broadcast_in_dim | solution.py:330
  84.1 17.8 %all-to-all-done.1 = bf16[64,160,128]{2,1,0:T(8,128)(2,1)} async-done(((bf16[64,160,128]{2,1,0:T(8,128)(2,1)}), bf16[64,160,128]{2,1,0:T(8,128)(2,1)}, u32[]{:S(2)}, u32[]{:S(2)}) %all-to-all-start.1) | async-done | bytes 2621472 | tf_op jit(solution)/shard_map/all_to_all | solution.py:293
  101.9 0.9 copy-done.3
  102.8 18.3 %translate.2 = (bf16[352,512]{1,0:T(8,128)(2,1)S(1)}, bf16[352,512]{1,0:T(8,128)(2,1)S(1)}) custom-call(s32[32,1,1664]{2,1,0:T(1,128)S(1)} %copy-done.3, s32[2]{0:T(128)S(1)} %pad_add_fusion.1.at_ref, bf16[1152,128]{1,0:T(8,128)(2,1)S(1)} %pad_maximum_fusion.own_ref, bf16[10240,128]{1,0:T(8,128)(2,1)} %bitcast.2.got_ref, bf16[8,512,512]{2,1,0:T(8,128)(2,1)} %ops_ref.3, ...), custom_call_target="tpu_custom_call" | custom-call | flops 2415919104 | bytes 41943040 | tf_op jit(solution)/shard_map/translate/pallas_call | solution.py:165
  121.1 1.3 collective-permute-start.10
  122.4 2.4 %collective-permute-start.9 = (bf16[352,512]{1,0:T(8,128)(2,1)S(1)}, bf16[352,512]{1,0:T(8,128)(2,1)S(1)}, u32[]{:S(2)}, u32[]{:S(2)}) collective-permute-start(bf16[352,512]{1,0:T(8,128)(2,1)S(1)} %get-tuple-element.31.own_ref), channel_id=1, source_target_pairs={{0,2},{1,3},{2,0},{3,1},{4,6},{5,7},{6,4},{7,5},{8,10},{9,11},{10,... | collective-permute-start | bytes 1081352 | tf_op jit(solution)/shard_map/ppermute | solution.py:276
  124.8 1.2 collective-permute-start.11
  126.1 16.0 %translate.3 = (bf16[288,512]{1,0:T(8,128)(2,1)S(1)}, f32[288,512]{1,0:T(8,128)S(1)}) custom-call(s32[32,1,1664]{2,1,0:T(1,128)S(1)} %copy-done.4, s32[2]{0:T(128)S(1)} %pad_add_fusion.1.at_ref, bf16[1152,128]{1,0:T(8,128)(2,1)S(1)} %pad_maximum_fusion.own_ref, bf16[10240,128]{1,0:T(8,128)(2,1)} %bitcast.2.got_ref, bf16[8,512,512]{2,1,0:T(8,128)(2,1)} %ops_ref.3, ...), custom_call_target="tpu_custom_call" | custom-call | flops 2415919104 | bytes 37748736 | tf_op jit(solution)/shard_map/translate/pallas_call | solution.py:165
  142.1 0.0 collective-permute-done.11.c_ref
  142.2 0.4 collective-permute-start.12
  142.6 5.5 %collective-permute-start.13 = (bf16[32,512]{1,0:T(8,128)(2,1)S(1)}, bf16[32,512]{1,0:T(8,128)(2,1)S(1)}, u32[]{:S(2)}, u32[]{:S(2)}) collective-permute-start(bf16[32,512]{1,0:T(8,128)(2,1)S(1)} %get-tuple-element.41), channel_id=1, source_target_pairs={{0,4},{4,8},{8,12},{12,16},{16,20},{20,24},{24,28},{28,32},{32,36}... | collective-permute-start | bytes 98312 | tf_op jit(solution)/shard_map/ppermute | solution.py:352
  148.1 1.9 %collective-permute-start.14 = (bf16[32,512]{1,0:T(8,128)(2,1)S(1)}, bf16[32,512]{1,0:T(8,128)(2,1)S(1)}, u32[]{:S(2)}, u32[]{:S(2)}) collective-permute-start(bf16[32,512]{1,0:T(8,128)(2,1)S(1)} %get-tuple-element.42), channel_id=1, source_target_pairs={{4,0},{8,4},{12,8},{16,12},{20,16},{24,20},{28,24},{32,28},{36,32}... | collective-permute-start | bytes 98312 | tf_op jit(solution)/shard_map/ppermute | solution.py:353
  150.1 3.3 %collective-permute-done.14.right_ref = bf16[32,512]{1,0:T(8,128)(2,1)S(1)} collective-permute-done((bf16[32,512]{1,0:T(8,128)(2,1)S(1)}, bf16[32,512]{1,0:T(8,128)(2,1)S(1)}, u32[]{:S(2)}, u32[]{:S(2)}) %collective-permute-start.14) | collective-permute-done | bytes 32800 | tf_op jit(solution)/shard_map/ppermute | solution.py:353
  153.4 1.0 finish.1
  154.3 2.1 %collective-permute-start.15 = (bf16[256,512]{1,0:T(8,128)(2,1)S(1)}, bf16[256,512]{1,0:T(8,128)(2,1)S(1)}, u32[]{:S(2)}, u32[]{:S(2)}) collective-permute-start(bf16[256,512]{1,0:T(8,128)(2,1)S(1)} %finish.1), channel_id=1, source_target_pairs={{0,2},{1,3},{2,0},{3,1},{4,6},{5,7},{6,4},{7,5},{8,10},{9,11},{10,... | collective-permute-start | bytes 786440 | tf_op jit(solution)/shard_map/ppermute | solution.py:276
  156.5 2.7 %collective-permute-start.17 = (bf16[256,512]{1,0:T(8,128)(2,1)S(1)}, bf16[256,512]{1,0:T(8,128)(2,1)S(1)}, u32[]{:S(2)}, u32[]{:S(2)}) collective-permute-start(bf16[256,512]{1,0:T(8,128)(2,1)S(1)} %finish.1), channel_id=1, source_target_pairs={{0,3},{1,0},{2,1},{3,2},{4,7},{5,4},{6,5},{7,6},{8,11},{9,8},{10,9... | collective-permute-start | bytes 786440 | tf_op jit(solution)/shard_map/ppermute | solution.py:276
  159.1 0.1 broadcast_in_dim.66
  159.3 4.8 %collective-permute-done.15 = bf16[256,512]{1,0:T(8,128)(2,1)S(1)} collective-permute-done((bf16[256,512]{1,0:T(8,128)(2,1)S(1)}, bf16[256,512]{1,0:T(8,128)(2,1)S(1)}, u32[]{:S(2)}, u32[]{:S(2)}) %collective-permute-start.15) | collective-permute-done | bytes 262176 | tf_op jit(solution)/shard_map/ppermute | solution.py:276
  164.1 4.5 %collective-permute-done.16 = bf16[256,512]{1,0:T(8,128)(2,1)S(1)} collective-permute-done((bf16[256,512]{1,0:T(8,128)(2,1)S(1)}, bf16[256,512]{1,0:T(8,128)(2,1)S(1)}, u32[]{:S(2)}, u32[]{:S(2)}) %collective-permute-start.16) | collective-permute-done | bytes 262176 | tf_op jit(solution)/shard_map/ppermute | solution.py:276
  168.6 0.0 copy-start.5
  168.6 0.9 copy-done.5
  169.5 0.7 constant_dynamic-update-slice_fusion.6
  (40 shorter events, 0.3 us)
Async XLA Ops:
  0.0 15.5 %copy-start = (bf16[1024,512]{1,0:T(8,128)(2,1)S(1)}, bf16[1024,512]{1,0:T(8,128)(2,1)}, u32[]{:S(2)}) copy-start(bf16[1024,512]{1,0:T(8,128)(2,1)} %param.9) | copy-start | bytes 3145732
  2.4 23.3 %all-to-all-start = ((s32[64,1,160]{2,1,0:T(1,128)}), s32[64,1,160]{2,1,0:T(1,128)S(1)}, u32[]{:S(2)}, u32[]{:S(2)}) async-start(s32[64,1,160]{2,1,0:T(1,128)} %compare_select_fusion.1), calls=%async_computation | async-start | bytes 131072 | tf_op jit(solution)/shard_map/all_to_all | solution.py:284
  16.4 24.0 %copy-start.7 = (s32[8,1024]{1,0:T(8,128)S(1)}, s32[8,1024]{1,0:T(8,128)}, u32[]{:S(2)}) copy-start(s32[8,1024]{1,0:T(8,128)} %param.11) | copy-start | bytes 98308
  16.4 24.1 %copy-start.9 = (s32[8,128]{1,0:T(8,128)S(1)}, s32[8,128]{1,0:T(8,128)}, u32[]{:S(2)}) copy-start(s32[8,128]{1,0:T(8,128)} %param.14) | copy-start | bytes 12292
  16.4 29.0 %copy-start.8 = (s32[1024]{0:T(1024)S(1)}, s32[1024]{0:T(1024)}, u32[]{:S(2)}) copy-start(s32[1024]{0:T(1024)} %param.17) | copy-start | bytes 12292
  33.6 1.5 copy-start.1
  35.1 66.8 %all-to-all-start.1 = ((bf16[64,160,128]{2,1,0:T(8,128)(2,1)}), bf16[64,160,128]{2,1,0:T(8,128)(2,1)}, u32[]{:S(2)}, u32[]{:S(2)}) async-start(bf16[64,160,128]{2,1,0:T(8,128)(2,1)} %copy-done.1), calls=%async_computation.1 | async-start | bytes 5242880 | tf_op jit(solution)/shard_map/all_to_all | solution.py:293
  40.5 5.2 %collective-permute-start = (s32[8,1152]{1,0:T(8,128)S(1)}, s32[8,1152]{1,0:T(8,128)S(1)}, u32[]{:S(2)}, u32[]{:S(2)}) collective-permute-start(s32[8,1152]{1,0:T(8,128)S(1)} %constant_dynamic-update-slice_fusion), channel_id=1, source_target_pairs={{0,1},{1,2},{2,3},{3,0},{4,5},{5,6},{6,7},{7,4},{8,9},{9,10},{10,1... | collective-permute-start | bytes 110600 | tf_op jit(solution)/shard_map/ppermute | solution.py:276
  41.8 4.3 %collective-permute-start.1 = (s32[8,1152]{1,0:T(8,128)S(1)}, s32[8,1152]{1,0:T(8,128)S(1)}, u32[]{:S(2)}, u32[]{:S(2)}) collective-permute-start(s32[8,1152]{1,0:T(8,128)S(1)} %constant_dynamic-update-slice_fusion), channel_id=1, source_target_pairs={{0,2},{1,3},{2,0},{3,1},{4,6},{5,7},{6,4},{7,5},{8,10},{9,11},{10,... | collective-permute-start | bytes 110600 | tf_op jit(solution)/shard_map/ppermute | solution.py:276
  44.2 3.2 %collective-permute-start.2 = (s32[8,1152]{1,0:T(8,128)S(1)}, s32[8,1152]{1,0:T(8,128)S(1)}, u32[]{:S(2)}, u32[]{:S(2)}) collective-permute-start(s32[8,1152]{1,0:T(8,128)S(1)} %constant_dynamic-update-slice_fusion), channel_id=1, source_target_pairs={{0,3},{1,0},{2,1},{3,2},{4,7},{5,4},{6,5},{7,6},{8,11},{9,8},{10,9... | collective-permute-start | bytes 110600 | tf_op jit(solution)/shard_map/ppermute | solution.py:276
  50.0 13.3 %collective-permute-start.3 = (bf16[4,128,512]{2,1,0:T(8,128)(2,1)}, bf16[4,128,512]{2,1,0:T(8,128)(2,1)S(1)}, u32[]{:S(2)}, u32[]{:S(2)}) collective-permute-start(bf16[4,128,512]{2,1,0:T(8,128)(2,1)} %get-tuple-element.45), channel_id=1, source_target_pairs={{0,1},{1,2},{2,3},{3,0},{4,5},{5,6},{6,7},{7,4},{8,9},{9,10},{10,1... | collective-permute-start | bytes 1572872 | tf_op jit(solution)/shard_map/ppermute | solution.py:276
  50.3 24.7 %collective-permute-start.5 = (bf16[4,128,512]{2,1,0:T(8,128)(2,1)}, bf16[4,128,512]{2,1,0:T(8,128)(2,1)S(1)}, u32[]{:S(2)}, u32[]{:S(2)}) collective-permute-start(bf16[4,128,512]{2,1,0:T(8,128)(2,1)} %get-tuple-element.44), channel_id=1, source_target_pairs={{0,2},{1,3},{2,0},{3,1},{4,6},{5,7},{6,4},{7,5},{8,10},{9,11},{10,... | collective-permute-start | bytes 1572872 | tf_op jit(solution)/shard_map/ppermute | solution.py:276
  53.5 24.3 %collective-permute-start.7 = (bf16[4,128,512]{2,1,0:T(8,128)(2,1)}, bf16[4,128,512]{2,1,0:T(8,128)(2,1)S(1)}, u32[]{:S(2)}, u32[]{:S(2)}) collective-permute-start(bf16[4,128,512]{2,1,0:T(8,128)(2,1)} %get-tuple-element.43), channel_id=1, source_target_pairs={{0,3},{1,0},{2,1},{3,2},{4,7},{5,4},{6,5},{7,6},{8,11},{9,8},{10,9... | collective-permute-start | bytes 1572872 | tf_op jit(solution)/shard_map/ppermute | solution.py:276
  53.6 0.7 copy-start.6
  63.3 38.6 %collective-permute-start.4 = (bf16[4,128,512]{2,1,0:T(8,128)(2,1)S(1)}, bf16[4,128,512]{2,1,0:T(8,128)(2,1)S(1)}, u32[]{:S(2)}, u32[]{:S(2)}) collective-permute-start(bf16[4,128,512]{2,1,0:T(8,128)(2,1)S(1)} %collective-permute-done.3.refs_0_), channel_id=1, source_target_pairs={{0,4},{4,0},{8,12},{12,8},{16,20},{20,16},{24,28},{28,24},{32,36},... | collective-permute-start | bytes 1572872 | tf_op jit(solution)/shard_map/ppermute | solution.py:279
  75.0 26.9 %collective-permute-start.6 = (bf16[4,128,512]{2,1,0:T(8,128)(2,1)S(1)}, bf16[4,128,512]{2,1,0:T(8,128)(2,1)}, u32[]{:S(2)}, u32[]{:S(2)}) collective-permute-start(bf16[4,128,512]{2,1,0:T(8,128)(2,1)S(1)} %collective-permute-done.5.refs_2_), channel_id=1, source_target_pairs={{0,4},{4,0},{8,12},{12,8},{16,20},{20,16},{24,28},{28,24},{32,36},... | collective-permute-start | bytes 1572872 | tf_op jit(solution)/shard_map/ppermute | solution.py:279
  77.9 24.0 %collective-permute-start.8 = (bf16[4,128,512]{2,1,0:T(8,128)(2,1)S(1)}, bf16[4,128,512]{2,1,0:T(8,128)(2,1)}, u32[]{:S(2)}, u32[]{:S(2)}) collective-permute-start(bf16[4,128,512]{2,1,0:T(8,128)(2,1)S(1)} %collective-permute-done.7.refs_4_), channel_id=1, source_target_pairs={{0,4},{4,0},{8,12},{12,8},{16,20},{20,16},{24,28},{28,24},{32,36},... | collective-permute-start | bytes 1572872 | tf_op jit(solution)/shard_map/ppermute | solution.py:279
  101.9 0.9 copy-start.3
  102.8 23.3 %copy-start.4 = (s32[32,1,1664]{2,1,0:T(1,128)S(1)}, s32[32,1,1664]{2,1,0:T(1,128)}, u32[]{:S(2)}) copy-start(s32[32,1,1664]{2,1,0:T(1,128)} %broadcast_in_dim.81.idx_ref) | copy-start | bytes 638980
  121.1 21.0 %collective-permute-start.10 = (bf16[352,512]{1,0:T(8,128)(2,1)S(1)}, bf16[352,512]{1,0:T(8,128)(2,1)S(1)}, u32[]{:S(2)}, u32[]{:S(2)}) collective-permute-start(bf16[352,512]{1,0:T(8,128)(2,1)S(1)} %get-tuple-element.32), channel_id=1, source_target_pairs={{0,1},{1,2},{2,3},{3,0},{4,5},{5,6},{6,7},{7,4},{8,9},{9,10},{10,1... | collective-permute-start | bytes 1081352 | tf_op jit(solution)/shard_map/ppermute | solution.py:276
  122.4 19.8 %collective-permute-start.9 = (bf16[352,512]{1,0:T(8,128)(2,1)S(1)}, bf16[352,512]{1,0:T(8,128)(2,1)S(1)}, u32[]{:S(2)}, u32[]{:S(2)}) collective-permute-start(bf16[352,512]{1,0:T(8,128)(2,1)S(1)} %get-tuple-element.31.own_ref), channel_id=1, source_target_pairs={{0,2},{1,3},{2,0},{3,1},{4,6},{5,7},{6,4},{7,5},{8,10},{9,11},{10,... | collective-permute-start | bytes 1081352 | tf_op jit(solution)/shard_map/ppermute | solution.py:276
  124.8 28.5 %copy-start.2 = (bf16[8,512,512]{2,1,0:T(8,128)(2,1)S(1)}, bf16[8,512,512]{2,1,0:T(8,128)(2,1)}, u32[]{:S(2)}) copy-start(bf16[8,512,512]{2,1,0:T(8,128)(2,1)} %l2l_ref.1) | copy-start | bytes 12582916
  124.8 17.3 %collective-permute-start.11 = (bf16[64,512]{1,0:T(8,128)(2,1)S(1)}, bf16[64,512]{1,0:T(8,128)(2,1)S(1)}, u32[]{:S(2)}, u32[]{:S(2)}) collective-permute-start(bf16[64,512]{1,0:T(8,128)(2,1)S(1)} %slice.19), channel_id=1, source_target_pairs={{0,3},{1,0},{2,1},{3,2},{4,7},{5,4},{6,5},{7,6},{8,11},{9,8},{10,9... | collective-permute-start | bytes 196616 | tf_op jit(solution)/shard_map/ppermute | solution.py:276
  142.2 11.2 %collective-permute-start.12 = (bf16[288,512]{1,0:T(8,128)(2,1)S(1)}, bf16[288,512]{1,0:T(8,128)(2,1)S(1)}, u32[]{:S(2)}, u32[]{:S(2)}) collective-permute-start(bf16[288,512]{1,0:T(8,128)(2,1)S(1)} %get-tuple-element.38), channel_id=1, source_target_pairs={{0,3},{1,0},{2,1},{3,2},{4,7},{5,4},{6,5},{7,6},{8,11},{9,8},{10,9... | collective-permute-start | bytes 884744 | tf_op jit(solution)/shard_map/ppermute | solution.py:276
  142.6 7.4 %collective-permute-start.13 = (bf16[32,512]{1,0:T(8,128)(2,1)S(1)}, bf16[32,512]{1,0:T(8,128)(2,1)S(1)}, u32[]{:S(2)}, u32[]{:S(2)}) collective-permute-start(bf16[32,512]{1,0:T(8,128)(2,1)S(1)} %get-tuple-element.41), channel_id=1, source_target_pairs={{0,4},{4,8},{8,12},{12,16},{16,20},{20,24},{24,28},{28,32},{32,36}... | collective-permute-start | bytes 98312 | tf_op jit(solution)/shard_map/ppermute | solution.py:352
  148.1 5.2 %collective-permute-start.14 = (bf16[32,512]{1,0:T(8,128)(2,1)S(1)}, bf16[32,512]{1,0:T(8,128)(2,1)S(1)}, u32[]{:S(2)}, u32[]{:S(2)}) collective-permute-start(bf16[32,512]{1,0:T(8,128)(2,1)S(1)} %get-tuple-element.42), channel_id=1, source_target_pairs={{4,0},{8,4},{12,8},{16,12},{20,16},{24,20},{28,24},{32,28},{36,32}... | collective-permute-start | bytes 98312 | tf_op jit(solution)/shard_map/ppermute | solution.py:353
  154.3 9.7 %collective-permute-start.15 = (bf16[256,512]{1,0:T(8,128)(2,1)S(1)}, bf16[256,512]{1,0:T(8,128)(2,1)S(1)}, u32[]{:S(2)}, u32[]{:S(2)}) collective-permute-start(bf16[256,512]{1,0:T(8,128)(2,1)S(1)} %finish.1), channel_id=1, source_target_pairs={{0,2},{1,3},{2,0},{3,1},{4,6},{5,7},{6,4},{7,5},{8,10},{9,11},{10,... | collective-permute-start | bytes 786440 | tf_op jit(solution)/shard_map/ppermute | solution.py:276
  156.5 12.1 %collective-permute-start.16 = (bf16[256,512]{1,0:T(8,128)(2,1)S(1)}, bf16[256,512]{1,0:T(8,128)(2,1)S(1)}, u32[]{:S(2)}, u32[]{:S(2)}) collective-permute-start(bf16[256,512]{1,0:T(8,128)(2,1)S(1)} %finish.1), channel_id=1, source_target_pairs={{0,1},{1,2},{2,3},{3,0},{4,5},{5,6},{6,7},{7,4},{8,9},{9,10},{10,1... | collective-permute-start | bytes 786440 | tf_op jit(solution)/shard_map/ppermute | solution.py:276
  156.5 12.1 %collective-permute-start.17 = (bf16[256,512]{1,0:T(8,128)(2,1)S(1)}, bf16[256,512]{1,0:T(8,128)(2,1)S(1)}, u32[]{:S(2)}, u32[]{:S(2)}) collective-permute-start(bf16[256,512]{1,0:T(8,128)(2,1)S(1)} %finish.1), channel_id=1, source_target_pairs={{0,3},{1,0},{2,1},{3,2},{4,7},{5,4},{6,5},{7,6},{8,11},{9,8},{10,9... | collective-permute-start | bytes 786440 | tf_op jit(solution)/shard_map/ppermute | solution.py:276
  168.6 1.0 copy-start.5

commit v5 on v4

--- a/solution.py
+++ b/solution.py
@@ -11,6 +11,7 @@
 LANES = 128
 CORES = 2
 COARSE_FACTOR = 0.5
+EARLY = 144
 VMEM_LIMIT = 48 << 20
 
 
@@ -23,11 +24,11 @@
     lax.fori_loop(0, source.shape[0] // block, step, 0)
 
 
-def gather_rows(lists, table, out, count, unroll):
+def gather_rows(lists, table, out, first, count, unroll):
     def step(i, carry):
         for k in range(unroll):
             r = i * unroll + k
-            picked = [table[pl.ds(entries[0, r], 1), :] for entries in lists]
+            picked = [table[pl.ds(entries[0, first + r], 1), :] for entries in lists]
             for s, row in enumerate(picked):
                 out[s, pl.ds(r, 1), :] = row
         return carry
@@ -44,7 +45,7 @@
     table[pl.ds(count, 8), :] = jnp.zeros((8, LANES), jnp.float32)
     for copy in copies:
         copy.wait()
-    gather_rows(lists, table, rows, rows.shape[1], 2)
+    gather_rows(lists, table, rows, 0, rows.shape[1], 2)
 
     def narrow(s, carry):
         out_ref[s] = rows[s].astype(out_ref.dtype)
@@ -89,12 +90,12 @@
     return total
 
 
-def translate_kernel(shifts, halo, idx_ref, at_ref, own_ref, got_ref, ops_ref, *refs):
+def translate_kernel(jobs, halo, idx_ref, at_ref, own_ref, got_ref, ops_ref, *refs):
     weight_refs, refs = refs[:6], refs[6:]
-    outs, refs = refs[: len(shifts)], refs[len(shifts) :]
+    outs, refs = refs[: len(jobs)], refs[len(jobs) :]
     table, landed, rows, weights, got_sem, list_sem, weight_sem = refs[:7]
     lists = refs[7:]
-    operators, chunk = rows.shape[:2]
+    operators = rows.shape[0]
     members, ops = 4, ops_ref.shape[0]
     me, core = at_ref[0], at_ref[1]
     own, got = own_ref.shape[0], landed.shape[0]
@@ -106,11 +107,14 @@
             pltpu.make_async_copy(got_ref.at[part, :], landed.at[part, :], got_sem.at[n])
         )
     stride = (idx_ref.shape[2] - LANES) // members
-    sets = [(pl.multiple_of(lax.rem(me + s, members) * stride, LANES), chunk) for s in shifts]
+    sets = [
+        (pl.multiple_of(lax.rem(me + shift, members) * stride, LANES), first, count)
+        for shift, first, count in jobs
+    ]
     if halo:
-        sets = [(members * stride, halo)] + sets
+        sets = [(members * stride, 0, halo)] + sets
     copies = []
-    for n, (start, _) in enumerate(sets):
+    for n, (start, _, _) in enumerate(sets):
         batch = []
         for o in range(operators):
             entries = lists[n * operators + o]
@@ -138,39 +142,42 @@
         widen(
             landed.at[pl.ds(n * piece, piece), :], table.at[pl.ds(own + n * piece, piece), :], 512
         )
-    for n, (_, count) in enumerate(sets):
+    for n, (_, first, count) in enumerate(sets):
         for copy in copies[n]:
             copy.wait()
         chosen = lists[n * operators : (n + 1) * operators]
-        edge_rows = halo and n == 0
-        gather_rows(chosen, table, rows, count, 8)
+        gather_rows(chosen, table, rows, first, count, 8)
         if n == 0:
             for copy in heavy:
                 copy.wait()
         total = operator_sum(rows, weights, count)
-        if edge_rows:
+        if halo and n == 0:
             for out in outs:
-                out[pl.ds(chunk, halo), :] = total.astype(out.dtype)
+                out[pl.ds(out.shape[0] - halo, halo), :] = total.astype(out.dtype)
         else:
             out = outs[n - (1 if halo else 0)]
-            out[pl.ds(0, chunk), :] = total.astype(out.dtype)
-
-
-def translate(idx, at, own, got, operators, weights, chunk, shifts, halo, dtypes):
+            out[pl.ds(0, count), :] = total.astype(out.dtype)
+
+
+def translate(idx, at, own, got, operators, weights, jobs, halo, dtypes):
     every, columns = idx.shape[0], operators.shape[2]
     vmem = pl.BlockSpec(memory_space=pltpu.VMEM)
     hbm = pl.BlockSpec(memory_space=pltpu.HBM)
     stride = (idx.shape[2] - LANES) // 4
-    lengths = ([LANES] if halo else []) + [stride] * len(shifts)
+    lengths = ([LANES] if halo else []) + [stride] * len(jobs)
+    counts = [count for _, _, count in jobs]
     return pl.pallas_call(
-        functools.partial(translate_kernel, shifts, halo),
-        out_shape=[jax.ShapeDtypeStruct((chunk + halo, columns), dtype) for dtype in dtypes],
+        functools.partial(translate_kernel, jobs, halo),
+        out_shape=[
+            jax.ShapeDtypeStruct((count + halo, columns), dtype)
+            for count, dtype in zip(counts, dtypes)
+        ],
         in_specs=[hbm, pl.BlockSpec(memory_space=pltpu.SMEM), vmem] + [hbm] * (2 + len(weights)),
-        out_specs=[vmem] * len(shifts),
+        out_specs=[vmem] * len(jobs),
         scratch_shapes=[
             pltpu.VMEM((own.shape[0] + got.shape[0] + 8, LANES), jnp.float32),
             pltpu.VMEM(got.shape, own.dtype),
-            pltpu.VMEM((every, chunk, LANES), jnp.float32),
+            pltpu.VMEM((every, max(counts), LANES), jnp.float32),
             pltpu.VMEM((every, LANES, columns), operators.dtype),
             pltpu.SemaphoreType.DMA((4,)),
             pltpu.SemaphoreType.DMA((len(lengths),)),
@@ -179,8 +186,8 @@
         + [pltpu.SMEM((1, length), jnp.int32) for length in lengths for _ in range(every)],
         compiler_params=pltpu.CompilerParams(vmem_limit_bytes=VMEM_LIMIT),
         cost_estimate=pl.CostEstimate(
-            flops=2 * every * LANES * columns * chunk * len(shifts),
-            bytes_accessed=2 * every * (chunk * len(shifts) + halo) * LANES * 8,
+            flops=2 * every * LANES * columns * sum(counts),
+            bytes_accessed=2 * every * (sum(counts) + halo) * LANES * 8,
             transcendentals=0,
         ),
         name="translate",
@@ -210,17 +217,20 @@
 
 
 def finish_kernel(
-    own_ref, a_ref, b_ref, c_ref, place_ref, left_ref, right_ref, l2l_ref, out_ref, acc
+    own_ref, a_ref, b_ref, early_ref, late_ref, place_ref, left_ref, right_ref, l2l_ref, out_ref, acc
 ):
     rows, columns = out_ref.shape
     octants = l2l_ref.shape[0]
     count = rows // octants
+    split = own_ref.shape[0] - late_ref.shape[0]
 
     def total(first, size):
         part = own_ref[pl.ds(first, size), :]
-        for ref in (a_ref, b_ref, c_ref):
+        for ref in (a_ref, b_ref):
             part = part + ref[pl.ds(first, size), :].astype(jnp.float32)
-        return part
+        head = [early_ref[pl.ds(first, split - first), :]] if first < split else []
+        tail = late_ref[pl.ds(max(first - split, 0), size - max(split - first, 0)), :]
+        return part + jnp.concatenate(head + [tail], axis=0).astype(jnp.float32)
 
     parent = (total(rows, count) * COARSE_FACTOR).astype(jnp.bfloat16)
     slabs = columns // LANES
@@ -248,7 +258,7 @@
     return pl.pallas_call(
         finish_kernel,
         out_shape=jax.ShapeDtypeStruct((rows, columns), jnp.bfloat16),
-        in_specs=[vmem] * 8,
+        in_specs=[vmem] * 9,
         out_specs=vmem,
         scratch_shapes=[pltpu.VMEM((columns // LANES, rows, LANES), jnp.float32)],
         compiler_params=pltpu.CompilerParams(vmem_limit_bytes=VMEM_LIMIT),
@@ -340,18 +350,19 @@
     place = lax.dynamic_slice_in_dim(place, me * quarter_f, quarter_f, 0)[None, :]
     got, place, idx = lax.optimization_barrier((got, place, idx))
 
-    def sums(shifts, halo, dtypes):
-        return translate(idx, at, own, got, operators, weights, chunk, shifts, halo, dtypes)
-
-    away = sums((2, 1), 2 * R, (jnp.bfloat16, jnp.bfloat16))
-    halo_3 = shifted(away[0][chunk:], 3)
-    others = [shifted(part, s) for part, s in zip(away, (2, 1))]
-    last, mine = sums((3, 0), 0, (jnp.bfloat16, jnp.float32))
-    others, halo_3, last, mine = lax.optimization_barrier((others, halo_3, last, mine))
-    head, tail = edges([away[0]] + others + [halo_3], 2 * R)
+    def sums(jobs, halo, dtypes):
+        return translate(idx, at, own, got, operators, weights, jobs, halo, dtypes)
+
+    narrow = jnp.bfloat16
+    whole = (0, chunk)
+    away = sums(((2, *whole), (1, *whole), (3, 0, EARLY)), 2 * R, (narrow, narrow, narrow))
+    others = [shifted(part, s) for part, s in zip(away, (2, 1, 3))]
+    late, mine = sums(((3, EARLY, chunk - EARLY), (0, *whole)), 0, (narrow, jnp.float32))
+    others, late, mine = lax.optimization_barrier((others, late, mine))
+    head, tail = edges([away[0]] + others, 2 * R)
     from_left = lax.ppermute(tail, "box", [(i, i + 1) for i in range(blocks - 1)])
     from_right = lax.ppermute(head, "box", [(i + 1, i) for i in range(blocks - 1)])
-    others = others + [shifted(last, 3)]
+    others = others + [shifted(late, 3)]
     done = finish(mine, others, place, from_left, from_right, l2l_ops)
     out = jnp.zeros((rows_f, coefficients), jnp.bfloat16)
     for s in (0, 2, 1, 3):

time: 171 us -> 170 us (level)
  local copies, waits for them, and re-layouts: 19.7 us -> 14.8 us
  waiting for transfers between devices: 49 us -> 52.8 us
    all_to_all x1, waiting for transfers between devices: 17.8 us -> 21.7 us  [per_device(): got = lax.all_to_all(sent, 'box', split_axis=0, concat_axis=0, tiled=True)]
    unnamed x26 -> x22, local copies, waits for them, and re-layouts: 5.67 us -> 4.08 us
  transfers between devices with their start and end apart: 20 -> 20, of which waited for: 8 -> 9; matrix products, arithmetic and copies ran while one was open for 11% -> 9% of each run, Pallas kernels for 9% -> 8%
where the time goes in v5:
time: 170 us; the launch traced here: 169 us
  waiting for transfers between devices  52.8 us (31%)
  starting transfers between devices  51 us (30%)
  Pallas kernels  43.7 us (26%)
  local copies, waits for them, and re-layouts  14.8 us (9%)
  other arithmetic  6.51 us (4%)
    pallas_call x2, Pallas kernels, translate(): pl.pallas_call(functools.partial(translate_kernel, jobs, halo), out_shape...  34.8 us
    all_to_all x1, waiting for transfers between devices, per_device(): got = lax.all_to_all(sent, 'box', split_axis=0, concat_axis=0, tiled=True)  21.7 us
    ppermute x13, starting transfers between devices, shifted(): lax.ppermute(value, 'grp', [(i, (i + by) % members) for i in range(member...  19.2 us
    ppermute x13, waiting for transfers between devices, shifted(): lax.ppermute(value, 'grp', [(i, (i + by) % members) for i in range(member...  18.7 us
    all_to_all x1, starting transfers between devices, per_device(): lax.all_to_all(requests, 'box', split_axis=0, concat_axis=0, tiled=True)  13.2 us
    all_to_all x1, waiting for transfers between devices, per_device(): lax.all_to_all(requests, 'box', split_axis=0, concat_axis=0, tiled=True)  9.19 us
    pallas_call x1, Pallas kernels, pick(): pl.pallas_call(pick_kernel, out_shape=jax.ShapeDtypeStruct((parts, length...  7.93 us
    ppermute x3, starting transfers between devices, swapped(): return lax.ppermute(value, 'box', [(i, i ^ 1) for i in range(blocks)])  6.94 us
  transfers between devices with their start and end apart: 20, of which 9 were waited for; matrix products, arithmetic and copies ran while one was open for 9% of the time, Pallas kernels for 8%

profile of v5, /device:TPU:1, one launch (start us, length us, event | category | flops | bytes accessed | tf_op | source)
XLA Modules:
  0.0 169.3 jit_solution(7150750048548348194)
XLA Ops:
  0.0 0.9 copy.10
  0.9 1.5 compare_select_fusion.1
  2.4 13.2 %all-to-all-start = ((s32[64,1,160]{2,1,0:T(1,128)}), s32[64,1,160]{2,1,0:T(1,128)S(1)}, u32[]{:S(2)}, u32[]{:S(2)}) async-start(s32[64,1,160]{2,1,0:T(1,128)} %compare_select_fusion.1), calls=%async_computation | async-start | bytes 131072 | tf_op jit(solution)/shard_map/all_to_all | solution.py:294
  15.6 0.8 constant_dynamic-slice_fusion.3
  16.4 0.0 copy-start.5
  16.4 0.0 copy-start.7
  16.4 0.0 copy-start.6
  16.4 9.2 %all-to-all-done.wanted_ref = s32[64,1,160]{2,1,0:T(1,128)S(1)} async-done(((s32[64,1,160]{2,1,0:T(1,128)}), s32[64,1,160]{2,1,0:T(1,128)S(1)}, u32[]{:S(2)}, u32[]{:S(2)}) %all-to-all-start) | async-done | bytes 40992 | tf_op jit(solution)/shard_map/all_to_all | solution.py:294
  25.6 7.9 %pick.1 = bf16[64,160,128]{2,1,0:T(8,128)(2,1)S(1)} custom-call(s32[64,1,160]{2,1,0:T(1,128)S(1)} %all-to-all-done.wanted_ref, bf16[1152,128]{1,0:T(8,128)(2,1)S(1)} %pad_maximum_fusion.own_ref), custom_call_target="tpu_custom_call" | custom-call | bytes 20971520 | tf_op jit(solution)/shard_map/pick/pallas_call | solution.py:60
  33.6 1.5 copy-done.1
  35.1 5.3 %all-to-all-start.1 = ((bf16[64,160,128]{2,1,0:T(8,128)(2,1)}), bf16[64,160,128]{2,1,0:T(8,128)(2,1)}, u32[]{:S(2)}, u32[]{:S(2)}) async-start(bf16[64,160,128]{2,1,0:T(8,128)(2,1)} %copy-done.1), calls=%async_computation.1 | async-start | bytes 5242880 | tf_op jit(solution)/shard_map/all_to_all | solution.py:303
  40.5 1.3 collective-permute-start
  41.8 2.5 %collective-permute-start.1 = (s32[8,1152]{1,0:T(8,128)S(1)}, s32[8,1152]{1,0:T(8,128)S(1)}, u32[]{:S(2)}, u32[]{:S(2)}) collective-permute-start(s32[8,1152]{1,0:T(8,128)S(1)} %constant_dynamic-update-slice_fusion), channel_id=1, source_target_pairs={{0,2},{1,3},{2,0},{3,1},{4,6},{5,7},{6,4},{7,5},{8,10},{9,11},{10,... | collective-permute-start | bytes 110600 | tf_op jit(solution)/shard_map/ppermute | solution.py:286
  44.2 1.2 collective-permute-start.2
  45.4 0.1 pad_add_fusion.1.at_ref
  45.5 0.1 pad.4.clone
  45.6 0.1 dynamic_slice.20
  45.6 0.4 collective-permute-done.1
  46.1 1.3 collective-permute-done.2
  47.4 2.6 %constant_dynamic-slice_fusion = (bf16[4,128,512]{2,1,0:T(8,128)(2,1)}, bf16[4,128,512]{2,1,0:T(8,128)(2,1)}, bf16[4,128,512]{2,1,0:T(8,128)(2,1)}) fusion(bf16[8,512,512]{2,1,0:T(8,128)(2,1)} %ops_ref.3, s32[]{:T(128)S(6)} %select_n.174, s32[]{:T(128)S(6)} %select_n.180, s32[]{:T(128)S(6)} %select_n.178, s32[]{:T(128)S(6)} %select_n.176), kind=kLoop, calls=%fused_computation.51 | loop fusion | bytes 3145744 | tf_op jit(solution)/shard_map/dynamic_slice | solution.py:315
  50.0 0.3 collective-permute-start.3
  50.3 3.3 %collective-permute-start.5 = (bf16[4,128,512]{2,1,0:T(8,128)(2,1)}, bf16[4,128,512]{2,1,0:T(8,128)(2,1)S(1)}, u32[]{:S(2)}, u32[]{:S(2)}) collective-permute-start(bf16[4,128,512]{2,1,0:T(8,128)(2,1)} %get-tuple-element.46), channel_id=1, source_target_pairs={{0,2},{1,3},{2,0},{3,1},{4,6},{5,7},{6,4},{7,5},{8,10},{9,11},{10,... | collective-permute-start | bytes 1572872 | tf_op jit(solution)/shard_map/ppermute | solution.py:286
  53.5 0.0 collective-permute-start.7
  53.6 0.6 copy-done.4
  54.3 0.8 fusion.19
  55.1 1.1 copy.11
  56.2 4.0 %gather_fusion = s32[1024,32]{1,0:T(8,128)} fusion(s32[1024,32]{1,0:T(8,128)S(1)} %copy.11, s32[1024]{0:T(1024)S(1)} %get-tuple-element.52), kind=kCustom, calls=%fused_computation | custom fusion | bytes 266240 | tf_op jit(solution)/shard_map/jit(_take)/gather | solution.py:328
  60.2 1.4 select_select_fusion
  61.6 0.8 copy.12
  62.4 0.7 fusion.12
  63.2 0.1 reshape.108
  63.3 4.1 %collective-permute-start.4 = (bf16[4,128,512]{2,1,0:T(8,128)(2,1)S(1)}, bf16[4,128,512]{2,1,0:T(8,128)(2,1)}, u32[]{:S(2)}, u32[]{:S(2)}) collective-permute-start(bf16[4,128,512]{2,1,0:T(8,128)(2,1)S(1)} %collective-permute-done.3.refs_0_), channel_id=1, source_target_pairs={{0,4},{4,0},{8,12},{12,8},{16,20},{20,16},{24,28},{28,24},{32,36},... | collective-permute-start | bytes 1572872 | tf_op jit(solution)/shard_map/ppermute | solution.py:289
  67.3 7.7 %collective-permute-done.5.refs_2_ = bf16[4,128,512]{2,1,0:T(8,128)(2,1)S(1)} collective-permute-done((bf16[4,128,512]{2,1,0:T(8,128)(2,1)}, bf16[4,128,512]{2,1,0:T(8,128)(2,1)S(1)}, u32[]{:S(2)}, u32[]{:S(2)}) %collective-permute-start.5) | collective-permute-done | bytes 524320 | tf_op jit(solution)/shard_map/ppermute | solution.py:286
  75.0 2.9 %collective-permute-start.6 = (bf16[4,128,512]{2,1,0:T(8,128)(2,1)S(1)}, bf16[4,128,512]{2,1,0:T(8,128)(2,1)}, u32[]{:S(2)}, u32[]{:S(2)}) collective-permute-start(bf16[4,128,512]{2,1,0:T(8,128)(2,1)S(1)} %collective-permute-done.5.refs_2_), channel_id=1, source_target_pairs={{0,4},{4,0},{8,12},{12,8},{16,20},{20,16},{24,28},{28,24},{32,36},... | collective-permute-start | bytes 1572872 | tf_op jit(solution)/shard_map/ppermute | solution.py:289
  77.9 0.0 collective-permute-start.8
  77.9 0.9 add_add_fusion
  78.8 1.1 fusion.3
  79.9 0.1 fusion.18
  80.0 0.1 concatenate.42
  80.1 0.1 broadcast_in_dim.81.idx_ref
  80.2 21.7 %all-to-all-done.1 = bf16[64,160,128]{2,1,0:T(8,128)(2,1)} async-done(((bf16[64,160,128]{2,1,0:T(8,128)(2,1)}), bf16[64,160,128]{2,1,0:T(8,128)(2,1)}, u32[]{:S(2)}, u32[]{:S(2)}) %all-to-all-start.1) | async-done | bytes 2621472 | tf_op jit(solution)/shard_map/all_to_all | solution.py:303
  101.9 0.0 collective-permute-done.4.refs_1_
  101.9 21.9 %translate.2 = (bf16[352,512]{1,0:T(8,128)(2,1)S(1)}, bf16[352,512]{1,0:T(8,128)(2,1)S(1)}, bf16[208,512]{1,0:T(8,128)(2,1)S(1)}) custom-call(s32[32,1,1664]{2,1,0:T(1,128)S(1)} %broadcast_in_dim.81.idx_ref, s32[2]{0:T(128)S(1)} %pad_add_fusion.1.at_ref, bf16[1152,128]{1,0:T(8,128)(2,1)S(1)} %pad_maximum_fusion.own_ref, bf16[10240,128]{1,0:T(8,128)(2,1)} %bitcast.2.got_ref, ...), custom_call_target="tpu_custom_call" | custom-call | flops 3019898880 | bytes 51380224 | tf_op jit(solution)/shard_map/translate/pallas_call | solution.py:169
  123.8 1.3 collective-permute-start.10
  125.1 2.4 %collective-permute-start.9 = (bf16[352,512]{1,0:T(8,128)(2,1)S(1)}, bf16[352,512]{1,0:T(8,128)(2,1)S(1)}, u32[]{:S(2)}, u32[]{:S(2)}) collective-permute-start(bf16[352,512]{1,0:T(8,128)(2,1)S(1)} %get-tuple-element.32.own_ref), channel_id=1, source_target_pairs={{0,2},{1,3},{2,0},{3,1},{4,6},{5,7},{6,4},{7,5},{8,10},{9,11},{10,... | collective-permute-start | bytes 1081352 | tf_op jit(solution)/shard_map/ppermute | solution.py:286
  127.6 1.2 collective-permute-start.11
  128.7 12.9 %translate.3 = (bf16[144,512]{1,0:T(8,128)(2,1)S(1)}, f32[288,512]{1,0:T(8,128)S(1)}) custom-call(s32[32,1,1664]{2,1,0:T(1,128)S(1)} %broadcast_in_dim.81.idx_ref, s32[2]{0:T(128)S(1)} %pad_add_fusion.1.at_ref, bf16[1152,128]{1,0:T(8,128)(2,1)S(1)} %pad_maximum_fusion.own_ref, bf16[10240,128]{1,0:T(8,128)(2,1)} %bitcast.2.got_ref, ...), custom_call_target="tpu_custom_call" | custom-call | flops 1811939328 | bytes 28311552 | tf_op jit(solution)/shard_map/translate/pallas_call | solution.py:169
  141.6 0.0 collective-permute-done.10.b_ref
  141.6 0.4 collective-permute-done.9.a_ref
  142.0 0.9 collective-permute-start.12
  143.0 4.5 %collective-permute-start.13 = (bf16[32,512]{1,0:T(8,128)(2,1)S(1)}, bf16[32,512]{1,0:T(8,128)(2,1)S(1)}, u32[]{:S(2)}, u32[]{:S(2)}) collective-permute-start(bf16[32,512]{1,0:T(8,128)(2,1)S(1)} %get-tuple-element.43), channel_id=1, source_target_pairs={{0,4},{4,8},{8,12},{12,16},{16,20},{20,24},{24,28},{28,32},{32,36}... | collective-permute-start | bytes 98312 | tf_op jit(solution)/shard_map/ppermute | solution.py:363
  147.5 1.9 %collective-permute-start.14 = (bf16[32,512]{1,0:T(8,128)(2,1)S(1)}, bf16[32,512]{1,0:T(8,128)(2,1)S(1)}, u32[]{:S(2)}, u32[]{:S(2)}) collective-permute-start(bf16[32,512]{1,0:T(8,128)(2,1)S(1)} %get-tuple-element.44), channel_id=1, source_target_pairs={{4,0},{8,4},{12,8},{16,12},{20,16},{24,20},{28,24},{32,28},{36,32}... | collective-permute-start | bytes 98312 | tf_op jit(solution)/shard_map/ppermute | solution.py:364
  149.5 0.0 collective-permute-done.13.left_ref
  149.5 3.3 %collective-permute-done.14.right_ref = bf16[32,512]{1,0:T(8,128)(2,1)S(1)} collective-permute-done((bf16[32,512]{1,0:T(8,128)(2,1)S(1)}, bf16[32,512]{1,0:T(8,128)(2,1)S(1)}, u32[]{:S(2)}, u32[]{:S(2)}) %collective-permute-start.14) | collective-permute-done | bytes 32800 | tf_op jit(solution)/shard_map/ppermute | solution.py:364
  152.8 1.0 finish.1
  153.8 2.2 %collective-permute-start.15 = (bf16[256,512]{1,0:T(8,128)(2,1)S(1)}, bf16[256,512]{1,0:T(8,128)(2,1)S(1)}, u32[]{:S(2)}, u32[]{:S(2)}) collective-permute-start(bf16[256,512]{1,0:T(8,128)(2,1)S(1)} %finish.1), channel_id=1, source_target_pairs={{0,2},{1,3},{2,0},{3,1},{4,6},{5,7},{6,4},{7,5},{8,10},{9,11},{10,... | collective-permute-start | bytes 786440 | tf_op jit(solution)/shard_map/ppermute | solution.py:286
  155.9 0.0 collective-permute-start.16
  155.9 2.7 %collective-permute-start.17 = (bf16[256,512]{1,0:T(8,128)(2,1)S(1)}, bf16[256,512]{1,0:T(8,128)(2,1)S(1)}, u32[]{:S(2)}, u32[]{:S(2)}) collective-permute-start(bf16[256,512]{1,0:T(8,128)(2,1)S(1)} %finish.1), channel_id=1, source_target_pairs={{0,3},{1,0},{2,1},{3,2},{4,7},{5,4},{6,5},{7,6},{8,11},{9,8},{10,9... | collective-permute-start | bytes 786440 | tf_op jit(solution)/shard_map/ppermute | solution.py:286
  158.6 0.1 broadcast_in_dim.66
  158.7 4.8 %collective-permute-done.15 = bf16[256,512]{1,0:T(8,128)(2,1)S(1)} collective-permute-done((bf16[256,512]{1,0:T(8,128)(2,1)S(1)}, bf16[256,512]{1,0:T(8,128)(2,1)S(1)}, u32[]{:S(2)}, u32[]{:S(2)}) %collective-permute-start.15) | collective-permute-done | bytes 262176 | tf_op jit(solution)/shard_map/ppermute | solution.py:286
  163.5 4.0 %collective-permute-done.16 = bf16[256,512]{1,0:T(8,128)(2,1)S(1)} collective-permute-done((bf16[256,512]{1,0:T(8,128)(2,1)S(1)}, bf16[256,512]{1,0:T(8,128)(2,1)S(1)}, u32[]{:S(2)}, u32[]{:S(2)}) %collective-permute-start.16) | collective-permute-done | bytes 262176 | tf_op jit(solution)/shard_map/ppermute | solution.py:286
  167.6 0.0 copy-start.3
  167.6 0.9 copy-done.3
  168.5 0.7 constant_dynamic-update-slice_fusion.6
  (35 shorter events, 0.3 us)
Async XLA Ops:
  0.0 15.5 %copy-start = (bf16[1024,512]{1,0:T(8,128)(2,1)S(1)}, bf16[1024,512]{1,0:T(8,128)(2,1)}, u32[]{:S(2)}) copy-start(bf16[1024,512]{1,0:T(8,128)(2,1)} %param.9) | copy-start | bytes 3145732
  2.4 23.3 %all-to-all-start = ((s32[64,1,160]{2,1,0:T(1,128)}), s32[64,1,160]{2,1,0:T(1,128)S(1)}, u32[]{:S(2)}, u32[]{:S(2)}) async-start(s32[64,1,160]{2,1,0:T(1,128)} %compare_select_fusion.1), calls=%async_computation | async-start | bytes 131072 | tf_op jit(solution)/shard_map/all_to_all | solution.py:294
  16.4 24.0 %copy-start.5 = (s32[8,1024]{1,0:T(8,128)S(1)}, s32[8,1024]{1,0:T(8,128)}, u32[]{:S(2)}) copy-start(s32[8,1024]{1,0:T(8,128)} %param.11) | copy-start | bytes 98308
  16.4 24.1 %copy-start.7 = (s32[8,128]{1,0:T(8,128)S(1)}, s32[8,128]{1,0:T(8,128)}, u32[]{:S(2)}) copy-start(s32[8,128]{1,0:T(8,128)} %param.14) | copy-start | bytes 12292
  16.4 29.0 %copy-start.6 = (s32[1024]{0:T(1024)S(1)}, s32[1024]{0:T(1024)}, u32[]{:S(2)}) copy-start(s32[1024]{0:T(1024)} %param.17) | copy-start | bytes 12292
  33.5 1.5 copy-start.1
  35.1 66.8 %all-to-all-start.1 = ((bf16[64,160,128]{2,1,0:T(8,128)(2,1)}), bf16[64,160,128]{2,1,0:T(8,128)(2,1)}, u32[]{:S(2)}, u32[]{:S(2)}) async-start(bf16[64,160,128]{2,1,0:T(8,128)(2,1)} %copy-done.1), calls=%async_computation.1 | async-start | bytes 5242880 | tf_op jit(solution)/shard_map/all_to_all | solution.py:303
  40.5 5.2 %collective-permute-start = (s32[8,1152]{1,0:T(8,128)S(1)}, s32[8,1152]{1,0:T(8,128)S(1)}, u32[]{:S(2)}, u32[]{:S(2)}) collective-permute-start(s32[8,1152]{1,0:T(8,128)S(1)} %constant_dynamic-update-slice_fusion), channel_id=1, source_target_pairs={{0,1},{1,2},{2,3},{3,0},{4,5},{5,6},{6,7},{7,4},{8,9},{9,10},{10,1... | collective-permute-start | bytes 110600 | tf_op jit(solution)/shard_map/ppermute | solution.py:286
  41.8 4.3 %collective-permute-start.1 = (s32[8,1152]{1,0:T(8,128)S(1)}, s32[8,1152]{1,0:T(8,128)S(1)}, u32[]{:S(2)}, u32[]{:S(2)}) collective-permute-start(s32[8,1152]{1,0:T(8,128)S(1)} %constant_dynamic-update-slice_fusion), channel_id=1, source_target_pairs={{0,2},{1,3},{2,0},{3,1},{4,6},{5,7},{6,4},{7,5},{8,10},{9,11},{10,... | collective-permute-start | bytes 110600 | tf_op jit(solution)/shard_map/ppermute | solution.py:286
  44.2 3.2 %collective-permute-start.2 = (s32[8,1152]{1,0:T(8,128)S(1)}, s32[8,1152]{1,0:T(8,128)S(1)}, u32[]{:S(2)}, u32[]{:S(2)}) collective-permute-start(s32[8,1152]{1,0:T(8,128)S(1)} %constant_dynamic-update-slice_fusion), channel_id=1, source_target_pairs={{0,3},{1,0},{2,1},{3,2},{4,7},{5,4},{6,5},{7,6},{8,11},{9,8},{10,9... | collective-permute-start | bytes 110600 | tf_op jit(solution)/shard_map/ppermute | solution.py:286
  50.0 13.3 %collective-permute-start.3 = (bf16[4,128,512]{2,1,0:T(8,128)(2,1)}, bf16[4,128,512]{2,1,0:T(8,128)(2,1)S(1)}, u32[]{:S(2)}, u32[]{:S(2)}) collective-permute-start(bf16[4,128,512]{2,1,0:T(8,128)(2,1)} %get-tuple-element.47), channel_id=1, source_target_pairs={{0,1},{1,2},{2,3},{3,0},{4,5},{5,6},{6,7},{7,4},{8,9},{9,10},{10,1... | collective-permute-start | bytes 1572872 | tf_op jit(solution)/shard_map/ppermute | solution.py:286
  50.3 24.7 %collective-permute-start.5 = (bf16[4,128,512]{2,1,0:T(8,128)(2,1)}, bf16[4,128,512]{2,1,0:T(8,128)(2,1)S(1)}, u32[]{:S(2)}, u32[]{:S(2)}) collective-permute-start(bf16[4,128,512]{2,1,0:T(8,128)(2,1)} %get-tuple-element.46), channel_id=1, source_target_pairs={{0,2},{1,3},{2,0},{3,1},{4,6},{5,7},{6,4},{7,5},{8,10},{9,11},{10,... | collective-permute-start | bytes 1572872 | tf_op jit(solution)/shard_map/ppermute | solution.py:286
  53.5 24.3 %collective-permute-start.7 = (bf16[4,128,512]{2,1,0:T(8,128)(2,1)}, bf16[4,128,512]{2,1,0:T(8,128)(2,1)S(1)}, u32[]{:S(2)}, u32[]{:S(2)}) collective-permute-start(bf16[4,128,512]{2,1,0:T(8,128)(2,1)} %get-tuple-element.45), channel_id=1, source_target_pairs={{0,3},{1,0},{2,1},{3,2},{4,7},{5,4},{6,5},{7,6},{8,11},{9,8},{10,9... | collective-permute-start | bytes 1572872 | tf_op jit(solution)/shard_map/ppermute | solution.py:286
  53.6 0.7 copy-start.4
  63.3 38.6 %collective-permute-start.4 = (bf16[4,128,512]{2,1,0:T(8,128)(2,1)S(1)}, bf16[4,128,512]{2,1,0:T(8,128)(2,1)}, u32[]{:S(2)}, u32[]{:S(2)}) collective-permute-start(bf16[4,128,512]{2,1,0:T(8,128)(2,1)S(1)} %collective-permute-done.3.refs_0_), channel_id=1, source_target_pairs={{0,4},{4,0},{8,12},{12,8},{16,20},{20,16},{24,28},{28,24},{32,36},... | collective-permute-start | bytes 1572872 | tf_op jit(solution)/shard_map/ppermute | solution.py:289
  75.0 26.9 %collective-permute-start.6 = (bf16[4,128,512]{2,1,0:T(8,128)(2,1)S(1)}, bf16[4,128,512]{2,1,0:T(8,128)(2,1)}, u32[]{:S(2)}, u32[]{:S(2)}) collective-permute-start(bf16[4,128,512]{2,1,0:T(8,128)(2,1)S(1)} %collective-permute-done.5.refs_2_), channel_id=1, source_target_pairs={{0,4},{4,0},{8,12},{12,8},{16,20},{20,16},{24,28},{28,24},{32,36},... | collective-permute-start | bytes 1572872 | tf_op jit(solution)/shard_map/ppermute | solution.py:289
  77.9 24.0 %collective-permute-start.8 = (bf16[4,128,512]{2,1,0:T(8,128)(2,1)S(1)}, bf16[4,128,512]{2,1,0:T(8,128)(2,1)}, u32[]{:S(2)}, u32[]{:S(2)}) collective-permute-start(bf16[4,128,512]{2,1,0:T(8,128)(2,1)S(1)} %collective-permute-done.7.refs_4_), channel_id=1, source_target_pairs={{0,4},{4,0},{8,12},{12,8},{16,20},{20,16},{24,28},{28,24},{32,36},... | collective-permute-start | bytes 1572872 | tf_op jit(solution)/shard_map/ppermute | solution.py:289
  123.8 17.8 %collective-permute-start.10 = (bf16[352,512]{1,0:T(8,128)(2,1)S(1)}, bf16[352,512]{1,0:T(8,128)(2,1)S(1)}, u32[]{:S(2)}, u32[]{:S(2)}) collective-permute-start(bf16[352,512]{1,0:T(8,128)(2,1)S(1)} %get-tuple-element.33), channel_id=1, source_target_pairs={{0,1},{1,2},{2,3},{3,0},{4,5},{5,6},{6,7},{7,4},{8,9},{9,10},{10,1... | collective-permute-start | bytes 1081352 | tf_op jit(solution)/shard_map/ppermute | solution.py:286
  125.1 16.9 %collective-permute-start.9 = (bf16[352,512]{1,0:T(8,128)(2,1)S(1)}, bf16[352,512]{1,0:T(8,128)(2,1)S(1)}, u32[]{:S(2)}, u32[]{:S(2)}) collective-permute-start(bf16[352,512]{1,0:T(8,128)(2,1)S(1)} %get-tuple-element.32.own_ref), channel_id=1, source_target_pairs={{0,2},{1,3},{2,0},{3,1},{4,6},{5,7},{6,4},{7,5},{8,10},{9,11},{10,... | collective-permute-start | bytes 1081352 | tf_op jit(solution)/shard_map/ppermute | solution.py:286
  127.6 25.2 %copy-start.2 = (bf16[8,512,512]{2,1,0:T(8,128)(2,1)S(1)}, bf16[8,512,512]{2,1,0:T(8,128)(2,1)}, u32[]{:S(2)}) copy-start(bf16[8,512,512]{2,1,0:T(8,128)(2,1)} %l2l_ref.1) | copy-start | bytes 12582916
  127.6 14.0 %collective-permute-start.11 = (bf16[208,512]{1,0:T(8,128)(2,1)S(1)}, bf16[208,512]{1,0:T(8,128)(2,1)S(1)}, u32[]{:S(2)}, u32[]{:S(2)}) collective-permute-start(bf16[208,512]{1,0:T(8,128)(2,1)S(1)} %get-tuple-element.34), channel_id=1, source_target_pairs={{0,3},{1,0},{2,1},{3,2},{4,7},{5,4},{6,5},{7,6},{8,11},{9,8},{10,9... | collective-permute-start | bytes 638984 | tf_op jit(solution)/shard_map/ppermute | solution.py:286
  142.0 10.7 %collective-permute-start.12 = (bf16[144,512]{1,0:T(8,128)(2,1)S(1)}, bf16[144,512]{1,0:T(8,128)(2,1)S(1)}, u32[]{:S(2)}, u32[]{:S(2)}) collective-permute-start(bf16[144,512]{1,0:T(8,128)(2,1)S(1)} %get-tuple-element.41), channel_id=1, source_target_pairs={{0,3},{1,0},{2,1},{3,2},{4,7},{5,4},{6,5},{7,6},{8,11},{9,8},{10,9... | collective-permute-start | bytes 442376 | tf_op jit(solution)/shard_map/ppermute | solution.py:286
  143.0 6.4 %collective-permute-start.13 = (bf16[32,512]{1,0:T(8,128)(2,1)S(1)}, bf16[32,512]{1,0:T(8,128)(2,1)S(1)}, u32[]{:S(2)}, u32[]{:S(2)}) collective-permute-start(bf16[32,512]{1,0:T(8,128)(2,1)S(1)} %get-tuple-element.43), channel_id=1, source_target_pairs={{0,4},{4,8},{8,12},{12,16},{16,20},{20,24},{24,28},{28,32},{32,36}... | collective-permute-start | bytes 98312 | tf_op jit(solution)/shard_map/ppermute | solution.py:363
  147.5 5.2 %collective-permute-start.14 = (bf16[32,512]{1,0:T(8,128)(2,1)S(1)}, bf16[32,512]{1,0:T(8,128)(2,1)S(1)}, u32[]{:S(2)}, u32[]{:S(2)}) collective-permute-start(bf16[32,512]{1,0:T(8,128)(2,1)S(1)} %get-tuple-element.44), channel_id=1, source_target_pairs={{4,0},{8,4},{12,8},{16,12},{20,16},{24,20},{28,24},{32,28},{36,32}... | collective-permute-start | bytes 98312 | tf_op jit(solution)/shard_map/ppermute | solution.py:364
  153.8 9.7 %collective-permute-start.15 = (bf16[256,512]{1,0:T(8,128)(2,1)S(1)}, bf16[256,512]{1,0:T(8,128)(2,1)S(1)}, u32[]{:S(2)}, u32[]{:S(2)}) collective-permute-start(bf16[256,512]{1,0:T(8,128)(2,1)S(1)} %finish.1), channel_id=1, source_target_pairs={{0,2},{1,3},{2,0},{3,1},{4,6},{5,7},{6,4},{7,5},{8,10},{9,11},{10,... | collective-permute-start | bytes 786440 | tf_op jit(solution)/shard_map/ppermute | solution.py:286
  155.9 11.6 %collective-permute-start.16 = (bf16[256,512]{1,0:T(8,128)(2,1)S(1)}, bf16[256,512]{1,0:T(8,128)(2,1)S(1)}, u32[]{:S(2)}, u32[]{:S(2)}) collective-permute-start(bf16[256,512]{1,0:T(8,128)(2,1)S(1)} %finish.1), channel_id=1, source_target_pairs={{0,1},{1,2},{2,3},{3,0},{4,5},{5,6},{6,7},{7,4},{8,9},{9,10},{10,1... | collective-permute-start | bytes 786440 | tf_op jit(solution)/shard_map/ppermute | solution.py:286
  155.9 11.6 %collective-permute-start.17 = (bf16[256,512]{1,0:T(8,128)(2,1)S(1)}, bf16[256,512]{1,0:T(8,128)(2,1)S(1)}, u32[]{:S(2)}, u32[]{:S(2)}) collective-permute-start(bf16[256,512]{1,0:T(8,128)(2,1)S(1)} %finish.1), channel_id=1, source_target_pairs={{0,3},{1,0},{2,1},{3,2},{4,7},{5,4},{6,5},{7,6},{8,11},{9,8},{10,9... | collective-permute-start | bytes 786440 | tf_op jit(solution)/shard_map/ppermute | solution.py:286
  167.6 1.0 copy-start.3

commit v6 on v5

--- a/solution.py
+++ b/solution.py
@@ -362,6 +362,7 @@
     head, tail = edges([away[0]] + others, 2 * R)
     from_left = lax.ppermute(tail, "box", [(i, i + 1) for i in range(blocks - 1)])
     from_right = lax.ppermute(head, "box", [(i + 1, i) for i in range(blocks - 1)])
+    late, from_left = lax.optimization_barrier((late, from_left))
     others = others + [shifted(late, 3)]
     done = finish(mine, others, place, from_left, from_right, l2l_ops)
     out = jnp.zeros((rows_f, coefficients), jnp.bfloat16)

time: 170 us -> 173 us (1.018)
  waiting for transfers between devices: 52.8 us -> 55.1 us
  transfers between devices with their start and end apart: 20 -> 20, of which waited for: 9 -> 10; matrix products, arithmetic and copies ran while one was open for 9% -> 9% of each run, Pallas kernels for 8% -> 8%
where the time goes in v6:
time: 173 us; the launch traced here: 171 us
  waiting for transfers between devices  55.1 us (32%)
  starting transfers between devices  50.7 us (29%)
  Pallas kernels  43.7 us (25%)
  local copies, waits for them, and re-layouts  14.8 us (9%)
  other arithmetic  6.51 us (4%)
    pallas_call x2, Pallas kernels, translate(): pl.pallas_call(functools.partial(translate_kernel, jobs, halo), out_shape...  34.8 us
    all_to_all x1, waiting for transfers between devices, per_device(): got = lax.all_to_all(sent, 'box', split_axis=0, concat_axis=0, tiled=True)  21.7 us
    ppermute x13, waiting for transfers between devices, shifted(): lax.ppermute(value, 'grp', [(i, (i + by) % members) for i in range(member...  19.1 us
    ppermute x13, starting transfers between devices, shifted(): lax.ppermute(value, 'grp', [(i, (i + by) % members) for i in range(member...  18.2 us
    all_to_all x1, starting transfers between devices, per_device(): lax.all_to_all(requests, 'box', split_axis=0, concat_axis=0, tiled=True)  13.2 us
    all_to_all x1, waiting for transfers between devices, per_device(): lax.all_to_all(requests, 'box', split_axis=0, concat_axis=0, tiled=True)  9.19 us
    pallas_call x1, Pallas kernels, pick(): pl.pallas_call(pick_kernel, out_shape=jax.ShapeDtypeStruct((parts, length...  7.93 us
    ppermute x3, starting transfers between devices, swapped(): return lax.ppermute(value, 'box', [(i, i ^ 1) for i in range(blocks)])  6.94 us
  transfers between devices with their start and end apart: 20, of which 10 were waited for; matrix products, arithmetic and copies ran while one was open for 9% of the time, Pallas kernels for 8%

profile of v6, /device:TPU:1, one launch (start us, length us, event | category | flops | bytes accessed | tf_op | source)
XLA Modules:
  0.0 171.2 jit_solution(6823267075733977837)
XLA Ops:
  0.0 0.9 copy.10
  0.9 1.5 compare_select_fusion.1
  2.4 13.2 %all-to-all-start = ((s32[64,1,160]{2,1,0:T(1,128)}), s32[64,1,160]{2,1,0:T(1,128)S(1)}, u32[]{:S(2)}, u32[]{:S(2)}) async-start(s32[64,1,160]{2,1,0:T(1,128)} %compare_select_fusion.1), calls=%async_computation | async-start | bytes 131072 | tf_op jit(solution)/shard_map/all_to_all | solution.py:294
  15.6 0.8 constant_dynamic-slice_fusion.3
  16.4 0.0 copy-start.5
  16.4 0.0 copy-start.7
  16.4 0.0 copy-start.6
  16.4 9.2 %all-to-all-done.wanted_ref = s32[64,1,160]{2,1,0:T(1,128)S(1)} async-done(((s32[64,1,160]{2,1,0:T(1,128)}), s32[64,1,160]{2,1,0:T(1,128)S(1)}, u32[]{:S(2)}, u32[]{:S(2)}) %all-to-all-start) | async-done | bytes 40992 | tf_op jit(solution)/shard_map/all_to_all | solution.py:294
  25.6 7.9 %pick.1 = bf16[64,160,128]{2,1,0:T(8,128)(2,1)S(1)} custom-call(s32[64,1,160]{2,1,0:T(1,128)S(1)} %all-to-all-done.wanted_ref, bf16[1152,128]{1,0:T(8,128)(2,1)S(1)} %pad_maximum_fusion.own_ref), custom_call_target="tpu_custom_call" | custom-call | bytes 20971520 | tf_op jit(solution)/shard_map/pick/pallas_call | solution.py:60
  33.6 1.5 copy-done.1
  35.1 5.3 %all-to-all-start.1 = ((bf16[64,160,128]{2,1,0:T(8,128)(2,1)}), bf16[64,160,128]{2,1,0:T(8,128)(2,1)}, u32[]{:S(2)}, u32[]{:S(2)}) async-start(bf16[64,160,128]{2,1,0:T(8,128)(2,1)} %copy-done.1), calls=%async_computation.1 | async-start | bytes 5242880 | tf_op jit(solution)/shard_map/all_to_all | solution.py:303
  40.5 1.3 collective-permute-start
  41.8 2.5 %collective-permute-start.1 = (s32[8,1152]{1,0:T(8,128)S(1)}, s32[8,1152]{1,0:T(8,128)S(1)}, u32[]{:S(2)}, u32[]{:S(2)}) collective-permute-start(s32[8,1152]{1,0:T(8,128)S(1)} %constant_dynamic-update-slice_fusion), channel_id=1, source_target_pairs={{0,2},{1,3},{2,0},{3,1},{4,6},{5,7},{6,4},{7,5},{8,10},{9,11},{10,... | collective-permute-start | bytes 110600 | tf_op jit(solution)/shard_map/ppermute | solution.py:286
  44.2 1.2 collective-permute-start.2
  45.4 0.1 pad_add_fusion.1.at_ref
  45.5 0.1 pad.4.clone
  45.6 0.1 dynamic_slice.20
  45.6 0.0 collective-permute-done
  45.6 0.4 collective-permute-done.1
  46.1 1.3 collective-permute-done.2
  47.4 2.6 %constant_dynamic-slice_fusion = (bf16[4,128,512]{2,1,0:T(8,128)(2,1)}, bf16[4,128,512]{2,1,0:T(8,128)(2,1)}, bf16[4,128,512]{2,1,0:T(8,128)(2,1)}) fusion(bf16[8,512,512]{2,1,0:T(8,128)(2,1)} %ops_ref.3, s32[]{:T(128)S(6)} %select_n.174, s32[]{:T(128)S(6)} %select_n.180, s32[]{:T(128)S(6)} %select_n.178, s32[]{:T(128)S(6)} %select_n.176), kind=kLoop, calls=%fused_computation.51 | loop fusion | bytes 3145744 | tf_op jit(solution)/shard_map/dynamic_slice | solution.py:315
  50.0 0.3 collective-permute-start.3
  50.3 3.3 %collective-permute-start.5 = (bf16[4,128,512]{2,1,0:T(8,128)(2,1)}, bf16[4,128,512]{2,1,0:T(8,128)(2,1)S(1)}, u32[]{:S(2)}, u32[]{:S(2)}) collective-permute-start(bf16[4,128,512]{2,1,0:T(8,128)(2,1)} %get-tuple-element.50), channel_id=1, source_target_pairs={{0,2},{1,3},{2,0},{3,1},{4,6},{5,7},{6,4},{7,5},{8,10},{9,11},{10,... | collective-permute-start | bytes 1572872 | tf_op jit(solution)/shard_map/ppermute | solution.py:286
  53.5 0.0 collective-permute-start.7
  53.6 0.6 copy-done.4
  54.3 0.8 fusion.19
  55.1 1.1 copy.11
  56.2 4.0 %gather_fusion = s32[1024,32]{1,0:T(8,128)} fusion(s32[1024,32]{1,0:T(8,128)S(1)} %copy.11, s32[1024]{0:T(1024)S(1)} %get-tuple-element.56), kind=kCustom, calls=%fused_computation | custom fusion | bytes 266240 | tf_op jit(solution)/shard_map/jit(_take)/gather | solution.py:328
  60.2 1.4 select_select_fusion
  61.6 0.8 copy.12
  62.4 0.7 fusion.12
  63.2 0.1 reshape.108
  63.3 0.0 collective-permute-done.3.refs_0_
  63.3 4.1 %collective-permute-start.4 = (bf16[4,128,512]{2,1,0:T(8,128)(2,1)S(1)}, bf16[4,128,512]{2,1,0:T(8,128)(2,1)}, u32[]{:S(2)}, u32[]{:S(2)}) collective-permute-start(bf16[4,128,512]{2,1,0:T(8,128)(2,1)S(1)} %collective-permute-done.3.refs_0_), channel_id=1, source_target_pairs={{0,4},{4,0},{8,12},{12,8},{16,20},{20,16},{24,28},{28,24},{32,36},... | collective-permute-start | bytes 1572872 | tf_op jit(solution)/shard_map/ppermute | solution.py:289
  67.4 7.7 %collective-permute-done.5.refs_2_ = bf16[4,128,512]{2,1,0:T(8,128)(2,1)S(1)} collective-permute-done((bf16[4,128,512]{2,1,0:T(8,128)(2,1)}, bf16[4,128,512]{2,1,0:T(8,128)(2,1)S(1)}, u32[]{:S(2)}, u32[]{:S(2)}) %collective-permute-start.5) | collective-permute-done | bytes 524320 | tf_op jit(solution)/shard_map/ppermute | solution.py:286
  75.0 2.9 %collective-permute-start.6 = (bf16[4,128,512]{2,1,0:T(8,128)(2,1)S(1)}, bf16[4,128,512]{2,1,0:T(8,128)(2,1)}, u32[]{:S(2)}, u32[]{:S(2)}) collective-permute-start(bf16[4,128,512]{2,1,0:T(8,128)(2,1)S(1)} %collective-permute-done.5.refs_2_), channel_id=1, source_target_pairs={{0,4},{4,0},{8,12},{12,8},{16,20},{20,16},{24,28},{28,24},{32,36},... | collective-permute-start | bytes 1572872 | tf_op jit(solution)/shard_map/ppermute | solution.py:289
  77.9 0.0 collective-permute-start.8
  77.9 0.9 add_add_fusion
  78.8 1.1 fusion.3
  79.9 0.1 fusion.18
  80.0 0.1 concatenate.42
  80.1 0.1 broadcast_in_dim.81.idx_ref
  80.2 21.7 %all-to-all-done.1 = bf16[64,160,128]{2,1,0:T(8,128)(2,1)} async-done(((bf16[64,160,128]{2,1,0:T(8,128)(2,1)}), bf16[64,160,128]{2,1,0:T(8,128)(2,1)}, u32[]{:S(2)}, u32[]{:S(2)}) %all-to-all-start.1) | async-done | bytes 2621472 | tf_op jit(solution)/shard_map/all_to_all | solution.py:303
  101.9 0.0 collective-permute-done.4.refs_1_
  101.9 0.0 collective-permute-done.6.refs_3_
  101.9 21.9 %translate.2 = (bf16[352,512]{1,0:T(8,128)(2,1)S(1)}, bf16[352,512]{1,0:T(8,128)(2,1)S(1)}, bf16[208,512]{1,0:T(8,128)(2,1)S(1)}) custom-call(s32[32,1,1664]{2,1,0:T(1,128)S(1)} %broadcast_in_dim.81.idx_ref, s32[2]{0:T(128)S(1)} %pad_add_fusion.1.at_ref, bf16[1152,128]{1,0:T(8,128)(2,1)S(1)} %pad_maximum_fusion.own_ref, bf16[10240,128]{1,0:T(8,128)(2,1)} %bitcast.2.got_ref, ...), custom_call_target="tpu_custom_call" | custom-call | flops 3019898880 | bytes 51380224 | tf_op jit(solution)/shard_map/translate/pallas_call | solution.py:169
  123.8 1.3 collective-permute-start.10
  125.1 2.5 %collective-permute-start.9 = (bf16[352,512]{1,0:T(8,128)(2,1)S(1)}, bf16[352,512]{1,0:T(8,128)(2,1)S(1)}, u32[]{:S(2)}, u32[]{:S(2)}) collective-permute-start(bf16[352,512]{1,0:T(8,128)(2,1)S(1)} %get-tuple-element.34.own_ref), channel_id=1, source_target_pairs={{0,2},{1,3},{2,0},{3,1},{4,6},{5,7},{6,4},{7,5},{8,10},{9,11},{10,... | collective-permute-start | bytes 1081352 | tf_op jit(solution)/shard_map/ppermute | solution.py:286
  127.6 1.2 collective-permute-start.11
  128.7 12.9 %translate.3 = (bf16[144,512]{1,0:T(8,128)(2,1)S(1)}, f32[288,512]{1,0:T(8,128)S(1)}) custom-call(s32[32,1,1664]{2,1,0:T(1,128)S(1)} %broadcast_in_dim.81.idx_ref, s32[2]{0:T(128)S(1)} %pad_add_fusion.1.at_ref, bf16[1152,128]{1,0:T(8,128)(2,1)S(1)} %pad_maximum_fusion.own_ref, bf16[10240,128]{1,0:T(8,128)(2,1)} %bitcast.2.got_ref, ...), custom_call_target="tpu_custom_call" | custom-call | flops 1811939328 | bytes 28311552 | tf_op jit(solution)/shard_map/translate/pallas_call | solution.py:169
  141.6 0.4 collective-permute-done.9.a_ref
  142.1 5.2 %collective-permute-start.12 = (bf16[32,512]{1,0:T(8,128)(2,1)S(1)}, bf16[32,512]{1,0:T(8,128)(2,1)S(1)}, u32[]{:S(2)}, u32[]{:S(2)}) collective-permute-start(bf16[32,512]{1,0:T(8,128)(2,1)S(1)} %get-tuple-element.44), channel_id=1, source_target_pairs={{0,4},{4,8},{8,12},{12,16},{16,20},{20,24},{24,28},{28,32},{32,36}... | collective-permute-start | bytes 98312 | tf_op jit(solution)/shard_map/ppermute | solution.py:363
  147.2 1.0 collective-permute-done.12.left_ref
  148.2 1.9 %collective-permute-start.14 = (bf16[32,512]{1,0:T(8,128)(2,1)S(1)}, bf16[32,512]{1,0:T(8,128)(2,1)S(1)}, u32[]{:S(2)}, u32[]{:S(2)}) collective-permute-start(bf16[32,512]{1,0:T(8,128)(2,1)S(1)} %get-tuple-element.48), channel_id=1, source_target_pairs={{4,0},{8,4},{12,8},{16,12},{20,16},{24,20},{28,24},{32,28},{36,32}... | collective-permute-start | bytes 98312 | tf_op jit(solution)/shard_map/ppermute | solution.py:364
  150.2 4.1 %collective-permute-done.14.right_ref = bf16[32,512]{1,0:T(8,128)(2,1)S(1)} collective-permute-done((bf16[32,512]{1,0:T(8,128)(2,1)S(1)}, bf16[32,512]{1,0:T(8,128)(2,1)S(1)}, u32[]{:S(2)}, u32[]{:S(2)}) %collective-permute-start.14) | collective-permute-done | bytes 32800 | tf_op jit(solution)/shard_map/ppermute | solution.py:364
  154.3 1.0 finish.1
  155.3 2.2 %collective-permute-start.15 = (bf16[256,512]{1,0:T(8,128)(2,1)S(1)}, bf16[256,512]{1,0:T(8,128)(2,1)S(1)}, u32[]{:S(2)}, u32[]{:S(2)}) collective-permute-start(bf16[256,512]{1,0:T(8,128)(2,1)S(1)} %finish.1), channel_id=1, source_target_pairs={{0,2},{1,3},{2,0},{3,1},{4,6},{5,7},{6,4},{7,5},{8,10},{9,11},{10,... | collective-permute-start | bytes 786440 | tf_op jit(solution)/shard_map/ppermute | solution.py:286
  157.4 2.7 %collective-permute-start.17 = (bf16[256,512]{1,0:T(8,128)(2,1)S(1)}, bf16[256,512]{1,0:T(8,128)(2,1)S(1)}, u32[]{:S(2)}, u32[]{:S(2)}) collective-permute-start(bf16[256,512]{1,0:T(8,128)(2,1)S(1)} %finish.1), channel_id=1, source_target_pairs={{0,3},{1,0},{2,1},{3,2},{4,7},{5,4},{6,5},{7,6},{8,11},{9,8},{10,9... | collective-permute-start | bytes 786440 | tf_op jit(solution)/shard_map/ppermute | solution.py:286
  160.1 0.1 broadcast_in_dim.66
  160.2 4.8 %collective-permute-done.15 = bf16[256,512]{1,0:T(8,128)(2,1)S(1)} collective-permute-done((bf16[256,512]{1,0:T(8,128)(2,1)S(1)}, bf16[256,512]{1,0:T(8,128)(2,1)S(1)}, u32[]{:S(2)}, u32[]{:S(2)}) %collective-permute-start.15) | collective-permute-done | bytes 262176 | tf_op jit(solution)/shard_map/ppermute | solution.py:286
  165.0 4.5 %collective-permute-done.16 = bf16[256,512]{1,0:T(8,128)(2,1)S(1)} collective-permute-done((bf16[256,512]{1,0:T(8,128)(2,1)S(1)}, bf16[256,512]{1,0:T(8,128)(2,1)S(1)}, u32[]{:S(2)}, u32[]{:S(2)}) %collective-permute-start.16) | collective-permute-done | bytes 262176 | tf_op jit(solution)/shard_map/ppermute | solution.py:286
  169.5 0.0 copy-start.3
  169.5 0.9 copy-done.3
  170.5 0.7 constant_dynamic-update-slice_fusion.6
  (35 shorter events, 0.3 us)
Async XLA Ops:
  0.0 15.5 %copy-start = (bf16[1024,512]{1,0:T(8,128)(2,1)S(1)}, bf16[1024,512]{1,0:T(8,128)(2,1)}, u32[]{:S(2)}) copy-start(bf16[1024,512]{1,0:T(8,128)(2,1)} %param.9) | copy-start | bytes 3145732
  2.4 23.3 %all-to-all-start = ((s32[64,1,160]{2,1,0:T(1,128)}), s32[64,1,160]{2,1,0:T(1,128)S(1)}, u32[]{:S(2)}, u32[]{:S(2)}) async-start(s32[64,1,160]{2,1,0:T(1,128)} %compare_select_fusion.1), calls=%async_computation | async-start | bytes 131072 | tf_op jit(solution)/shard_map/all_to_all | solution.py:294
  16.4 24.0 %copy-start.5 = (s32[8,1024]{1,0:T(8,128)S(1)}, s32[8,1024]{1,0:T(8,128)}, u32[]{:S(2)}) copy-start(s32[8,1024]{1,0:T(8,128)} %param.11) | copy-start | bytes 98308
  16.4 24.1 %copy-start.7 = (s32[8,128]{1,0:T(8,128)S(1)}, s32[8,128]{1,0:T(8,128)}, u32[]{:S(2)}) copy-start(s32[8,128]{1,0:T(8,128)} %param.14) | copy-start | bytes 12292
  16.4 29.0 %copy-start.6 = (s32[1024]{0:T(1024)S(1)}, s32[1024]{0:T(1024)}, u32[]{:S(2)}) copy-start(s32[1024]{0:T(1024)} %param.17) | copy-start | bytes 12292
  33.5 1.5 copy-start.1
  35.1 66.8 %all-to-all-start.1 = ((bf16[64,160,128]{2,1,0:T(8,128)(2,1)}), bf16[64,160,128]{2,1,0:T(8,128)(2,1)}, u32[]{:S(2)}, u32[]{:S(2)}) async-start(bf16[64,160,128]{2,1,0:T(8,128)(2,1)} %copy-done.1), calls=%async_computation.1 | async-start | bytes 5242880 | tf_op jit(solution)/shard_map/all_to_all | solution.py:303
  40.5 5.2 %collective-permute-start = (s32[8,1152]{1,0:T(8,128)S(1)}, s32[8,1152]{1,0:T(8,128)S(1)}, u32[]{:S(2)}, u32[]{:S(2)}) collective-permute-start(s32[8,1152]{1,0:T(8,128)S(1)} %constant_dynamic-update-slice_fusion), channel_id=1, source_target_pairs={{0,1},{1,2},{2,3},{3,0},{4,5},{5,6},{6,7},{7,4},{8,9},{9,10},{10,1... | collective-permute-start | bytes 110600 | tf_op jit(solution)/shard_map/ppermute | solution.py:286
  41.8 4.3 %collective-permute-start.1 = (s32[8,1152]{1,0:T(8,128)S(1)}, s32[8,1152]{1,0:T(8,128)S(1)}, u32[]{:S(2)}, u32[]{:S(2)}) collective-permute-start(s32[8,1152]{1,0:T(8,128)S(1)} %constant_dynamic-update-slice_fusion), channel_id=1, source_target_pairs={{0,2},{1,3},{2,0},{3,1},{4,6},{5,7},{6,4},{7,5},{8,10},{9,11},{10,... | collective-permute-start | bytes 110600 | tf_op jit(solution)/shard_map/ppermute | solution.py:286
  44.2 3.2 %collective-permute-start.2 = (s32[8,1152]{1,0:T(8,128)S(1)}, s32[8,1152]{1,0:T(8,128)S(1)}, u32[]{:S(2)}, u32[]{:S(2)}) collective-permute-start(s32[8,1152]{1,0:T(8,128)S(1)} %constant_dynamic-update-slice_fusion), channel_id=1, source_target_pairs={{0,3},{1,0},{2,1},{3,2},{4,7},{5,4},{6,5},{7,6},{8,11},{9,8},{10,9... | collective-permute-start | bytes 110600 | tf_op jit(solution)/shard_map/ppermute | solution.py:286
  50.0 13.3 %collective-permute-start.3 = (bf16[4,128,512]{2,1,0:T(8,128)(2,1)}, bf16[4,128,512]{2,1,0:T(8,128)(2,1)S(1)}, u32[]{:S(2)}, u32[]{:S(2)}) collective-permute-start(bf16[4,128,512]{2,1,0:T(8,128)(2,1)} %get-tuple-element.51), channel_id=1, source_target_pairs={{0,1},{1,2},{2,3},{3,0},{4,5},{5,6},{6,7},{7,4},{8,9},{9,10},{10,1... | collective-permute-start | bytes 1572872 | tf_op jit(solution)/shard_map/ppermute | solution.py:286
  50.3 24.7 %collective-permute-start.5 = (bf16[4,128,512]{2,1,0:T(8,128)(2,1)}, bf16[4,128,512]{2,1,0:T(8,128)(2,1)S(1)}, u32[]{:S(2)}, u32[]{:S(2)}) collective-permute-start(bf16[4,128,512]{2,1,0:T(8,128)(2,1)} %get-tuple-element.50), channel_id=1, source_target_pairs={{0,2},{1,3},{2,0},{3,1},{4,6},{5,7},{6,4},{7,5},{8,10},{9,11},{10,... | collective-permute-start | bytes 1572872 | tf_op jit(solution)/shard_map/ppermute | solution.py:286
  53.5 24.3 %collective-permute-start.7 = (bf16[4,128,512]{2,1,0:T(8,128)(2,1)}, bf16[4,128,512]{2,1,0:T(8,128)(2,1)S(1)}, u32[]{:S(2)}, u32[]{:S(2)}) collective-permute-start(bf16[4,128,512]{2,1,0:T(8,128)(2,1)} %get-tuple-element.49), channel_id=1, source_target_pairs={{0,3},{1,0},{2,1},{3,2},{4,7},{5,4},{6,5},{7,6},{8,11},{9,8},{10,9... | collective-permute-start | bytes 1572872 | tf_op jit(solution)/shard_map/ppermute | solution.py:286
  53.6 0.7 copy-start.4
  63.3 38.6 %collective-permute-start.4 = (bf16[4,128,512]{2,1,0:T(8,128)(2,1)S(1)}, bf16[4,128,512]{2,1,0:T(8,128)(2,1)}, u32[]{:S(2)}, u32[]{:S(2)}) collective-permute-start(bf16[4,128,512]{2,1,0:T(8,128)(2,1)S(1)} %collective-permute-done.3.refs_0_), channel_id=1, source_target_pairs={{0,4},{4,0},{8,12},{12,8},{16,20},{20,16},{24,28},{28,24},{32,36},... | collective-permute-start | bytes 1572872 | tf_op jit(solution)/shard_map/ppermute | solution.py:289
  75.0 26.9 %collective-permute-start.6 = (bf16[4,128,512]{2,1,0:T(8,128)(2,1)S(1)}, bf16[4,128,512]{2,1,0:T(8,128)(2,1)}, u32[]{:S(2)}, u32[]{:S(2)}) collective-permute-start(bf16[4,128,512]{2,1,0:T(8,128)(2,1)S(1)} %collective-permute-done.5.refs_2_), channel_id=1, source_target_pairs={{0,4},{4,0},{8,12},{12,8},{16,20},{20,16},{24,28},{28,24},{32,36},... | collective-permute-start | bytes 1572872 | tf_op jit(solution)/shard_map/ppermute | solution.py:289
  77.9 24.0 %collective-permute-start.8 = (bf16[4,128,512]{2,1,0:T(8,128)(2,1)S(1)}, bf16[4,128,512]{2,1,0:T(8,128)(2,1)}, u32[]{:S(2)}, u32[]{:S(2)}) collective-permute-start(bf16[4,128,512]{2,1,0:T(8,128)(2,1)S(1)} %collective-permute-done.7.refs_4_), channel_id=1, source_target_pairs={{0,4},{4,0},{8,12},{12,8},{16,20},{20,16},{24,28},{28,24},{32,36},... | collective-permute-start | bytes 1572872 | tf_op jit(solution)/shard_map/ppermute | solution.py:289
  123.8 17.8 %collective-permute-start.10 = (bf16[352,512]{1,0:T(8,128)(2,1)S(1)}, bf16[352,512]{1,0:T(8,128)(2,1)S(1)}, u32[]{:S(2)}, u32[]{:S(2)}) collective-permute-start(bf16[352,512]{1,0:T(8,128)(2,1)S(1)} %get-tuple-element.35), channel_id=1, source_target_pairs={{0,1},{1,2},{2,3},{3,0},{4,5},{5,6},{6,7},{7,4},{8,9},{9,10},{10,1... | collective-permute-start | bytes 1081352 | tf_op jit(solution)/shard_map/ppermute | solution.py:286
  125.1 16.9 %collective-permute-start.9 = (bf16[352,512]{1,0:T(8,128)(2,1)S(1)}, bf16[352,512]{1,0:T(8,128)(2,1)S(1)}, u32[]{:S(2)}, u32[]{:S(2)}) collective-permute-start(bf16[352,512]{1,0:T(8,128)(2,1)S(1)} %get-tuple-element.34.own_ref), channel_id=1, source_target_pairs={{0,2},{1,3},{2,0},{3,1},{4,6},{5,7},{6,4},{7,5},{8,10},{9,11},{10,... | collective-permute-start | bytes 1081352 | tf_op jit(solution)/shard_map/ppermute | solution.py:286
  127.6 26.7 %copy-start.2 = (bf16[8,512,512]{2,1,0:T(8,128)(2,1)S(1)}, bf16[8,512,512]{2,1,0:T(8,128)(2,1)}, u32[]{:S(2)}) copy-start(bf16[8,512,512]{2,1,0:T(8,128)(2,1)} %l2l_ref.1) | copy-start | bytes 12582916
  127.6 14.0 %collective-permute-start.11 = (bf16[208,512]{1,0:T(8,128)(2,1)S(1)}, bf16[208,512]{1,0:T(8,128)(2,1)S(1)}, u32[]{:S(2)}, u32[]{:S(2)}) collective-permute-start(bf16[208,512]{1,0:T(8,128)(2,1)S(1)} %get-tuple-element.36), channel_id=1, source_target_pairs={{0,3},{1,0},{2,1},{3,2},{4,7},{5,4},{6,5},{7,6},{8,11},{9,8},{10,9... | collective-permute-start | bytes 638984 | tf_op jit(solution)/shard_map/ppermute | solution.py:286
  142.1 6.2 %collective-permute-start.12 = (bf16[32,512]{1,0:T(8,128)(2,1)S(1)}, bf16[32,512]{1,0:T(8,128)(2,1)S(1)}, u32[]{:S(2)}, u32[]{:S(2)}) collective-permute-start(bf16[32,512]{1,0:T(8,128)(2,1)S(1)} %get-tuple-element.44), channel_id=1, source_target_pairs={{0,4},{4,8},{8,12},{12,16},{16,20},{20,24},{24,28},{28,32},{32,36}... | collective-permute-start | bytes 98312 | tf_op jit(solution)/shard_map/ppermute | solution.py:363
  148.2 6.0 %collective-permute-start.13 = (bf16[144,512]{1,0:T(8,128)(2,1)S(1)}, bf16[144,512]{1,0:T(8,128)(2,1)S(1)}, u32[]{:S(2)}, u32[]{:S(2)}) collective-permute-start(bf16[144,512]{1,0:T(8,128)(2,1)S(1)} %get-tuple-element.45), channel_id=1, source_target_pairs={{0,3},{1,0},{2,1},{3,2},{4,7},{5,4},{6,5},{7,6},{8,11},{9,8},{10,9... | collective-permute-start | bytes 442376 | tf_op jit(solution)/shard_map/ppermute | solution.py:286
  148.2 6.0 %collective-permute-start.14 = (bf16[32,512]{1,0:T(8,128)(2,1)S(1)}, bf16[32,512]{1,0:T(8,128)(2,1)S(1)}, u32[]{:S(2)}, u32[]{:S(2)}) collective-permute-start(bf16[32,512]{1,0:T(8,128)(2,1)S(1)} %get-tuple-element.48), channel_id=1, source_target_pairs={{4,0},{8,4},{12,8},{16,12},{20,16},{24,20},{28,24},{32,28},{36,32}... | collective-permute-start | bytes 98312 | tf_op jit(solution)/shard_map/ppermute | solution.py:364
  155.3 9.7 %collective-permute-start.15 = (bf16[256,512]{1,0:T(8,128)(2,1)S(1)}, bf16[256,512]{1,0:T(8,128)(2,1)S(1)}, u32[]{:S(2)}, u32[]{:S(2)}) collective-permute-start(bf16[256,512]{1,0:T(8,128)(2,1)S(1)} %finish.1), channel_id=1, source_target_pairs={{0,2},{1,3},{2,0},{3,1},{4,6},{5,7},{6,4},{7,5},{8,10},{9,11},{10,... | collective-permute-start | bytes 786440 | tf_op jit(solution)/shard_map/ppermute | solution.py:286
  157.4 12.0 %collective-permute-start.16 = (bf16[256,512]{1,0:T(8,128)(2,1)S(1)}, bf16[256,512]{1,0:T(8,128)(2,1)S(1)}, u32[]{:S(2)}, u32[]{:S(2)}) collective-permute-start(bf16[256,512]{1,0:T(8,128)(2,1)S(1)} %finish.1), channel_id=1, source_target_pairs={{0,1},{1,2},{2,3},{3,0},{4,5},{5,6},{6,7},{7,4},{8,9},{9,10},{10,1... | collective-permute-start | bytes 786440 | tf_op jit(solution)/shard_map/ppermute | solution.py:286
  157.4 12.1 %collective-permute-start.17 = (bf16[256,512]{1,0:T(8,128)(2,1)S(1)}, bf16[256,512]{1,0:T(8,128)(2,1)S(1)}, u32[]{:S(2)}, u32[]{:S(2)}) collective-permute-start(bf16[256,512]{1,0:T(8,128)(2,1)S(1)} %finish.1), channel_id=1, source_target_pairs={{0,3},{1,0},{2,1},{3,2},{4,7},{5,4},{6,5},{7,6},{8,11},{9,8},{10,9... | collective-permute-start | bytes 786440 | tf_op jit(solution)/shard_map/ppermute | solution.py:286
  169.5 1.0 copy-start.3
